TPU v7x, 32 devices: a whole 2x2x4 slice. The times are simulated.
32 devices in a mesh: gx: 2 (over x), gy: 4 (over y, core), gz: 4 (over z).
Axes of the slice: x: 2, y: 2, z: 4, core: 2. Of those that a mesh axis runs over, the one named last changes fastest.
Arguments:
- local_pos: float32 [4, 8, 4, 3, 64], P('gx', 'gy', 'gz'), as said below
- counts: int32 [4, 8, 4], P('gx', 'gy', 'gz'), may hold values from 8 to 64, as said below
- species: int32 [4, 8, 4, 64], P('gx', 'gy', 'gz'), may hold values from 0 to 9
- features: bfloat16 [4, 8, 4, 64, 128], P('gx', 'gy', 'gz'), may hold values from -6 to 6
- radial_weights: float32 [2, 8, 128], replicated, may hold values from -2 to 2
- coupling: float32 [3, 10, 128], replicated, may hold values from -3 to 3
- mixing: float32 [128, 128], replicated, may hold values from -0.5 to 0.5
- hidden_weights: float32 [128, 16], replicated, may hold values from -0.5 to 0.5
- output_weights: float32 [16], replicated, may hold values from -1.5 to 1.5
Outputs:
- atom_energy: float32 [4, 8, 4, 64], P('gx', 'gy', 'gz')
- forces: float32 [4, 8, 4, 3, 64], P('gx', 'gy', 'gz')
- feature_grad: float32 [4, 8, 4, 64, 128], P('gx', 'gy', 'gz')
Inputs may be any that keep to these rules, and one draw needn't show every extreme that they name: `counts`: every cell holds between 8 and 64 atoms, and at least one cell is full. `local_pos`: the slots of a cell sit on distinct sites of a 4 x 4 x 4 lattice of spacing 7 / 4, each moved by at most 0.3 spacings along each coordinate, so any two slots are 0.4 spacings apart or more.
All inputs are finite; a program needn't handle non-finite values.
Results may differ from a plain program's by a relative error of at most 0.0048.
Values may be sent and summed in bfloat16 or wider, within the bound.
A program may use at most 64 MiB of HBM per device.

v0:
```python
import jax
import jax.numpy as jnp
import numpy as np
from jax import lax
from jax.sharding import PartitionSpec as P

SIDE = 7.0
CUTOFF = 5.0
OFFSETS = (
    np.array(
        [
            [step_a, step_b, step_c]
            for step_a in (-1, 0, 1)
            for step_b in (-1, 0, 1)
            for step_c in (-1, 0, 1)
        ],
        dtype=np.float32,
    )
    * SIDE
)
middle_cell = 13


def extended(block, sides, width):
    for axis, dim in sides:
        count = lax.axis_size(axis)
        forward = [(i, i + 1) for i in range(count - 1)]
        forward.append((count - 1, 0))
        backward = [(target, source) for source, target in forward]
        low = lax.ppermute(
            lax.slice_in_dim(block, block.shape[dim] - width, None, axis=dim), axis, forward
        )
        high = lax.ppermute(lax.slice_in_dim(block, 0, width, axis=dim), axis, backward)
        block = jnp.concatenate([low, block, high], axis=dim)
    return block


def edge_terms(own_xyz, far_xyz, pair_weight, self_mask, basis_count):
    displace = far_xyz[:, None, :] - own_xyz[:, :, None]
    radius = jnp.sqrt(jnp.sum(displace * displace, axis=0) + self_mask)
    scaled = radius / CUTOFF
    envelope = 1.0 - 28.0 * scaled**6 + 48.0 * scaled**7 - 21.0 * scaled**8
    envelope = jnp.where(radius < CUTOFF, envelope, 0.0) * pair_weight
    orders = jnp.arange(1, basis_count + 1, dtype=jnp.float32)
    bessel = (
        jnp.sqrt(2.0 / CUTOFF)
        * jnp.sin(orders[:, None, None] * jnp.pi * radius[None] / CUTOFF)
        / radius[None]
    )
    radial_part = bessel * envelope[None]
    harmonics = jnp.concatenate(
        [jnp.ones_like(radius)[None], jnp.sqrt(3.0) * displace / radius[None]], axis=0
    )
    edge_values = radial_part[:, None] * harmonics[None]
    return edge_values.reshape(basis_count * 4, radius.shape[0], radius.shape[1])


def cell_terms(
    own_pos,
    own_kind,
    near_pos,
    near_feat,
    radial_weights,
    coupling,
    mixing,
    hidden_weights,
    output_weights,
):
    capacity = own_pos.shape[1]
    near_count = near_pos.shape[0] * capacity
    basis_count = radial_weights.shape[1]
    channels = near_feat.shape[1]
    far_xyz = (near_pos[:, :3, :] + OFFSETS[:, :, None]).transpose(1, 0, 2).reshape(3, near_count)
    far_occ = near_pos[:, 3, :].reshape(near_count)
    own_xyz = own_pos[:3]
    own_occ = own_pos[3]
    column = jnp.arange(near_count, dtype=jnp.int32)
    own_index = jnp.arange(capacity, dtype=jnp.int32)
    self_mask = (column[None, :] == own_index[:, None] + middle_cell * capacity).astype(jnp.float32)
    pair_weight = own_occ[:, None] * far_occ[None, :] * (1.0 - self_mask)

    def edges(xyz_own, xyz_far):
        return edge_terms(xyz_own, xyz_far, pair_weight, self_mask, basis_count)

    edge_values, pullback = jax.vjp(edges, own_xyz, far_xyz)
    edge_half = edge_values.astype(jnp.bfloat16).reshape(basis_count * 4 * capacity, near_count)
    summed = jnp.dot(edge_half, near_feat, preferred_element_type=jnp.float32)
    summed = summed.reshape(basis_count, 4, capacity, channels)
    scalar = jnp.sum(summed[:, 0] * radial_weights[0][:, None, :], axis=0)
    vector = jnp.sum(summed[:, 1:] * radial_weights[1][:, None, None, :], axis=0)
    kind_onehot = (
        own_kind[:, None] == jnp.arange(coupling.shape[1], dtype=jnp.int32)[None, :]
    ).astype(jnp.float32)
    weights = jnp.einsum("sk,qkc->qsc", kind_onehot, coupling, precision=lax.Precision.HIGHEST)
    length_sq = jnp.sum(vector * vector, axis=0)
    product = weights[0] * scalar + weights[1] * scalar * scalar + weights[2] * length_sq
    mixed_out = jnp.dot(product, mixing, precision=lax.Precision.HIGHEST)
    hidden = jnp.dot(mixed_out, hidden_weights, precision=lax.Precision.HIGHEST)
    logistic = jax.nn.sigmoid(hidden)
    energy = own_occ * jnp.sum(output_weights[None, :] * hidden * logistic, axis=1)
    d_hidden = (
        own_occ[:, None] * output_weights[None, :] * logistic * (1.0 + hidden * (1.0 - logistic))
    )
    d_mixed = jnp.dot(d_hidden, hidden_weights.T, precision=lax.Precision.HIGHEST)
    d_product = jnp.dot(d_mixed, mixing.T, precision=lax.Precision.HIGHEST)
    d_scalar = d_product * (weights[0] + 2.0 * weights[1] * scalar)
    d_vector = 2.0 * weights[2][None] * vector * d_product[None]
    d_first = radial_weights[0][:, None, :] * d_scalar[None]
    d_rest = radial_weights[1][:, None, None, :] * d_vector[None]
    d_summed = jnp.concatenate([d_first[:, None], d_rest], axis=1)
    d_half = d_summed.astype(jnp.bfloat16).reshape(basis_count * 4 * capacity, channels)
    d_edge = lax.dot_general(
        d_half, near_feat, (((1,), (1,)), ((), ())), preferred_element_type=jnp.float32
    )
    d_edge = d_edge.reshape(basis_count * 4, capacity, near_count)
    d_feat = lax.dot_general(
        edge_half, d_half, (((0,), (0,)), ((), ())), preferred_element_type=jnp.float32
    )
    d_own, d_far = pullback(d_edge)
    d_far = d_far.reshape(3, near_pos.shape[0], capacity).transpose(1, 0, 2)
    d_far = d_far.at[middle_cell].add(d_own)
    return (energy, d_far, d_feat.reshape(near_pos.shape[0], capacity, channels))


def fold_along(merged, axis_dim):
    extent = merged.shape[axis_dim]
    outer_rims = jnp.concatenate(
        [
            lax.slice_in_dim(merged, 0, 1, axis=axis_dim),
            lax.slice_in_dim(merged, extent - 1, extent, axis=axis_dim),
        ],
        axis=axis_dim,
    )
    if axis_dim == 0:
        arrived = extended(outer_rims.astype(jnp.bfloat16), (("gx", 0),), 1).astype(
            outer_rims.dtype
        )
    elif axis_dim == 1:
        arrived = extended(outer_rims.astype(jnp.bfloat16), (("gy", 1),), 1).astype(
            outer_rims.dtype
        )
    else:
        arrived = extended(outer_rims.astype(jnp.bfloat16), (("gz", 2),), 1).astype(
            outer_rims.dtype
        )
    interior = lax.slice_in_dim(merged, 1, extent - 1, axis=axis_dim)
    inner_count = extent - 2
    from_below = lax.slice_in_dim(arrived, 0, 1, axis=axis_dim)
    from_above = lax.slice_in_dim(arrived, 3, 4, axis=axis_dim)
    low_widths = [(0, 0)] * merged.ndim
    high_widths = [(0, 0)] * merged.ndim
    low_widths[axis_dim] = (0, inner_count - 1)
    high_widths[axis_dim] = (inner_count - 1, 0)
    return interior + jnp.pad(from_below, low_widths) + jnp.pad(from_above, high_widths)


def body(
    local_pos,
    counts,
    species,
    features,
    radial_weights,
    coupling,
    mixing,
    hidden_weights,
    output_weights,
):
    cells_x, cells_y, cells_z = counts.shape
    capacity = features.shape[3]
    channels = features.shape[4]
    occupied = (
        jnp.arange(capacity, dtype=jnp.int32)[None, None, None, :] < counts[..., None]
    ).astype(jnp.float32)
    with_occ = jnp.concatenate([local_pos, occupied[:, :, :, None, :]], axis=3)
    pos_padded = extended(with_occ, (("gx", 0), ("gy", 1), ("gz", 2)), 1)
    feat_padded = extended(features, (("gx", 0), ("gy", 1), ("gz", 2)), 1)

    def visit_cell(totals, cell_id):
        feat_total, pos_total = totals
        index_x = cell_id // (cells_y * cells_z)
        index_y = cell_id // cells_z % cells_y
        index_z = cell_id % cells_z
        near_pos = lax.dynamic_slice(
            pos_padded, (index_x, index_y, index_z, 0, 0), (3, 3, 3, 4, capacity)
        )
        near_pos = near_pos.reshape(27, 4, capacity)
        near_feat = lax.dynamic_slice(
            feat_padded, (index_x, index_y, index_z, 0, 0), (3, 3, 3, capacity, channels)
        )
        near_feat = near_feat.reshape(27 * capacity, channels)
        own_kind = lax.dynamic_slice(
            species, (index_x, index_y, index_z, 0), (1, 1, 1, capacity)
        ).reshape(capacity)
        energy, d_far, d_feat = cell_terms(
            near_pos[middle_cell],
            own_kind,
            near_pos,
            near_feat,
            radial_weights,
            coupling,
            mixing,
            hidden_weights,
            output_weights,
        )
        previous = lax.dynamic_slice(
            feat_total, (index_x, index_y, index_z, 0, 0), (3, 3, 3, capacity, channels)
        )
        feat_total = lax.dynamic_update_slice(
            feat_total,
            previous + d_feat.reshape(3, 3, 3, capacity, channels),
            (index_x, index_y, index_z, 0, 0),
        )
        previous_pos = lax.dynamic_slice(
            pos_total, (index_x, index_y, index_z, 0, 0), (3, 3, 3, 3, capacity)
        )
        pos_total = lax.dynamic_update_slice(
            pos_total,
            previous_pos + d_far.reshape(3, 3, 3, 3, capacity),
            (index_x, index_y, index_z, 0, 0),
        )
        return ((feat_total, pos_total), energy)

    padded_shape = (cells_x + 2, cells_y + 2, cells_z + 2)
    start = (
        jnp.zeros(padded_shape + (capacity, channels), jnp.float32),
        jnp.zeros(padded_shape + (3, capacity), jnp.float32),
    )
    (feat_total, pos_total), energies = lax.scan(
        visit_cell, start, jnp.arange(cells_x * cells_y * cells_z, dtype=jnp.int32)
    )
    merged = jnp.concatenate(
        [
            feat_total.reshape(padded_shape + (capacity * channels,)),
            pos_total.reshape(padded_shape + (3 * capacity,)),
        ],
        axis=3,
    )
    axis_order = (2, 1, 0)
    for axis_dim in axis_order:
        merged = fold_along(merged, axis_dim)
    feature_grad = merged[..., : capacity * channels].reshape(
        cells_x, cells_y, cells_z, capacity, channels
    )
    position_grad = merged[..., capacity * channels :].reshape(
        cells_x, cells_y, cells_z, 3, capacity
    )
    atom_energy = energies.reshape(cells_x, cells_y, cells_z, capacity)
    return (atom_energy, -position_grad, feature_grad)


def solution(mesh):
    placed = (
        P("gx", "gy", "gz", None, None),
        P("gx", "gy", "gz"),
        P("gx", "gy", "gz", None),
        P("gx", "gy", "gz", None, None),
        P(),
        P(),
        P(),
        P(),
        P(),
    )
    return jax.shard_map(
        body,
        mesh=mesh,
        in_specs=placed,
        out_specs=(
            P("gx", "gy", "gz", None),
            P("gx", "gy", "gz", None, None),
            P("gx", "gy", "gz", None, None),
        ),
        check_vma=False,
    )
```

profile of v0, /device:TPU:0, one launch (start us, length us, event | category | flops | bytes accessed | tf_op | source)
XLA Modules:
  0.0 347.8 jit_solution(653396643899108170)
XLA Ops:
  1.4 2.9 collective-permute-start.6
  5.9 2.0 collective-permute-start.1
  8.8 3.0 collective-permute-done.7
  11.9 1.7 collective-permute-start.9
  13.7 1.9 collective-permute-done.8
  15.7 1.6 collective-permute-start.10
  17.3 2.2 collective-permute-start.11
  19.5 1.2 collective-permute-start.2
  21.3 1.3 collective-permute-done.2
  22.7 3.8 %collective-permute-start.5 = (f32[4,4,1,4,64]{4,3,2,1,0:T(4,128)S(1)}, f32[4,4,1,4,64]{4,3,2,1,0:T(4,128)S(1)}, u32[]{:S(2)}, u32[]{:S(2)}) collective-permute-start(f32[4,4,1,4,64]{4,3,2,1,0:T(4,128)S(1)} %pad_maximum_fusion.8), channel_id=1, source_target_pairs={{1,0},{2,1},{3,2},{0,3},{5,4},{6,5},{7,6},{4,7},{9,8},{10,9},{11,1... | collective-permute-start | bytes 49160 | tf_op jit(solution)/shard_map/ppermute | solution.py:33
  26.6 1.3 copy.38
  27.9 4.5 %collective-permute-done.4 = f32[4,4,1,4,64]{4,3,2,1,0:T(4,128)S(1)} collective-permute-done((f32[4,4,1,4,64]{4,3,2,1,0:T(4,128)S(1)}, f32[4,4,1,4,64]{4,3,2,1,0:T(4,128)S(1)}, u32[]{:S(2)}, u32[]{:S(2)}) %collective-permute-start.4) | collective-permute-done | bytes 16416 | tf_op jit(solution)/shard_map/ppermute | solution.py:30
  34.4 1.4 broadcast_in_dim.24.clone
  36.4 279.0 %while.20 = (s32[]{:T(128)}, f32[4,4,3,64,128]{4,3,1,2,0:T(8,128)}, f32[4,4,3,3,64]{4,3,1,2,0:T(4,128)}, f32[4,64]{1,0:T(4,128)}, s32[4]{0:T(128)}, /*index=5*/f...) while((s32[]{:T(128)}, f32[4,4,3,64,128]{4,3,1,2,0:T(8,128)}, ...), condition=%wide.region_14.15_spmd.clone, body=%wide.region_0.14_spmd.sunk.clone.sunk | while | flops 2808300544 | bytes 117356464 | solution.py:228
  36.4 1.2 dynamic_slice.91
  41.6 12.2 %fusion.129 = f32[8,64,1728]{2,1,0:T(8,128)S(1)} fusion(f32[64,1728]{1,0:T(8,128)S(1)} %fusion.127, f32[64,1728]{1,0:T(8,128)S(1)} %get-tuple-element.600, f32[8]{0:T(128)S(1)} %get-tuple-element.601), kind=kLoop, calls=%fused_computation.12.clone.1 | loop fusion | flops 4423680 | bytes 4423712 | tf_op jit(solution)/shard_map/while/body/eval_jaxpr/jvp()/mul | solution.py:50
  54.3 1.6 copy-done.5
  55.9 2.2 fusion.130
  60.1 1.5 multiply_reduce_fusion.12
  61.6 1.0 fusion.135
  63.1 8.2 %multiply_reduce_fusion.13 = (f32[8,64,1728]{2,1,0:T(8,128)S(1)}, f32[4,64,1728]{2,1,0:T(8,128)S(1)}, bf16[8,4,64,1728]{3,2,1,0:T(8,128)(2,1)}) fusion(f32[4,64,1728]{2,1,0:T(8,128)S(1)} %concatenate.145, f32[8,64,1728]{2,1,0:T(8,128)} %copy-done, bf16[1728,128,1,1]{1,0,3,2:T(8,128)(2,1)} %bitcast.197, ...), kind=kOutput, calls=%fused_computation.clone.1 | convolution fusion | flops 926138368 | bytes 18661376 | tf_op jit(solution)/shard_map/while/body/eval_jaxpr/dot_general | solution.py:112
  71.3 15.6 %multiply_reduce_fusion.14 = (f32[64,1728]{1,0:T(8,128)S(1)}, f32[64,1728]{1,0:T(8,128)S(1)}, f32[64,1728]{1,0:T(8,128)S(1)}) fusion(f32[8,64,1728]{2,1,0:T(8,128)S(1)} %get-tuple-element.608, f32[64,1728]{1,0:T(8,128)S(1)} %get-tuple-element.609, f32[64,1728]{1,0:T(8,128)S(1)} %fusion.127, f32[64,1728]{1,0:T(8,128)S(1)} %get-tuple-element.600, ...), kind=kLoop, calls=%fused_computation.5.clone.1 | loop fusion | flops 12939264 | bytes 6193216 | tf_op jit(solution)/shard_map/while/body/eval_jaxpr/transpose(jvp())/reduce_sum | solution.py:46
  89.1 10.3 %copy.73 = bf16[1728,2048]{1,0:T(8,128)(2,1)} copy(bf16[1728,2048]{0,1:T(8,128)(2,1)} %bitcast.192) | data formatting | bytes 14155776 | tf_op jit(solution)/shard_map/while/body/eval_jaxpr/dot_general | solution.py:116
  99.5 5.1 %convolution_add_fusion.2 = f32[3,3,3,64,128]{4,3,2,1,0:T(8,128)S(1)} fusion(bf16[3,3,3,64,2048]{4,3,2,1,0:T(8,128)(2,1)} %bitcast.191, bf16[2048,128,1,1,1]{1,0,4,3,2:T(8,128)(2,1)S(1)} %bitcast.195, f32[4,4,3,64,128]{4,3,1,2,0:T(8,128)S(1)} %copy-done.3, s32[]{:T(128)S(6)} %select_n.140, s32[]{:T(128)S(6)} %select_n.142), kind=kOutput, calls=%fused_computation.19.clone.1 | convolution fusion | flops 906190848 | bytes 9371656 | tf_op jit(solution)/shard_map/while/body/eval_jaxpr/dot_general | solution.py:116
  104.8 1.3 dynamic_update_slice.43
  106.2 1.2 dynamic_slice.91
  111.3 12.2 %fusion.129 = f32[8,64,1728]{2,1,0:T(8,128)S(1)} fusion(f32[64,1728]{1,0:T(8,128)S(1)} %fusion.127, f32[64,1728]{1,0:T(8,128)S(1)} %get-tuple-element.600, f32[8]{0:T(128)S(1)} %get-tuple-element.601), kind=kLoop, calls=%fused_computation.12.clone.1 | loop fusion | flops 4423680 | bytes 4423712 | tf_op jit(solution)/shard_map/while/body/eval_jaxpr/jvp()/mul | solution.py:50
  124.0 1.6 copy-done.5
  125.6 2.2 fusion.130
  129.9 1.5 multiply_reduce_fusion.12
  132.8 8.2 %multiply_reduce_fusion.13 = (f32[8,64,1728]{2,1,0:T(8,128)S(1)}, f32[4,64,1728]{2,1,0:T(8,128)S(1)}, bf16[8,4,64,1728]{3,2,1,0:T(8,128)(2,1)}) fusion(f32[4,64,1728]{2,1,0:T(8,128)S(1)} %concatenate.145, f32[8,64,1728]{2,1,0:T(8,128)} %copy-done, bf16[1728,128,1,1]{1,0,3,2:T(8,128)(2,1)} %bitcast.197, ...), kind=kOutput, calls=%fused_computation.clone.1 | convolution fusion | flops 926138368 | bytes 18661376 | tf_op jit(solution)/shard_map/while/body/eval_jaxpr/dot_general | solution.py:112
  141.0 15.6 %multiply_reduce_fusion.14 = (f32[64,1728]{1,0:T(8,128)S(1)}, f32[64,1728]{1,0:T(8,128)S(1)}, f32[64,1728]{1,0:T(8,128)S(1)}) fusion(f32[8,64,1728]{2,1,0:T(8,128)S(1)} %get-tuple-element.608, f32[64,1728]{1,0:T(8,128)S(1)} %get-tuple-element.609, f32[64,1728]{1,0:T(8,128)S(1)} %fusion.127, f32[64,1728]{1,0:T(8,128)S(1)} %get-tuple-element.600, ...), kind=kLoop, calls=%fused_computation.5.clone.1 | loop fusion | flops 12939264 | bytes 6193216 | tf_op jit(solution)/shard_map/while/body/eval_jaxpr/transpose(jvp())/reduce_sum | solution.py:46
  158.8 10.3 %copy.73 = bf16[1728,2048]{1,0:T(8,128)(2,1)} copy(bf16[1728,2048]{0,1:T(8,128)(2,1)} %bitcast.192) | data formatting | bytes 14155776 | tf_op jit(solution)/shard_map/while/body/eval_jaxpr/dot_general | solution.py:116
  169.2 5.1 %convolution_add_fusion.2 = f32[3,3,3,64,128]{4,3,2,1,0:T(8,128)S(1)} fusion(bf16[3,3,3,64,2048]{4,3,2,1,0:T(8,128)(2,1)} %bitcast.191, bf16[2048,128,1,1,1]{1,0,4,3,2:T(8,128)(2,1)S(1)} %bitcast.195, f32[4,4,3,64,128]{4,3,1,2,0:T(8,128)S(1)} %copy-done.3, s32[]{:T(128)S(6)} %select_n.140, s32[]{:T(128)S(6)} %select_n.142), kind=kOutput, calls=%fused_computation.19.clone.1 | convolution fusion | flops 906190848 | bytes 9371656 | tf_op jit(solution)/shard_map/while/body/eval_jaxpr/dot_general | solution.py:116
  174.5 1.3 dynamic_update_slice.43
  175.9 1.2 dynamic_slice.91
  181.0 12.2 %fusion.129 = f32[8,64,1728]{2,1,0:T(8,128)S(1)} fusion(f32[64,1728]{1,0:T(8,128)S(1)} %fusion.127, f32[64,1728]{1,0:T(8,128)S(1)} %get-tuple-element.600, f32[8]{0:T(128)S(1)} %get-tuple-element.601), kind=kLoop, calls=%fused_computation.12.clone.1 | loop fusion | flops 4423680 | bytes 4423712 | tf_op jit(solution)/shard_map/while/body/eval_jaxpr/jvp()/mul | solution.py:50
  193.7 1.6 copy-done.5
  195.3 2.2 fusion.130
  199.6 1.5 multiply_reduce_fusion.12
  202.5 8.2 %multiply_reduce_fusion.13 = (f32[8,64,1728]{2,1,0:T(8,128)S(1)}, f32[4,64,1728]{2,1,0:T(8,128)S(1)}, bf16[8,4,64,1728]{3,2,1,0:T(8,128)(2,1)}) fusion(f32[4,64,1728]{2,1,0:T(8,128)S(1)} %concatenate.145, f32[8,64,1728]{2,1,0:T(8,128)} %copy-done, bf16[1728,128,1,1]{1,0,3,2:T(8,128)(2,1)} %bitcast.197, ...), kind=kOutput, calls=%fused_computation.clone.1 | convolution fusion | flops 926138368 | bytes 18661376 | tf_op jit(solution)/shard_map/while/body/eval_jaxpr/dot_general | solution.py:112
  210.7 15.6 %multiply_reduce_fusion.14 = (f32[64,1728]{1,0:T(8,128)S(1)}, f32[64,1728]{1,0:T(8,128)S(1)}, f32[64,1728]{1,0:T(8,128)S(1)}) fusion(f32[8,64,1728]{2,1,0:T(8,128)S(1)} %get-tuple-element.608, f32[64,1728]{1,0:T(8,128)S(1)} %get-tuple-element.609, f32[64,1728]{1,0:T(8,128)S(1)} %fusion.127, f32[64,1728]{1,0:T(8,128)S(1)} %get-tuple-element.600, ...), kind=kLoop, calls=%fused_computation.5.clone.1 | loop fusion | flops 12939264 | bytes 6193216 | tf_op jit(solution)/shard_map/while/body/eval_jaxpr/transpose(jvp())/reduce_sum | solution.py:46
  228.6 10.3 %copy.73 = bf16[1728,2048]{1,0:T(8,128)(2,1)} copy(bf16[1728,2048]{0,1:T(8,128)(2,1)} %bitcast.192) | data formatting | bytes 14155776 | tf_op jit(solution)/shard_map/while/body/eval_jaxpr/dot_general | solution.py:116
  239.0 5.1 %convolution_add_fusion.2 = f32[3,3,3,64,128]{4,3,2,1,0:T(8,128)S(1)} fusion(bf16[3,3,3,64,2048]{4,3,2,1,0:T(8,128)(2,1)} %bitcast.191, bf16[2048,128,1,1,1]{1,0,4,3,2:T(8,128)(2,1)S(1)} %bitcast.195, f32[4,4,3,64,128]{4,3,1,2,0:T(8,128)S(1)} %copy-done.3, s32[]{:T(128)S(6)} %select_n.140, s32[]{:T(128)S(6)} %select_n.142), kind=kOutput, calls=%fused_computation.19.clone.1 | convolution fusion | flops 906190848 | bytes 9371656 | tf_op jit(solution)/shard_map/while/body/eval_jaxpr/dot_general | solution.py:116
  244.2 1.3 dynamic_update_slice.43
  245.6 1.2 dynamic_slice.91
  250.8 12.2 %fusion.129 = f32[8,64,1728]{2,1,0:T(8,128)S(1)} fusion(f32[64,1728]{1,0:T(8,128)S(1)} %fusion.127, f32[64,1728]{1,0:T(8,128)S(1)} %get-tuple-element.600, f32[8]{0:T(128)S(1)} %get-tuple-element.601), kind=kLoop, calls=%fused_computation.12.clone.1 | loop fusion | flops 4423680 | bytes 4423712 | tf_op jit(solution)/shard_map/while/body/eval_jaxpr/jvp()/mul | solution.py:50
  263.4 1.6 copy-done.5
  265.1 2.2 fusion.130
  269.3 1.5 multiply_reduce_fusion.12
  272.2 8.2 %multiply_reduce_fusion.13 = (f32[8,64,1728]{2,1,0:T(8,128)S(1)}, f32[4,64,1728]{2,1,0:T(8,128)S(1)}, bf16[8,4,64,1728]{3,2,1,0:T(8,128)(2,1)}) fusion(f32[4,64,1728]{2,1,0:T(8,128)S(1)} %concatenate.145, f32[8,64,1728]{2,1,0:T(8,128)} %copy-done, bf16[1728,128,1,1]{1,0,3,2:T(8,128)(2,1)} %bitcast.197, ...), kind=kOutput, calls=%fused_computation.clone.1 | convolution fusion | flops 926138368 | bytes 18661376 | tf_op jit(solution)/shard_map/while/body/eval_jaxpr/dot_general | solution.py:112
  280.4 15.6 %multiply_reduce_fusion.14 = (f32[64,1728]{1,0:T(8,128)S(1)}, f32[64,1728]{1,0:T(8,128)S(1)}, f32[64,1728]{1,0:T(8,128)S(1)}) fusion(f32[8,64,1728]{2,1,0:T(8,128)S(1)} %get-tuple-element.608, f32[64,1728]{1,0:T(8,128)S(1)} %get-tuple-element.609, f32[64,1728]{1,0:T(8,128)S(1)} %fusion.127, f32[64,1728]{1,0:T(8,128)S(1)} %get-tuple-element.600, ...), kind=kLoop, calls=%fused_computation.5.clone.1 | loop fusion | flops 12939264 | bytes 6193216 | tf_op jit(solution)/shard_map/while/body/eval_jaxpr/transpose(jvp())/reduce_sum | solution.py:46
  298.3 10.3 %copy.73 = bf16[1728,2048]{1,0:T(8,128)(2,1)} copy(bf16[1728,2048]{0,1:T(8,128)(2,1)} %bitcast.192) | data formatting | bytes 14155776 | tf_op jit(solution)/shard_map/while/body/eval_jaxpr/dot_general | solution.py:116
  308.7 5.1 %convolution_add_fusion.2 = f32[3,3,3,64,128]{4,3,2,1,0:T(8,128)S(1)} fusion(bf16[3,3,3,64,2048]{4,3,2,1,0:T(8,128)(2,1)} %bitcast.191, bf16[2048,128,1,1,1]{1,0,4,3,2:T(8,128)(2,1)S(1)} %bitcast.195, f32[4,4,3,64,128]{4,3,1,2,0:T(8,128)S(1)} %copy-done.3, s32[]{:T(128)S(6)} %select_n.140, s32[]{:T(128)S(6)} %select_n.142), kind=kOutput, calls=%fused_computation.19.clone.1 | convolution fusion | flops 906190848 | bytes 9371656 | tf_op jit(solution)/shard_map/while/body/eval_jaxpr/dot_general | solution.py:116
  313.9 1.3 dynamic_update_slice.43
  315.5 1.9 reshape.633
  318.9 1.4 collective-permute-start.12
  320.3 2.4 collective-permute-start.13
  322.8 7.3 %collective-permute-done.12 = bf16[4,4,1,8384]{3,1,2,0:T(4,128)(2,1)S(1)} collective-permute-done((bf16[4,4,1,8384]{3,1,2,0:T(4,128)(2,1)S(1)}, bf16[4,4,1,8384]{3,1,2,0:T(4,128)(2,1)S(1)}, u32[]{:S(2)}, u32[]{:S(2)}) %collective-permute-start.12) | collective-permute-done | bytes 268320 | tf_op jit(solution)/shard_map/ppermute | solution.py:30
  330.1 4.3 %collective-permute-done.13 = bf16[4,4,1,8384]{3,1,2,0:T(4,128)(2,1)S(1)} collective-permute-done((bf16[4,4,1,8384]{3,1,2,0:T(4,128)(2,1)S(1)}, bf16[4,4,1,8384]{3,1,2,0:T(4,128)(2,1)S(1)}, u32[]{:S(2)}, u32[]{:S(2)}) %collective-permute-start.13) | collective-permute-done | bytes 268320 | tf_op jit(solution)/shard_map/ppermute | solution.py:33
  335.1 1.7 collective-permute-start.15
  337.2 2.4 collective-permute-done.14
  341.6 1.5 collective-permute-start.16
  343.2 2.0 collective-permute-done.17
  (399 shorter events, 44.3 us)
Async XLA Ops:
  1.4 6.6 %collective-permute-start.6 = (bf16[1,2,1,64,128]{4,3,2,1,0:T(8,128)(2,1)S(1)}, bf16[1,2,1,64,128]{4,3,2,1,0:T(8,128)(2,1)S(1)}, u32[]{:S(2)}, u32[]{:S(2)}) collective-permute-start(bf16[1,2,1,64,128]{4,3,2,1,0:T(8,128)(2,1)S(1)} %get-tuple-element.498), channel_id=1, source_target_pairs={{0,16},{16,0},{1,17},{17,1},{2,18},{18,2},{3,19},{19,3},{4,20},{20... | collective-permute-start | bytes 98312 | tf_op jit(solution)/shard_map/ppermute | solution.py:30
  5.8 7.8 %collective-permute-start = (f32[1,2,1,4,64]{4,3,2,1,0:T(4,128)S(1)}, f32[1,2,1,4,64]{4,3,2,1,0:T(4,128)S(1)}, u32[]{:S(2)}, u32[]{:S(2)}) collective-permute-start(f32[1,2,1,4,64]{4,3,2,1,0:T(4,128)S(1)} %get-tuple-element.501), channel_id=1, source_target_pairs={{0,16},{16,0},{1,17},{17,1},{2,18},{18,2},{3,19},{19,3},{4,20},{20... | collective-permute-start | bytes 6152 | tf_op jit(solution)/shard_map/ppermute | solution.py:30
  5.9 7.8 %collective-permute-start.1 = (f32[1,2,1,4,64]{4,3,2,1,0:T(4,128)S(1)}, f32[1,2,1,4,64]{4,3,2,1,0:T(4,128)S(1)}, u32[]{:S(2)}, u32[]{:S(2)}) collective-permute-start(f32[1,2,1,4,64]{4,3,2,1,0:T(4,128)S(1)} %get-tuple-element.502), channel_id=1, source_target_pairs={{16,0},{0,16},{17,1},{1,17},{18,2},{2,18},{19,3},{3,19},{20,4},{4,... | collective-permute-start | bytes 6152 | tf_op jit(solution)/shard_map/ppermute | solution.py:33
  7.9 3.9 %collective-permute-start.7 = (bf16[1,2,1,64,128]{4,3,2,1,0:T(8,128)(2,1)S(1)}, bf16[1,2,1,64,128]{4,3,2,1,0:T(8,128)(2,1)S(1)}, u32[]{:S(2)}, u32[]{:S(2)}) collective-permute-start(bf16[1,2,1,64,128]{4,3,2,1,0:T(8,128)(2,1)S(1)} %get-tuple-element.497), channel_id=1, source_target_pairs={{16,0},{0,16},{17,1},{1,17},{18,2},{2,18},{19,3},{3,19},{20,4},{4,... | collective-permute-start | bytes 98312 | tf_op jit(solution)/shard_map/ppermute | solution.py:33
  11.8 3.7 %collective-permute-start.8 = (bf16[4,1,1,64,128]{4,3,2,1,0:T(8,128)(2,1)S(1)}, bf16[4,1,1,64,128]{4,3,2,1,0:T(8,128)(2,1)S(1)}, u32[]{:S(2)}, u32[]{:S(2)}) collective-permute-start(bf16[4,1,1,64,128]{4,3,2,1,0:T(8,128)(2,1)S(1)} %get-tuple-element.495), channel_id=1, source_target_pairs={{0,4},{4,8},{8,12},{12,0},{1,5},{5,9},{9,13},{13,1},{2,6},{6,10},{... | collective-permute-start | bytes 196616 | tf_op jit(solution)/shard_map/ppermute | solution.py:30
  11.9 3.7 %collective-permute-start.9 = (bf16[4,1,1,64,128]{4,3,2,1,0:T(8,128)(2,1)S(1)}, bf16[4,1,1,64,128]{4,3,2,1,0:T(8,128)(2,1)S(1)}, u32[]{:S(2)}, u32[]{:S(2)}) collective-permute-start(bf16[4,1,1,64,128]{4,3,2,1,0:T(8,128)(2,1)S(1)} %get-tuple-element.496), channel_id=1, source_target_pairs={{4,0},{8,4},{12,8},{0,12},{5,1},{9,5},{13,9},{1,13},{6,2},{10,6},{... | collective-permute-start | bytes 196616 | tf_op jit(solution)/shard_map/ppermute | solution.py:33
  15.6 20.8 %copy-start.7 = (f32[128,128]{1,0:T(8,128)S(1)}, f32[128,128]{1,0:T(8,128)}, u32[]{:S(2)}) copy-start(f32[128,128]{1,0:T(8,128)} %param.20) | copy-start | bytes 196612
  15.6 20.8 %copy-start.14 = (f32[27,3]{1,0:T(8,128)S(1)}, f32[27,3]{1,0:T(8,128)}, u32[]{:S(2)}) copy-start(f32[27,3]{1,0:T(8,128)} %constant.446) | copy-start | bytes 976
  15.6 20.8 %copy-start.16 = (f32[2,8,128]{2,1,0:T(8,128)S(1)}, f32[2,8,128]{2,1,0:T(8,128)}, u32[]{:S(2)}) copy-start(f32[2,8,128]{2,1,0:T(8,128)} %param.18) | copy-start | bytes 24580
  15.7 17.2 %collective-permute-start.10 = (bf16[4,4,1,64,128]{4,3,2,1,0:T(8,128)(2,1)S(1)}, bf16[4,4,1,64,128]{4,3,2,1,0:T(8,128)(2,1)S(1)}, u32[]{:S(2)}, u32[]{:S(2)}) collective-permute-start(bf16[4,4,1,64,128]{4,3,2,1,0:T(8,128)(2,1)S(1)} %pad_maximum_fusion.6), channel_id=1, source_target_pairs={{0,1},{1,2},{2,3},{3,0},{4,5},{5,6},{6,7},{7,4},{8,9},{9,10},{10,1... | collective-permute-start | bytes 786440 | tf_op jit(solution)/shard_map/ppermute | solution.py:30
  17.3 15.6 %collective-permute-start.11 = (bf16[4,4,1,64,128]{4,3,2,1,0:T(8,128)(2,1)S(1)}, bf16[4,4,1,64,128]{4,3,2,1,0:T(8,128)(2,1)S(1)}, u32[]{:S(2)}, u32[]{:S(2)}) collective-permute-start(bf16[4,4,1,64,128]{4,3,2,1,0:T(8,128)(2,1)S(1)} %pad_maximum_fusion.6), channel_id=1, source_target_pairs={{1,0},{2,1},{3,2},{0,3},{5,4},{6,5},{7,6},{4,7},{9,8},{10,9},{11,1... | collective-permute-start | bytes 786440 | tf_op jit(solution)/shard_map/ppermute | solution.py:33
  19.5 3.1 collective-permute-start.2
  20.7 1.9 collective-permute-start.3
  22.7 9.7 %collective-permute-start.4 = (f32[4,4,1,4,64]{4,3,2,1,0:T(4,128)S(1)}, f32[4,4,1,4,64]{4,3,2,1,0:T(4,128)S(1)}, u32[]{:S(2)}, u32[]{:S(2)}) collective-permute-start(f32[4,4,1,4,64]{4,3,2,1,0:T(4,128)S(1)} %pad_maximum_fusion.8), channel_id=1, source_target_pairs={{0,1},{1,2},{2,3},{3,0},{4,5},{5,6},{6,7},{7,4},{8,9},{9,10},{10,1... | collective-permute-start | bytes 49160 | tf_op jit(solution)/shard_map/ppermute | solution.py:30
  22.7 10.1 %collective-permute-start.5 = (f32[4,4,1,4,64]{4,3,2,1,0:T(4,128)S(1)}, f32[4,4,1,4,64]{4,3,2,1,0:T(4,128)S(1)}, u32[]{:S(2)}, u32[]{:S(2)}) collective-permute-start(f32[4,4,1,4,64]{4,3,2,1,0:T(4,128)S(1)} %pad_maximum_fusion.8), channel_id=1, source_target_pairs={{1,0},{2,1},{3,2},{0,3},{5,4},{6,5},{7,6},{4,7},{9,8},{10,9},{11,1... | collective-permute-start | bytes 49160 | tf_op jit(solution)/shard_map/ppermute | solution.py:33
  40.3 13.6 %copy-start.17 = (s32[64]{0:T(128)}, s32[64]{0:T(128)S(1)}, u32[]{:S(2)}) copy-start(s32[64]{0:T(128)S(1)} %iota_add_fusion.3) | copy-start | bytes 772 | tf_op jit(solution)/shard_map/while
  40.7 13.2 %copy-start.19 = (f32[64]{0:T(128)}, f32[64]{0:T(128)S(1)}, u32[]{:S(2)}) copy-start(f32[64]{0:T(128)S(1)} %slice_bitcast_fusion.15) | copy-start | bytes 772 | tf_op jit(solution)/shard_map/while
  41.6 12.3 %copy-start.21 = (f32[8]{0:T(128)}, f32[8]{0:T(128)S(1)}, u32[]{:S(2)}) copy-start(f32[8]{0:T(128)S(1)} %get-tuple-element.601) | copy-start | bytes 100 | tf_op jit(solution)/shard_map/while
  63.0 8.2 %copy-start.1 = (bf16[8,3,64,128]{3,2,1,0:T(8,128)(2,1)}, bf16[8,3,64,128]{3,2,1,0:T(8,128)(2,1)S(1)}, u32[]{:S(2)}) copy-start(bf16[8,3,64,128]{3,2,1,0:T(8,128)(2,1)S(1)} %multiply_convert_fusion.8) | copy-start | bytes 1179652 | tf_op jit(solution)/shard_map/while
  63.1 8.2 %copy-start.22 = (f32[8]{0:T(128)S(1)}, f32[8]{0:T(128)}, u32[]{:S(2)}) copy-start(f32[8]{0:T(128)} %copy-done.21) | copy-start | bytes 100 | tf_op jit(solution)/shard_map/while
  63.1 8.2 %copy-start.23 = (f32[8]{0:T(128)S(1)}, f32[8]{0:T(128)}, u32[]{:S(2)}) copy-start(f32[8]{0:T(128)} %get-tuple-element.610) | copy-start | bytes 100 | tf_op jit(solution)/shard_map/while
  89.1 10.3 %copy-start.10 = (f32[4,4,3,3,64]{4,3,1,2,0:T(4,128)}, f32[4,4,3,3,64]{4,3,1,2,0:T(4,128)S(1)}, u32[]{:S(2)}) copy-start(f32[4,4,3,3,64]{4,3,1,2,0:T(4,128)S(1)} %copy_dynamic-update-slice_fusion.5) | copy-start | bytes 110596 | tf_op jit(solution)/shard_map/while
  89.1 10.3 %copy-start.2 = (bf16[8,3,64,128]{3,2,1,0:T(8,128)(2,1)S(1)}, bf16[8,3,64,128]{3,2,1,0:T(8,128)(2,1)}, u32[]{:S(2)}) copy-start(bf16[8,3,64,128]{3,2,1,0:T(8,128)(2,1)} %copy-done.1) | copy-start | bytes 1179652 | tf_op jit(solution)/shard_map/while
  89.1 10.4 %copy-start.3 = (f32[4,4,3,64,128]{4,3,1,2,0:T(8,128)S(1)}, f32[4,4,3,64,128]{4,3,1,2,0:T(8,128)}, u32[]{:S(2)}) copy-start(f32[4,4,3,64,128]{4,3,1,2,0:T(8,128)} %get-tuple-element.640) | copy-start | bytes 4718596 | tf_op jit(solution)/shard_map/while
  99.5 6.6 %copy-start.8 = (f32[128,128]{1,0:T(8,128)S(1)}, f32[128,128]{1,0:T(8,128)}, u32[]{:S(2)}) copy-start(f32[128,128]{1,0:T(8,128)} %get-tuple-element.702) | copy-start | bytes 196612 | tf_op jit(solution)/shard_map/while
  99.5 6.6 %copy-start.13 = (f32[4,4,3,4,64]{4,3,2,1,0:T(4,128)S(1)}, f32[4,4,3,4,64]{4,3,2,1,0:T(4,128)}, u32[]{:S(2)}) copy-start(f32[4,4,3,4,64]{4,3,2,1,0:T(4,128)} %copy-done.12) | copy-start | bytes 147460 | tf_op jit(solution)/shard_map/while
  110.0 13.6 %copy-start.17 = (s32[64]{0:T(128)}, s32[64]{0:T(128)S(1)}, u32[]{:S(2)}) copy-start(s32[64]{0:T(128)S(1)} %iota_add_fusion.3) | copy-start | bytes 772 | tf_op jit(solution)/shard_map/while
  110.4 13.2 %copy-start.19 = (f32[64]{0:T(128)}, f32[64]{0:T(128)S(1)}, u32[]{:S(2)}) copy-start(f32[64]{0:T(128)S(1)} %slice_bitcast_fusion.15) | copy-start | bytes 772 | tf_op jit(solution)/shard_map/while
  111.3 12.3 %copy-start.21 = (f32[8]{0:T(128)}, f32[8]{0:T(128)S(1)}, u32[]{:S(2)}) copy-start(f32[8]{0:T(128)S(1)} %get-tuple-element.601) | copy-start | bytes 100 | tf_op jit(solution)/shard_map/while
  132.7 8.2 %copy-start.1 = (bf16[8,3,64,128]{3,2,1,0:T(8,128)(2,1)}, bf16[8,3,64,128]{3,2,1,0:T(8,128)(2,1)S(1)}, u32[]{:S(2)}) copy-start(bf16[8,3,64,128]{3,2,1,0:T(8,128)(2,1)S(1)} %multiply_convert_fusion.8) | copy-start | bytes 1179652 | tf_op jit(solution)/shard_map/while
  132.8 8.2 %copy-start.22 = (f32[8]{0:T(128)S(1)}, f32[8]{0:T(128)}, u32[]{:S(2)}) copy-start(f32[8]{0:T(128)} %copy-done.21) | copy-start | bytes 100 | tf_op jit(solution)/shard_map/while
  132.8 8.2 %copy-start.23 = (f32[8]{0:T(128)S(1)}, f32[8]{0:T(128)}, u32[]{:S(2)}) copy-start(f32[8]{0:T(128)} %get-tuple-element.610) | copy-start | bytes 100 | tf_op jit(solution)/shard_map/while
  158.8 10.3 %copy-start.10 = (f32[4,4,3,3,64]{4,3,1,2,0:T(4,128)}, f32[4,4,3,3,64]{4,3,1,2,0:T(4,128)S(1)}, u32[]{:S(2)}) copy-start(f32[4,4,3,3,64]{4,3,1,2,0:T(4,128)S(1)} %copy_dynamic-update-slice_fusion.5) | copy-start | bytes 110596 | tf_op jit(solution)/shard_map/while
  158.8 10.3 %copy-start.2 = (bf16[8,3,64,128]{3,2,1,0:T(8,128)(2,1)S(1)}, bf16[8,3,64,128]{3,2,1,0:T(8,128)(2,1)}, u32[]{:S(2)}) copy-start(bf16[8,3,64,128]{3,2,1,0:T(8,128)(2,1)} %copy-done.1) | copy-start | bytes 1179652 | tf_op jit(solution)/shard_map/while
  158.8 10.4 %copy-start.3 = (f32[4,4,3,64,128]{4,3,1,2,0:T(8,128)S(1)}, f32[4,4,3,64,128]{4,3,1,2,0:T(8,128)}, u32[]{:S(2)}) copy-start(f32[4,4,3,64,128]{4,3,1,2,0:T(8,128)} %get-tuple-element.640) | copy-start | bytes 4718596 | tf_op jit(solution)/shard_map/while
  169.2 6.6 %copy-start.8 = (f32[128,128]{1,0:T(8,128)S(1)}, f32[128,128]{1,0:T(8,128)}, u32[]{:S(2)}) copy-start(f32[128,128]{1,0:T(8,128)} %get-tuple-element.702) | copy-start | bytes 196612 | tf_op jit(solution)/shard_map/while
  169.2 6.6 %copy-start.13 = (f32[4,4,3,4,64]{4,3,2,1,0:T(4,128)S(1)}, f32[4,4,3,4,64]{4,3,2,1,0:T(4,128)}, u32[]{:S(2)}) copy-start(f32[4,4,3,4,64]{4,3,2,1,0:T(4,128)} %copy-done.12) | copy-start | bytes 147460 | tf_op jit(solution)/shard_map/while
  179.7 13.6 %copy-start.17 = (s32[64]{0:T(128)}, s32[64]{0:T(128)S(1)}, u32[]{:S(2)}) copy-start(s32[64]{0:T(128)S(1)} %iota_add_fusion.3) | copy-start | bytes 772 | tf_op jit(solution)/shard_map/while
  180.1 13.2 %copy-start.19 = (f32[64]{0:T(128)}, f32[64]{0:T(128)S(1)}, u32[]{:S(2)}) copy-start(f32[64]{0:T(128)S(1)} %slice_bitcast_fusion.15) | copy-start | bytes 772 | tf_op jit(solution)/shard_map/while
  181.0 12.3 %copy-start.21 = (f32[8]{0:T(128)}, f32[8]{0:T(128)S(1)}, u32[]{:S(2)}) copy-start(f32[8]{0:T(128)S(1)} %get-tuple-element.601) | copy-start | bytes 100 | tf_op jit(solution)/shard_map/while
  202.5 8.2 %copy-start.1 = (bf16[8,3,64,128]{3,2,1,0:T(8,128)(2,1)}, bf16[8,3,64,128]{3,2,1,0:T(8,128)(2,1)S(1)}, u32[]{:S(2)}) copy-start(bf16[8,3,64,128]{3,2,1,0:T(8,128)(2,1)S(1)} %multiply_convert_fusion.8) | copy-start | bytes 1179652 | tf_op jit(solution)/shard_map/while
  202.5 8.2 %copy-start.22 = (f32[8]{0:T(128)S(1)}, f32[8]{0:T(128)}, u32[]{:S(2)}) copy-start(f32[8]{0:T(128)} %copy-done.21) | copy-start | bytes 100 | tf_op jit(solution)/shard_map/while
  202.5 8.2 %copy-start.23 = (f32[8]{0:T(128)S(1)}, f32[8]{0:T(128)}, u32[]{:S(2)}) copy-start(f32[8]{0:T(128)} %get-tuple-element.610) | copy-start | bytes 100 | tf_op jit(solution)/shard_map/while
  228.5 10.3 %copy-start.10 = (f32[4,4,3,3,64]{4,3,1,2,0:T(4,128)}, f32[4,4,3,3,64]{4,3,1,2,0:T(4,128)S(1)}, u32[]{:S(2)}) copy-start(f32[4,4,3,3,64]{4,3,1,2,0:T(4,128)S(1)} %copy_dynamic-update-slice_fusion.5) | copy-start | bytes 110596 | tf_op jit(solution)/shard_map/while
  228.5 10.3 %copy-start.2 = (bf16[8,3,64,128]{3,2,1,0:T(8,128)(2,1)S(1)}, bf16[8,3,64,128]{3,2,1,0:T(8,128)(2,1)}, u32[]{:S(2)}) copy-start(bf16[8,3,64,128]{3,2,1,0:T(8,128)(2,1)} %copy-done.1) | copy-start | bytes 1179652 | tf_op jit(solution)/shard_map/while
  228.5 10.4 %copy-start.3 = (f32[4,4,3,64,128]{4,3,1,2,0:T(8,128)S(1)}, f32[4,4,3,64,128]{4,3,1,2,0:T(8,128)}, u32[]{:S(2)}) copy-start(f32[4,4,3,64,128]{4,3,1,2,0:T(8,128)} %get-tuple-element.640) | copy-start | bytes 4718596 | tf_op jit(solution)/shard_map/while
  238.9 6.6 %copy-start.8 = (f32[128,128]{1,0:T(8,128)S(1)}, f32[128,128]{1,0:T(8,128)}, u32[]{:S(2)}) copy-start(f32[128,128]{1,0:T(8,128)} %get-tuple-element.702) | copy-start | bytes 196612 | tf_op jit(solution)/shard_map/while
  249.5 13.6 %copy-start.17 = (s32[64]{0:T(128)}, s32[64]{0:T(128)S(1)}, u32[]{:S(2)}) copy-start(s32[64]{0:T(128)S(1)} %iota_add_fusion.3) | copy-start | bytes 772 | tf_op jit(solution)/shard_map/while
  249.8 13.2 %copy-start.19 = (f32[64]{0:T(128)}, f32[64]{0:T(128)S(1)}, u32[]{:S(2)}) copy-start(f32[64]{0:T(128)S(1)} %slice_bitcast_fusion.15) | copy-start | bytes 772 | tf_op jit(solution)/shard_map/while
  250.8 12.3 %copy-start.21 = (f32[8]{0:T(128)}, f32[8]{0:T(128)S(1)}, u32[]{:S(2)}) copy-start(f32[8]{0:T(128)S(1)} %get-tuple-element.601) | copy-start | bytes 100 | tf_op jit(solution)/shard_map/while
  272.2 8.2 %copy-start.1 = (bf16[8,3,64,128]{3,2,1,0:T(8,128)(2,1)}, bf16[8,3,64,128]{3,2,1,0:T(8,128)(2,1)S(1)}, u32[]{:S(2)}) copy-start(bf16[8,3,64,128]{3,2,1,0:T(8,128)(2,1)S(1)} %multiply_convert_fusion.8) | copy-start | bytes 1179652 | tf_op jit(solution)/shard_map/while
  272.2 8.2 %copy-start.22 = (f32[8]{0:T(128)S(1)}, f32[8]{0:T(128)}, u32[]{:S(2)}) copy-start(f32[8]{0:T(128)} %copy-done.21) | copy-start | bytes 100 | tf_op jit(solution)/shard_map/while
  272.2 8.2 %copy-start.23 = (f32[8]{0:T(128)S(1)}, f32[8]{0:T(128)}, u32[]{:S(2)}) copy-start(f32[8]{0:T(128)} %get-tuple-element.610) | copy-start | bytes 100 | tf_op jit(solution)/shard_map/while
  298.2 10.3 %copy-start.10 = (f32[4,4,3,3,64]{4,3,1,2,0:T(4,128)}, f32[4,4,3,3,64]{4,3,1,2,0:T(4,128)S(1)}, u32[]{:S(2)}) copy-start(f32[4,4,3,3,64]{4,3,1,2,0:T(4,128)S(1)} %copy_dynamic-update-slice_fusion.5) | copy-start | bytes 110596 | tf_op jit(solution)/shard_map/while
  298.2 10.3 %copy-start.2 = (bf16[8,3,64,128]{3,2,1,0:T(8,128)(2,1)S(1)}, bf16[8,3,64,128]{3,2,1,0:T(8,128)(2,1)}, u32[]{:S(2)}) copy-start(bf16[8,3,64,128]{3,2,1,0:T(8,128)(2,1)} %copy-done.1) | copy-start | bytes 1179652 | tf_op jit(solution)/shard_map/while
  298.2 10.4 %copy-start.3 = (f32[4,4,3,64,128]{4,3,1,2,0:T(8,128)S(1)}, f32[4,4,3,64,128]{4,3,1,2,0:T(8,128)}, u32[]{:S(2)}) copy-start(f32[4,4,3,64,128]{4,3,1,2,0:T(8,128)} %get-tuple-element.640) | copy-start | bytes 4718596 | tf_op jit(solution)/shard_map/while
  308.6 6.6 %copy-start.8 = (f32[128,128]{1,0:T(8,128)S(1)}, f32[128,128]{1,0:T(8,128)}, u32[]{:S(2)}) copy-start(f32[128,128]{1,0:T(8,128)} %get-tuple-element.702) | copy-start | bytes 196612 | tf_op jit(solution)/shard_map/while
  308.6 6.6 %copy-start.13 = (f32[4,4,3,4,64]{4,3,2,1,0:T(4,128)S(1)}, f32[4,4,3,4,64]{4,3,2,1,0:T(4,128)}, u32[]{:S(2)}) copy-start(f32[4,4,3,4,64]{4,3,2,1,0:T(4,128)} %copy-done.12) | copy-start | bytes 147460 | tf_op jit(solution)/shard_map/while
  318.9 11.2 %collective-permute-start.12 = (bf16[4,4,1,8384]{3,1,2,0:T(4,128)(2,1)S(1)}, bf16[4,4,1,8384]{3,1,2,0:T(4,128)(2,1)S(1)}, u32[]{:S(2)}, u32[]{:S(2)}) collective-permute-start(bf16[4,4,1,8384]{3,1,2,0:T(4,128)(2,1)S(1)} %get-tuple-element.486), channel_id=1, source_target_pairs={{0,1},{1,2},{2,3},{3,0},{4,5},{5,6},{6,7},{7,4},{8,9},{9,10},{10,1... | collective-permute-start | bytes 804872 | tf_op jit(solution)/shard_map/ppermute | solution.py:30
  320.3 14.0 %collective-permute-start.13 = (bf16[4,4,1,8384]{3,1,2,0:T(4,128)(2,1)S(1)}, bf16[4,4,1,8384]{3,1,2,0:T(4,128)(2,1)S(1)}, u32[]{:S(2)}, u32[]{:S(2)}) collective-permute-start(bf16[4,4,1,8384]{3,1,2,0:T(4,128)(2,1)S(1)} %get-tuple-element.487), channel_id=1, source_target_pairs={{1,0},{2,1},{3,2},{0,3},{5,4},{6,5},{7,6},{4,7},{9,8},{10,9},{11,1... | collective-permute-start | bytes 804872 | tf_op jit(solution)/shard_map/ppermute | solution.py:33
  335.0 4.5 %collective-permute-start.14 = (bf16[4,1,1,8384]{3,1,2,0:T(2,128)(2,1)S(1)}, bf16[4,1,1,8384]{3,1,2,0:T(2,128)(2,1)S(1)}, u32[]{:S(2)}, u32[]{:S(2)}) collective-permute-start(bf16[4,1,1,8384]{3,1,2,0:T(2,128)(2,1)S(1)} %get-tuple-element.488), channel_id=1, source_target_pairs={{0,4},{4,8},{8,12},{12,0},{1,5},{5,9},{9,13},{13,1},{2,6},{6,10},{... | collective-permute-start | bytes 201224 | tf_op jit(solution)/shard_map/ppermute | solution.py:30
  335.1 4.6 %collective-permute-start.15 = (bf16[4,1,1,8384]{3,1,2,0:T(2,128)(2,1)S(1)}, bf16[4,1,1,8384]{3,1,2,0:T(2,128)(2,1)S(1)}, u32[]{:S(2)}, u32[]{:S(2)}) collective-permute-start(bf16[4,1,1,8384]{3,1,2,0:T(2,128)(2,1)S(1)} %get-tuple-element.491), channel_id=1, source_target_pairs={{4,0},{8,4},{12,8},{0,12},{5,1},{9,5},{13,9},{1,13},{6,2},{10,6},{... | collective-permute-start | bytes 201224 | tf_op jit(solution)/shard_map/ppermute | solution.py:33
  341.0 4.2 %collective-permute-start.17 = (bf16[1,2,1,8384]{3,1,2,0:T(2,128)(2,1)S(1)}, bf16[1,2,1,8384]{3,1,2,0:T(2,128)(2,1)S(1)}, u32[]{:S(2)}, u32[]{:S(2)}) collective-permute-start(bf16[1,2,1,8384]{3,1,2,0:T(2,128)(2,1)S(1)} %get-tuple-element.494), channel_id=1, source_target_pairs={{16,0},{0,16},{17,1},{1,17},{18,2},{2,18},{19,3},{3,19},{20,4},{4,... | collective-permute-start | bytes 100616 | tf_op jit(solution)/shard_map/ppermute | solution.py:33
  341.6 4.3 %collective-permute-start.16 = (bf16[1,2,1,8384]{3,1,0,2:T(2,128)(2,1)S(1)}, bf16[1,2,1,8384]{3,1,0,2:T(2,128)(2,1)S(1)}, u32[]{:S(2)}, u32[]{:S(2)}) collective-permute-start(bf16[1,2,1,8384]{3,1,0,2:T(2,128)(2,1)S(1)} %get-tuple-element.492), channel_id=1, source_target_pairs={{0,16},{16,0},{1,17},{17,1},{2,18},{18,2},{3,19},{19,3},{4,20},{20... | collective-permute-start | bytes 100616 | tf_op jit(solution)/shard_map/ppermute | solution.py:30
  (43 other events, 113.0 us)
where the time goes:
time: 350 us; the launch traced here: 348 us
  other arithmetic  130 us (37%)
  matrix products  77.6 us (22%)
  local copies, waits for them, and re-layouts  76 us (22%)
  waiting for transfers between devices  28.1 us (8%)
  starting transfers between devices  24.1 us (7%)
  loops' own time  11.1 us (3%)
    reduce_sum x4, other arithmetic, edge_terms(): jnp.sqrt(2.0 / CUTOFF)  62.3 us
    mul x4, other arithmetic, edge_terms(): radial_part = bessel * envelope[None]  49 us
    dot_general x4, local copies, waits for them, and re-layouts, cell_terms(): lax.dot_general(edge_half, d_half, (((0,), (0,)), ((), ())), preferred_el...  41.2 us
    dot_general x4, matrix products, cell_terms(): lax.dot_general(d_half, near_feat, (((1,), (1,)), ((), ())), preferred_el...  32.7 us
    dot_general x4, matrix products, cell_terms(): lax.dot_general(edge_half, d_half, (((0,), (0,)), ((), ())), preferred_el...  20.5 us
    ppermute x9, waiting for transfers between devices, extended(): lax.ppermute(lax.slice_in_dim(block, block.shape[dim] - width, None, axis...  18.1 us
    ppermute x9, starting transfers between devices, extended(): lax.ppermute(lax.slice_in_dim(block, 0, width, axis=dim), axis, backward)  15.2 us
    another operation x1, loops' own time, body(): lax.scan(visit_cell, start, jnp.arange(cells_x * cells_y * cells_z, dtype...  11.1 us
  transfers between devices with their start and end apart: 18, of which 11 were waited for; matrix products, arithmetic and copies ran while one was open for 1% of the time, Pallas kernels for 0%

commit v1 on v0

v1 whole, which is shorter than its diff:
```python
import functools
import math

import jax
import jax.numpy as jnp
import numpy as np
from jax import lax
from jax.experimental import pallas as pl
from jax.experimental.pallas import tpu as pltpu
from jax.sharding import PartitionSpec as P

SIDE = 7.0
CUTOFF = 5.0
JITTER = 0.3
BLOCK = 2
HIGH = lax.Precision.HIGHEST


def lattice_of(capacity):
    lat = round(capacity ** (1.0 / 3.0))
    spacing = SIDE / lat
    reach = 0
    while (reach + 1 - 2 * JITTER) * spacing < CUTOFF:
        reach += 1
    return lat, spacing, reach


def pair_fields(pj, pi):
    dx = pj[0:1, :] - pi[:, 0:1]
    dy = pj[1:2, :] - pi[:, 1:2]
    dz = pj[2:3, :] - pi[:, 2:3]
    sq = dx * dx + dy * dy + dz * dz
    near = jnp.logical_and(sq < CUTOFF * CUTOFF, sq > 0.01)
    weight = jnp.where(near, pj[3:4, :] * pi[:, 3:4], 0.0)
    safe = jnp.where(near, sq, 1.0)
    inv = lax.rsqrt(safe)
    r = safe * inv
    u = r * (1.0 / CUTOFF)
    u2 = u * u
    u5 = u2 * u2 * u
    env = 1.0 + u5 * u * (-28.0 + u * (48.0 - 21.0 * u))
    denv = u5 * (-168.0 + u * (336.0 - 168.0 * u)) * (1.0 / CUTOFF)
    amp = weight * inv * math.sqrt(2.0 / CUTOFF)
    q = amp * env
    p = amp * denv - q * inv
    t = u * math.pi - 0.5 * math.pi
    t2 = t * t
    cos_t = 1.0 + t2 * (
        -1.0 / 2 + t2 * (1.0 / 24 + t2 * (-1.0 / 720 + t2 * (1.0 / 40320 + t2 * (-1.0 / 3628800 + t2 * (1.0 / 479001600)))))
    )
    sin_t = t * (
        1.0 + t2 * (-1.0 / 6 + t2 * (1.0 / 120 + t2 * (-1.0 / 5040 + t2 * (1.0 / 362880 + t2 * (-1.0 / 39916800)))))
    )
    return dx * inv, dy * inv, dz * inv, inv, q, p, cos_t, -sin_t


def compute_kernel(
    dims,
    feat_ref,
    posj_ref,
    rpos_ref,
    radial_ref,
    coupling_ref,
    mixing_ref,
    hw_ref,
    ow_ref,
    fgrad_ref,
    fj_ref,
    node_ref,
    slab_ref,
    edge_ref,
    field_ref,
    sv_ref,
    en_ref,
    acc_ref,
    g_ref,
):
    sx, sy, sz, reach, nb = dims
    nbx, nby = sx // BLOCK, sy // BLOCK
    wide = BLOCK + 2 * reach
    depth = sz + 2 * reach
    rows = wide * depth
    near = wide * rows
    own = BLOCK * BLOCK * sz
    px = sx + 2 * reach
    chunks = [(c, min(128, near - c)) for c in range(0, near, 128)]
    root3 = math.sqrt(3.0)

    def build(x, carry):
        full = feat_ref[x].astype(jnp.float32)
        for by in range(nby):
            start = by * BLOCK * depth
            slab_ref[by, x] = full[start : start + rows].astype(jnp.bfloat16)
            acc_ref[by, x] = jnp.zeros((rows, full.shape[1]), jnp.float32)
        return carry

    lax.fori_loop(0, px, build, 0)

    def forward(blk, carry):
        by, bx = blk // nbx, lax.rem(blk, nbx)
        pi = rpos_ref[blk]
        for c, w in chunks:
            pj = posj_ref[blk, :, c : c + w]
            nx, ny, nz, inv, q, p, s1, c1 = pair_fields(pj, pi)
            field_ref[blk, 0, :, c : c + w] = nx
            field_ref[blk, 1, :, c : c + w] = ny
            field_ref[blk, 2, :, c : c + w] = nz
            field_ref[blk, 3, :, c : c + w] = inv
            field_ref[blk, 4, :, c : c + w] = q
            field_ref[blk, 5, :, c : c + w] = p
            field_ref[blk, 6, :, c : c + w] = s1
            field_ref[blk, 7, :, c : c + w] = c1
            twice = 2.0 * c1
            before, now = jnp.zeros_like(s1), s1
            q3 = root3 * q
            qs = (q, q3 * nx, q3 * ny, q3 * nz)
            for b in range(nb):
                for m in range(4):
                    k = (b * 4 + m) * own
                    edge_ref[blk, k : k + own, c : c + w] = (qs[m] * now).astype(jnp.bfloat16)
                before, now = now, twice * now - before
        slab = slab_ref[by, pl.ds(bx * BLOCK, wide)].reshape(near, -1)
        summed = jnp.dot(edge_ref[blk], slab, preferred_element_type=jnp.float32)
        for m in range(4):
            total = None
            for b in range(nb):
                k = (b * 4 + m) * own
                term = summed[k : k + own] * radial_ref[min(m, 1), b : b + 1, :]
                total = term if total is None else total + term
            sv_ref[m, pl.ds(blk * own, own)] = total
        return carry

    lax.fori_loop(0, nbx * nby, forward, 0)

    flat = rpos_ref[...].reshape(nbx * nby * own, -1)
    occ = flat[:, 3:4]
    kind = flat[:, 4:5]
    spec = lax.broadcasted_iota(jnp.int32, (flat.shape[0], coupling_ref.shape[1]), 1)
    onehot = (kind.astype(jnp.int32) == spec).astype(jnp.float32)
    wq = [
        jnp.dot(onehot, coupling_ref[n], precision=HIGH, preferred_element_type=jnp.float32)
        for n in range(3)
    ]
    scalar = sv_ref[0]
    length_sq = sv_ref[1] * sv_ref[1] + sv_ref[2] * sv_ref[2] + sv_ref[3] * sv_ref[3]
    product = wq[0] * scalar + wq[1] * scalar * scalar + wq[2] * length_sq
    fold = jnp.dot(mixing_ref[...], hw_ref[...], precision=HIGH, preferred_element_type=jnp.float32)
    hidden = jnp.dot(product, fold, precision=HIGH, preferred_element_type=jnp.float32)
    logistic = jax.nn.sigmoid(hidden)
    energy = occ * jnp.sum(ow_ref[...] * hidden * logistic, axis=1, keepdims=True)
    d_hidden = occ * ow_ref[...] * logistic * (1.0 + hidden * (1.0 - logistic))
    d_product = lax.dot_general(
        d_hidden, fold, (((1,), (1,)), ((), ())), precision=HIGH, preferred_element_type=jnp.float32
    )
    en_ref[...] = jnp.broadcast_to(energy, en_ref.shape)
    sv_ref[0] = d_product * (wq[0] + 2.0 * wq[1] * scalar)
    twice_d = 2.0 * wq[2] * d_product
    for m in range(1, 4):
        sv_ref[m] = twice_d * sv_ref[m]

    def backward(blk, carry):
        by, bx = blk // nbx, lax.rem(blk, nbx)
        parts = []
        for b in range(nb):
            for m in range(4):
                parts.append(
                    sv_ref[m, pl.ds(blk * own, own)] * radial_ref[min(m, 1), b : b + 1, :]
                )
        d_full = jnp.concatenate(parts, axis=0)
        d_half = d_full.astype(jnp.bfloat16)
        slab = slab_ref[by, pl.ds(bx * BLOCK, wide)].reshape(near, -1)
        g_ref[...] = lax.dot_general(
            d_half, slab, (((1,), (1,)), ((), ())), preferred_element_type=jnp.float32
        )
        d_turn = d_full.T.astype(jnp.bfloat16)
        turned = jnp.dot(d_turn, edge_ref[blk], preferred_element_type=jnp.float32)
        acc_ref[by, pl.ds(bx * BLOCK, wide)] += turned.T.reshape(wide, rows, -1)
        total = [jnp.zeros((own, 1), jnp.float32) for _ in range(3)]
        for c, w in chunks:
            nx, ny, nz, inv, q, p, s1, c1 = (field_ref[blk, n, :, c : c + w] for n in range(8))
            twice = 2.0 * c1
            s_before, s_now = jnp.zeros_like(s1), s1
            c_before, c_now = jnp.ones_like(c1), c1
            s_sum = [None] * 4
            c_sum = [None] * 4
            for b in range(nb):
                scaled = (b + 1.0) * c_now
                for m in range(4):
                    k = (b * 4 + m) * own
                    g = g_ref[k : k + own, c : c + w]
                    s_sum[m] = g * s_now if b == 0 else s_sum[m] + g * s_now
                    c_sum[m] = g * scaled if b == 0 else c_sum[m] + g * scaled
                s_before, s_now = s_now, twice * s_now - s_before
                c_before, c_now = c_now, twice * c_now - c_before
            s_dot = nx * s_sum[1] + ny * s_sum[2] + nz * s_sum[3]
            c_dot = nx * c_sum[1] + ny * c_sum[2] + nz * c_sum[3]
            slope = (q * (math.pi / CUTOFF)) * (c_sum[0] + root3 * c_dot) + p * (
                s_sum[0] + root3 * s_dot
            )
            across = root3 * q * inv
            along = slope - across * s_dot
            outs = [
                along * n + across * s_sum[m + 1] for m, n in enumerate((nx, ny, nz))
            ]
            for m in range(3):
                fj_ref[blk, m : m + 1, c : c + w] = -jnp.sum(outs[m], axis=0, keepdims=True)
                total[m] = total[m] + jnp.sum(outs[m], axis=1, keepdims=True)
        lane = lax.broadcasted_iota(jnp.int32, (own, node_ref.shape[1]), 1)
        here = pl.ds(blk * own, own)
        node_ref[here] = jnp.where(
            lane == 0,
            total[0],
            jnp.where(lane == 1, total[1], jnp.where(lane == 2, total[2], en_ref[here])),
        )
        return carry

    lax.fori_loop(0, nbx * nby, backward, 0)

    def merge(x, carry):
        fgrad_ref[x] = jnp.zeros(fgrad_ref.shape[1:], jnp.float32)
        for by in range(nby):
            start = by * BLOCK * depth
            fgrad_ref[x, start : start + rows] += acc_ref[by, x]
        return carry

    lax.fori_loop(0, px, merge, 0)


def shift(block, axis, up):
    count = lax.axis_size(axis)
    pairs = [(i, (i + 1) % count) for i in range(count)]
    if not up:
        pairs = [(b, a) for a, b in pairs]
    return lax.ppermute(block, axis, pairs)


def widen(block, axis, dim, reach):
    extent = block.shape[dim]
    low = shift(lax.slice_in_dim(block, extent - reach, extent, axis=dim), axis, True)
    high = shift(lax.slice_in_dim(block, 0, reach, axis=dim), axis, False)
    return jnp.concatenate([low, block, high], axis=dim)


def fold_back(block, axis, dim, reach):
    extent = block.shape[dim]
    low = lax.slice_in_dim(block, 0, reach, axis=dim).astype(jnp.bfloat16)
    high = lax.slice_in_dim(block, extent - reach, extent, axis=dim).astype(jnp.bfloat16)
    to_high = shift(low, axis, False).astype(block.dtype)
    to_low = shift(high, axis, True).astype(block.dtype)
    core = lax.slice_in_dim(block, reach, extent - reach, axis=dim)
    rest = extent - 3 * reach
    low_pad = [(0, 0)] * block.ndim
    high_pad = [(0, 0)] * block.ndim
    low_pad[dim] = (0, rest)
    high_pad[dim] = (rest, 0)
    return core + jnp.pad(to_low, low_pad) + jnp.pad(to_high, high_pad)


def body(
    local_pos,
    counts,
    species,
    features,
    radial_weights,
    coupling,
    mixing,
    hidden_weights,
    output_weights,
):
    cx, cy, cz = counts.shape
    capacity, channels = features.shape[3:]
    nb = radial_weights.shape[1]
    lat, spacing, reach = lattice_of(capacity)
    sx, sy, sz = cx * lat, cy * lat, cz * lat
    nbx, nby = sx // BLOCK, sy // BLOCK
    wide, depth = BLOCK + 2 * reach, sz + 2 * reach
    near, own = wide * wide * depth, BLOCK * BLOCK * sz
    px, py = sx + 2 * reach, sy + 2 * reach
    rows_full = -(-py * depth // 16) * 16

    occupied = (jnp.arange(capacity, dtype=jnp.int32) < counts[..., None]).astype(jnp.float32)
    site = jnp.clip(jnp.floor(local_pos * (1.0 / spacing)).astype(jnp.int32), 0, lat - 1)
    code = (site[:, :, :, 0] * lat + site[:, :, :, 1]) * lat + site[:, :, :, 2]
    place = code[:, :, :, None, :] == jnp.arange(capacity, dtype=jnp.int32)[:, None]
    place_half = place.astype(jnp.bfloat16)
    place_full = place.astype(jnp.float32)
    feat_sites = jnp.einsum(
        "xyzts,xyzsc->xyztc", place_half, features, preferred_element_type=jnp.float32
    ).astype(jnp.bfloat16)
    small = jnp.concatenate(
        [
            local_pos,
            occupied[:, :, :, None],
            species.astype(jnp.float32)[:, :, :, None],
        ],
        axis=3,
    )
    small_sites = jnp.einsum("xyzks,xyzts->kxyzt", small, place_full, precision=HIGH)

    feat_grid = feat_sites.reshape(cx, cy, cz, lat, lat, lat, channels)
    feat_grid = feat_grid.transpose(0, 3, 1, 4, 2, 5, 6).reshape(sx, sy, sz, channels)
    small_grid = small_sites.reshape(5, cx, cy, cz, lat, lat, lat)
    small_grid = small_grid.transpose(0, 1, 4, 2, 5, 3, 6).reshape(5, sx, sy, sz)

    feat_pad = widen(feat_grid, "gz", 2, reach)
    feat_pad = widen(feat_pad, "gy", 1, reach)
    feat_pad = widen(feat_pad, "gx", 0, reach)
    feat_pad = feat_pad.reshape(px, py * depth, channels)
    feat_pad = jnp.pad(feat_pad, ((0, 0), (0, rows_full - py * depth), (0, 0)))
    pos_pad = small_grid[:4]
    for axis, dim in (("gz", 3), ("gy", 2), ("gx", 1)):
        pos_pad = widen(pos_pad, axis, dim, reach)
    steps = [
        np.floor((np.arange(n) - reach) / lat).astype(np.float32) * SIDE
        for n in (px, py, depth)
    ]
    shifts = np.zeros((4, px, py, depth), np.float32)
    shifts[0] = steps[0][:, None, None]
    shifts[1] = steps[1][None, :, None]
    shifts[2] = steps[2][None, None, :]
    pos_pad = pos_pad + shifts
    posj = jnp.stack(
        [
            pos_pad[:, bx * BLOCK : bx * BLOCK + wide, by * BLOCK : by * BLOCK + wide].reshape(4, near)
            for by in range(nby)
            for bx in range(nbx)
        ]
    )
    own_shift = np.concatenate(
        [shifts[:, reach : reach + sx, reach : reach + sy, reach : reach + sz], np.zeros((1, sx, sy, sz), np.float32)]
    )
    rpos = (small_grid + own_shift).reshape(5, nbx, BLOCK, nby, BLOCK, sz)
    rpos = rpos.transpose(3, 1, 2, 4, 5, 0).reshape(nby * nbx, own, 5)
    rpos = jnp.pad(rpos, ((0, 0), (0, 0), (0, 3)))

    spec_pad = -(-coupling.shape[1] // 8) * 8 - coupling.shape[1]
    total_own = sx * sy * sz
    rows = wide * depth
    blocks = nbx * nby
    vmem = pl.BlockSpec(memory_space=pltpu.VMEM)
    fgrad, fj, node = pl.pallas_call(
        functools.partial(compute_kernel, (sx, sy, sz, reach, nb)),
        out_shape=(
            jax.ShapeDtypeStruct((px, rows_full, channels), jnp.float32),
            jax.ShapeDtypeStruct((blocks, 3, near), jnp.float32),
            jax.ShapeDtypeStruct((total_own, 128), jnp.float32),
        ),
        in_specs=[vmem] * 8,
        out_specs=(vmem, vmem, vmem),
        scratch_shapes=[
            pltpu.VMEM((nby, px, rows, channels), jnp.bfloat16),
            pltpu.VMEM((blocks, nb * 4 * own, near), jnp.bfloat16),
            pltpu.VMEM((blocks, 8, own, near), jnp.float32),
            pltpu.VMEM((4, total_own, channels), jnp.float32),
            pltpu.VMEM((total_own, 128), jnp.float32),
            pltpu.VMEM((nby, px, rows, channels), jnp.float32),
            pltpu.VMEM((nb * 4 * own, near), jnp.float32),
        ],
        compiler_params=pltpu.CompilerParams(vmem_limit_bytes=50 * 1024 * 1024),
        name="pair_layer",
    )(
        feat_pad,
        posj,
        rpos,
        radial_weights,
        jnp.pad(coupling, ((0, 0), (0, spec_pad), (0, 0))),
        mixing,
        hidden_weights,
        output_weights[None, :],
    )

    grad = fgrad[:, : py * depth].reshape(px, py, depth, channels)
    for axis, dim in (("gx", 0), ("gy", 1), ("gz", 2)):
        grad = fold_back(grad, axis, dim, reach)
    fj = fj.reshape(nby, nbx, 3, wide, wide, depth)
    force = jnp.zeros((3, px, py, depth), jnp.float32)
    for by in range(nby):
        for bx in range(nbx):
            force = force + jnp.pad(
                fj[by, bx],
                (
                    (0, 0),
                    (bx * BLOCK, px - wide - bx * BLOCK),
                    (by * BLOCK, py - wide - by * BLOCK),
                    (0, 0),
                ),
            )
    for axis, dim in (("gx", 1), ("gy", 2), ("gz", 3)):
        force = fold_back(force, axis, dim, reach)
    node = node[:, :4].reshape(nby, nbx, BLOCK, BLOCK, sz, 4)
    node = node.transpose(5, 1, 2, 0, 3, 4).reshape(4, sx, sy, sz)
    node = node + jnp.pad(force, ((0, 1), (0, 0), (0, 0), (0, 0)))

    def to_cells(grid):
        lead = grid.shape[3:]
        cells = grid.reshape((cx, lat, cy, lat, cz, lat) + lead)
        cells = cells.transpose((0, 2, 4, 1, 3, 5) + tuple(range(6, cells.ndim)))
        return cells.reshape((cx, cy, cz, capacity) + lead)

    feature_grad = jnp.einsum("xyzts,xyztc->xyzsc", place_full, to_cells(grad), precision=HIGH)
    node_slots = jnp.einsum(
        "xyzts,xyztk->xyzks", place_full, to_cells(node.transpose(1, 2, 3, 0)), precision=HIGH
    )
    return (node_slots[:, :, :, 3], node_slots[:, :, :, :3], feature_grad)


def solution(mesh):
    placed = (
        P("gx", "gy", "gz", None, None),
        P("gx", "gy", "gz"),
        P("gx", "gy", "gz", None),
        P("gx", "gy", "gz", None, None),
        P(),
        P(),
        P(),
        P(),
        P(),
    )
    return jax.shard_map(
        body,
        mesh=mesh,
        in_specs=placed,
        out_specs=(
            P("gx", "gy", "gz", None),
            P("gx", "gy", "gz", None, None),
            P("gx", "gy", "gz", None, None),
        ),
        check_vma=False,
    )
```

time: 350 us -> 105 us (0.30)
  other arithmetic: 130 us -> 3.84 us
  matrix products: 77.6 us -> 1.71 us
  local copies, waits for them, and re-layouts: 76 us -> 15 us
  Pallas kernels: 0 us -> 21.3 us
  loops' own time: 11.1 us -> 0 us
  starting transfers between devices: 24.1 us -> 32.3 us
    dot_general x32 -> x4, matrix products: 77.6 us -> 1.71 us  [the longest x1 0.92 us: body(): jnp.einsum('xyzts,xyztc->xyzsc', place_full, to_cells(grad), precision=HIGH)]
    reduce_sum x28 -> x0, other arithmetic: 67.3 us -> none  [the longest x4 62.3 us: edge_terms(): jnp.sqrt(2.0 / CUTOFF)]
    mul x28 -> x0, other arithmetic: 55 us -> none  [the longest x4 49 us: edge_terms(): radial_part = bessel * envelope[None]]
    dot_general x4 -> x0, local copies, waits for them, and re-layouts: 41.2 us -> none  [cell_terms(): lax.dot_general(edge_half, d_half, (((0,), (0,)), ((), ())), preferred_el...]
    pallas_call x0 -> x1, Pallas kernels: none -> 21.3 us  [body(): pl.pallas_call(functools.partial(compute_kernel, (sx, sy, sz, reach, nb))...]
    another operation x1 -> x0, loops' own time: 11.1 us -> none  [body(): lax.scan(visit_cell, start, jnp.arange(cells_x * cells_y * cells_z, dtype...]
    while x168 -> x0, local copies, waits for them, and re-layouts: 8.26 us -> none
    ppermute x18 -> x24, starting transfers between devices: 24.1 us -> 32.3 us  [shift(): return lax.ppermute(block, axis, pairs)]
  transfers between devices with their start and end apart: 18 -> 24, of which waited for: 11 -> 14; matrix products, arithmetic and copies ran while one was open for 1% -> 11% of each run, Pallas kernels for 0% -> 0%
where the time goes in v1:
time: 105 us
  starting transfers between devices  32.3 us (31%)
  waiting for transfers between devices  29.4 us (28%)
  Pallas kernels  21.3 us (20%)
  local copies, waits for them, and re-layouts  15 us (14%)
  other arithmetic  3.84 us (4%)
  matrix products  1.71 us (2%)
  between operations  1.2 us (1%)
    ppermute x24, starting transfers between devices, shift(): return lax.ppermute(block, axis, pairs)  32.3 us
    ppermute x24, waiting for transfers between devices, shift(): return lax.ppermute(block, axis, pairs)  29.4 us
    pallas_call x1, Pallas kernels, body(): pl.pallas_call(functools.partial(compute_kernel, (sx, sy, sz, reach, nb))...  21.3 us
    slice x17, local copies, waits for them, and re-layouts, body(): pos_pad[:, bx * BLOCK:bx * BLOCK + wide, by * BLOCK:by * BLOCK + wide]  4.77 us
    unnamed x36, local copies, waits for them, and re-layouts  2.78 us
    another operation x17, local copies, waits for them, and re-layouts, body(): jnp.stack([pos_pad[:, bx * BLOCK:bx * BLOCK + wide, by * BLOCK:by * BLOCK...  2.28 us
  transfers between devices with their start and end apart: 24, of which 14 were waited for; matrix products, arithmetic and copies ran while one was open for 11% of the time, Pallas kernels for 0%

profile of v1, /device:TPU:0, one launch (start us, length us, event | category | flops | bytes accessed | tf_op | source)
XLA Modules:
  0.0 104.8 jit_solution(10241635251709887922)
XLA Ops:
  0.6 0.7 convert_clamp_fusion
  1.4 0.7 copy.125
  2.1 0.7 convert_element_type.88
  2.8 0.7 compare_convert_fusion
  4.0 0.5 copy.128
  4.5 0.3 copy.181
  4.8 3.1 %collective-permute-start.6 = (f32[4,8,8,3]{2,1,3,0:T(8,128)S(1)}, f32[4,8,8,3]{2,1,3,0:T(8,128)S(1)}, u32[]{:S(2)}, u32[]{:S(2)}) collective-permute-start(f32[4,8,8,3]{2,1,3,0:T(8,128)S(1)} %get-tuple-element.81), channel_id=1, source_target_pairs={{0,1},{1,2},{2,3},{3,0},{4,5},{5,6},{6,7},{7,4},{8,9},{9,10},{10,1... | collective-permute-start | bytes 9224 | tf_op jit(solution)/shard_map/ppermute | solution.py:234
  7.9 2.1 %collective-permute-start.7 = (f32[4,8,8,3]{2,1,3,0:T(8,128)S(1)}, f32[4,8,8,3]{2,1,3,0:T(8,128)S(1)}, u32[]{:S(2)}, u32[]{:S(2)}) collective-permute-start(f32[4,8,8,3]{2,1,3,0:T(8,128)S(1)} %get-tuple-element.82), channel_id=1, source_target_pairs={{1,0},{2,1},{3,2},{0,3},{5,4},{6,5},{7,6},{4,7},{9,8},{10,9},{11,1... | collective-permute-start | bytes 9224 | tf_op jit(solution)/shard_map/ppermute | solution.py:234
  10.0 0.3 convolution_convert_fusion
  10.4 1.8 %collective-permute-done.6 = f32[4,8,8,3]{2,1,3,0:T(8,128)S(1)} collective-permute-done((f32[4,8,8,3]{2,1,3,0:T(8,128)S(1)}, f32[4,8,8,3]{2,1,3,0:T(8,128)S(1)}, u32[]{:S(2)}, u32[]{:S(2)}) %collective-permute-start.6) | collective-permute-done | bytes 3104 | tf_op jit(solution)/shard_map/ppermute | solution.py:234
  12.1 0.4 collective-permute-done.7
  12.8 1.7 %collective-permute-start.9 = (f32[4,8,3,10]{2,1,3,0:T(8,128)S(1)}, f32[4,8,3,10]{2,1,3,0:T(8,128)S(1)}, u32[]{:S(2)}, u32[]{:S(2)}) collective-permute-start(f32[4,8,3,10]{2,1,3,0:T(8,128)S(1)} %get-tuple-element.76), channel_id=1, source_target_pairs={{4,0},{8,4},{12,8},{0,12},{5,1},{9,5},{13,9},{1,13},{6,2},{10,6},{... | collective-permute-start | bytes 11528 | tf_op jit(solution)/shard_map/ppermute | solution.py:234
  14.5 0.6 fusion.34
  15.1 1.0 %collective-permute-start = (bf16[8,8,3,128]{3,0,2,1:T(8,128)(2,1)}, bf16[8,8,3,128]{3,0,2,1:T(8,128)(2,1)S(1)}, u32[]{:S(2)}, u32[]{:S(2)}) collective-permute-start(bf16[8,8,3,128]{3,0,2,1:T(8,128)(2,1)} %get-tuple-element.83), channel_id=1, source_target_pairs={{0,1},{1,2},{2,3},{3,0},{4,5},{5,6},{6,7},{7,4},{8,9},{9,10},{10,1... | collective-permute-start | bytes 147464 | tf_op jit(solution)/shard_map/ppermute | solution.py:234
  16.2 2.8 %collective-permute-start.1 = (bf16[8,8,3,128]{3,0,2,1:T(8,128)(2,1)S(1)}, bf16[8,8,3,128]{3,0,2,1:T(8,128)(2,1)S(1)}, u32[]{:S(2)}, u32[]{:S(2)}) collective-permute-start(bf16[8,8,3,128]{3,0,2,1:T(8,128)(2,1)S(1)} %get-tuple-element.84), channel_id=1, source_target_pairs={{1,0},{2,1},{3,2},{0,3},{5,4},{6,5},{7,6},{4,7},{9,8},{10,9},{11,1... | collective-permute-start | bytes 147464 | tf_op jit(solution)/shard_map/ppermute | solution.py:234
  19.2 1.6 %collective-permute-start.10 = (f32[4,3,14,10]{2,1,3,0:T(4,128)S(1)}, f32[4,3,14,10]{2,1,3,0:T(4,128)S(1)}, u32[]{:S(2)}, u32[]{:S(2)}) collective-permute-start(f32[4,3,14,10]{2,1,3,0:T(4,128)S(1)} %get-tuple-element.73), channel_id=1, source_target_pairs={{0,16},{16,0},{1,17},{17,1},{2,18},{18,2},{3,19},{19,3},{4,20},{20... | collective-permute-start | bytes 20168 | tf_op jit(solution)/shard_map/ppermute | solution.py:234
  20.7 0.5 collective-permute-start.11
  21.5 2.8 %collective-permute-done.10 = f32[4,3,14,10]{2,1,3,0:T(4,128)S(1)} collective-permute-done((f32[4,3,14,10]{2,1,3,0:T(4,128)S(1)}, f32[4,3,14,10]{2,1,3,0:T(4,128)S(1)}, u32[]{:S(2)}, u32[]{:S(2)}) %collective-permute-start.10) | collective-permute-done | bytes 6752 | tf_op jit(solution)/shard_map/ppermute | solution.py:234
  24.3 1.2 %collective-permute-done.11 = f32[4,3,14,10]{2,1,3,0:T(4,128)S(1)} collective-permute-done((f32[4,3,14,10]{2,1,3,0:T(4,128)S(1)}, f32[4,3,14,10]{2,1,3,0:T(4,128)S(1)}, u32[]{:S(2)}, u32[]{:S(2)}) %collective-permute-start.11) | collective-permute-done | bytes 6752 | tf_op jit(solution)/shard_map/ppermute | solution.py:234
  25.7 0.6 fusion.25
  26.3 0.3 copy.130
  26.7 0.3 copy.131
  27.2 0.3 copy.132
  27.6 0.3 copy.133
  28.0 0.3 copy.134
  28.4 0.3 copy.135
  28.8 0.3 copy.136
  29.2 0.3 copy.137
  29.6 0.3 copy.138
  30.0 0.3 copy.139
  30.4 0.3 copy.140
  30.8 0.3 copy.141
  31.2 0.3 copy.142
  33.1 1.7 %collective-permute-start.3 = (bf16[8,3,10,128]{3,0,2,1:T(8,128)(2,1)S(1)}, bf16[8,3,10,128]{3,0,2,1:T(8,128)(2,1)S(1)}, u32[]{:S(2)}, u32[]{:S(2)}) collective-permute-start(bf16[8,3,10,128]{3,0,2,1:T(8,128)(2,1)S(1)} %get-tuple-element.78), channel_id=1, source_target_pairs={{4,0},{8,4},{12,8},{0,12},{5,1},{9,5},{13,9},{1,13},{6,2},{10,6},{... | collective-permute-start | bytes 184328 | tf_op jit(solution)/shard_map/ppermute | solution.py:234
  34.9 1.9 %collective-permute-done.2 = bf16[8,3,10,128]{3,0,2,1:T(8,128)(2,1)S(1)} collective-permute-done((bf16[8,3,10,128]{3,0,2,1:T(8,128)(2,1)S(1)}, bf16[8,3,10,128]{3,0,2,1:T(8,128)(2,1)S(1)}, u32[]{:S(2)}, u32[]{:S(2)}) %collective-permute-start.2) | collective-permute-done | bytes 61472 | tf_op jit(solution)/shard_map/ppermute | solution.py:234
  36.9 1.6 %collective-permute-start.4 = (bf16[3,14,10,128]{3,0,2,1:T(4,128)(2,1)S(1)}, bf16[3,14,10,128]{3,0,2,1:T(4,128)(2,1)S(1)}, u32[]{:S(2)}, u32[]{:S(2)}) collective-permute-start(bf16[3,14,10,128]{3,0,2,1:T(4,128)(2,1)S(1)} %get-tuple-element.67), channel_id=1, source_target_pairs={{0,16},{16,0},{1,17},{17,1},{2,18},{18,2},{3,19},{19,3},{4,20},{20... | collective-permute-start | bytes 322568 | tf_op jit(solution)/shard_map/ppermute | solution.py:234
  38.5 0.5 collective-permute-start.5
  39.0 4.1 %collective-permute-done.4 = bf16[3,14,10,128]{3,0,2,1:T(4,128)(2,1)S(1)} collective-permute-done((bf16[3,14,10,128]{3,0,2,1:T(4,128)(2,1)S(1)}, bf16[3,14,10,128]{3,0,2,1:T(4,128)(2,1)S(1)}, u32[]{:S(2)}, u32[]{:S(2)}) %collective-permute-start.4) | collective-permute-done | bytes 107552 | tf_op jit(solution)/shard_map/ppermute | solution.py:234
  43.1 3.1 %collective-permute-done.5 = bf16[3,14,10,128]{3,0,2,1:T(4,128)(2,1)S(1)} collective-permute-done((bf16[3,14,10,128]{3,0,2,1:T(4,128)(2,1)S(1)}, bf16[3,14,10,128]{3,0,2,1:T(4,128)(2,1)S(1)}, u32[]{:S(2)}, u32[]{:S(2)}) %collective-permute-start.5) | collective-permute-done | bytes 107552 | tf_op jit(solution)/shard_map/ppermute | solution.py:234
  46.2 0.3 pad_maximum_fusion
  46.7 0.6 copy-done.1
  47.3 21.3 %pair_layer.1 = (f32[14,144,128]{2,1,0:T(8,128)S(1)}, f32[16,3,640]{2,1,0:T(4,128)S(1)}, f32[256,128]{1,0:T(8,128)S(1)}) custom-call(bf16[14,144,128]{2,1,0:T(8,128)(2,1)S(1)} %pad.164.feat_ref, f32[16,4,640]{2,1,0:T(4,128)S(1)} %constant_dynamic-update-slice_fusion.posj_ref, f32[16,16,8]{2,1,0:T(8,128)S(1)} %pad.165.rpos_ref, f32[2,8,128]{2,1,0:T(8,128)S(1)} %copy-done.2, ...), custom_call_target="tpu_custom_call" | custom-call | tf_op jit(solution)/shard_map/pair_layer/pallas_call | solution.py:341
  68.6 1.6 %reshape.124 = f32[4,4,3,8,8,10]{5,4,3,2,1,0:T(8,128)S(1)} reshape(f32[16,3,640]{2,1,0:T(4,128)S(1)} %get-tuple-element.7) | data formatting | bytes 245760 | tf_op jit(solution)/shard_map/reshape | solution.py:375
  70.4 0.3 fusion.23
  70.7 1.6 %collective-permute-start.12 = (bf16[3,3,14,10]{3,2,1,0:T(8,128)(2,1)S(1)}, bf16[3,3,14,10]{3,2,1,0:T(8,128)(2,1)S(1)}, u32[]{:S(2)}, u32[]{:S(2)}) collective-permute-start(bf16[3,3,14,10]{3,2,1,0:T(8,128)(2,1)S(1)} %get-tuple-element.69), channel_id=1, source_target_pairs={{0,16},{16,0},{1,17},{17,1},{2,18},{18,2},{3,19},{19,3},{4,20},{20... | collective-permute-start | bytes 7568 | tf_op jit(solution)/shard_map/ppermute | solution.py:234
  72.3 0.5 collective-permute-start.13
  72.8 1.9 %collective-permute-done.12 = bf16[3,3,14,10]{3,2,1,0:T(8,128)(2,1)S(1)} collective-permute-done((bf16[3,3,14,10]{3,2,1,0:T(8,128)(2,1)S(1)}, bf16[3,3,14,10]{3,2,1,0:T(8,128)(2,1)S(1)}, u32[]{:S(2)}, u32[]{:S(2)}) %collective-permute-start.12) | collective-permute-done | bytes 2552 | tf_op jit(solution)/shard_map/ppermute | solution.py:234
  74.8 1.5 %collective-permute-done.13 = bf16[3,3,14,10]{3,2,1,0:T(8,128)(2,1)S(1)} collective-permute-done((bf16[3,3,14,10]{3,2,1,0:T(8,128)(2,1)S(1)}, bf16[3,3,14,10]{3,2,1,0:T(8,128)(2,1)S(1)}, u32[]{:S(2)}, u32[]{:S(2)}) %collective-permute-start.13) | collective-permute-done | bytes 2552 | tf_op jit(solution)/shard_map/ppermute | solution.py:234
  76.4 1.7 %collective-permute-start.15 = (bf16[3,8,3,10]{3,2,1,0:T(4,128)(2,1)S(1)}, bf16[3,8,3,10]{3,2,1,0:T(4,128)(2,1)S(1)}, u32[]{:S(2)}, u32[]{:S(2)}) collective-permute-start(bf16[3,8,3,10]{3,2,1,0:T(4,128)(2,1)S(1)} %get-tuple-element.80), channel_id=1, source_target_pairs={{4,0},{8,4},{12,8},{0,12},{5,1},{9,5},{13,9},{1,13},{6,2},{10,6},{... | collective-permute-start | bytes 4328 | tf_op jit(solution)/shard_map/ppermute | solution.py:234
  78.2 1.4 %collective-permute-done.14 = bf16[3,8,3,10]{3,2,1,0:T(4,128)(2,1)S(1)} collective-permute-done((bf16[3,8,3,10]{3,2,1,0:T(4,128)(2,1)S(1)}, bf16[3,8,3,10]{3,2,1,0:T(4,128)(2,1)S(1)}, u32[]{:S(2)}, u32[]{:S(2)}) %collective-permute-start.14) | collective-permute-done | bytes 1472 | tf_op jit(solution)/shard_map/ppermute | solution.py:234
  79.8 0.7 collective-permute-start.16
  80.4 3.2 %collective-permute-start.17 = (bf16[3,8,8,3]{3,2,1,0:T(8,128)(2,1)S(1)}, bf16[3,8,8,3]{3,2,1,0:T(8,128)(2,1)S(1)}, u32[]{:S(2)}, u32[]{:S(2)}) collective-permute-start(bf16[3,8,8,3]{3,2,1,0:T(8,128)(2,1)S(1)} %get-tuple-element.86), channel_id=1, source_target_pairs={{1,0},{2,1},{3,2},{0,3},{5,4},{6,5},{7,6},{4,7},{9,8},{10,9},{11,1... | collective-permute-start | bytes 3464 | tf_op jit(solution)/shard_map/ppermute | solution.py:234
  84.0 0.6 collective-permute-start.18
  84.7 1.5 %collective-permute-start.19 = (bf16[3,14,10,128]{3,0,2,1:T(4,128)(2,1)S(1)}, bf16[3,14,10,128]{3,0,2,1:T(4,128)(2,1)S(1)}, u32[]{:S(2)}, u32[]{:S(2)}) collective-permute-start(bf16[3,14,10,128]{3,0,2,1:T(4,128)(2,1)S(1)} %bitcast.143), channel_id=1, source_target_pairs={{16,0},{0,16},{17,1},{1,17},{18,2},{2,18},{19,3},{3,19},{20,4},{4,... | collective-permute-start | bytes 322568 | tf_op jit(solution)/shard_map/ppermute | solution.py:234
  86.2 0.6 copy.149
  87.1 3.2 %collective-permute-done.18 = bf16[3,14,10,128]{3,0,2,1:T(4,128)(2,1)S(1)} collective-permute-done((bf16[3,14,10,128]{3,0,2,1:T(4,128)(2,1)S(1)}, bf16[3,14,10,128]{3,0,2,1:T(4,128)(2,1)S(1)}, u32[]{:S(2)}, u32[]{:S(2)}) %collective-permute-start.18) | collective-permute-done | bytes 107552 | tf_op jit(solution)/shard_map/ppermute | solution.py:234
  90.4 3.1 %collective-permute-done.19 = bf16[3,14,10,128]{3,0,2,1:T(4,128)(2,1)S(1)} collective-permute-done((bf16[3,14,10,128]{3,0,2,1:T(4,128)(2,1)S(1)}, bf16[3,14,10,128]{3,0,2,1:T(4,128)(2,1)S(1)}, u32[]{:S(2)}, u32[]{:S(2)}) %collective-permute-start.19) | collective-permute-done | bytes 107552 | tf_op jit(solution)/shard_map/ppermute | solution.py:234
  93.8 1.6 %collective-permute-start.21 = (bf16[8,3,10,128]{3,0,2,1:T(8,128)(2,1)S(1)}, bf16[8,3,10,128]{3,0,2,1:T(8,128)(2,1)S(1)}, u32[]{:S(2)}, u32[]{:S(2)}) collective-permute-start(bf16[8,3,10,128]{3,0,2,1:T(8,128)(2,1)S(1)} %get-tuple-element.66), channel_id=1, source_target_pairs={{4,0},{8,4},{12,8},{0,12},{5,1},{9,5},{13,9},{1,13},{6,2},{10,6},{... | collective-permute-start | bytes 184328 | tf_op jit(solution)/shard_map/ppermute | solution.py:234
  95.7 1.6 %collective-permute-done.20 = bf16[8,3,10,128]{3,0,2,1:T(8,128)(2,1)S(1)} collective-permute-done((bf16[8,3,10,128]{3,0,2,1:T(8,128)(2,1)S(1)}, bf16[8,3,10,128]{3,0,2,1:T(8,128)(2,1)S(1)}, u32[]{:S(2)}, u32[]{:S(2)}) %collective-permute-start.20) | collective-permute-done | bytes 61472 | tf_op jit(solution)/shard_map/ppermute | solution.py:234
  97.5 3.8 %collective-permute-start.23 = (bf16[8,8,3,128]{3,0,2,1:T(8,128)(2,1)S(1)}, bf16[8,8,3,128]{3,0,2,1:T(8,128)(2,1)S(1)}, u32[]{:S(2)}, u32[]{:S(2)}) collective-permute-start(bf16[8,8,3,128]{3,0,2,1:T(8,128)(2,1)S(1)} %get-tuple-element.72), channel_id=1, source_target_pairs={{1,0},{2,1},{3,2},{0,3},{5,4},{6,5},{7,6},{4,7},{9,8},{10,9},{11,1... | collective-permute-start | bytes 147464 | tf_op jit(solution)/shard_map/ppermute | solution.py:234
  101.3 0.6 slice_bitcast_fusion.16
  101.9 0.6 copy.174
  102.5 1.3 %collective-permute-done.22 = bf16[8,8,3,128]{3,0,2,1:T(8,128)(2,1)S(1)} collective-permute-done((bf16[8,8,3,128]{3,0,2,1:T(8,128)(2,1)S(1)}, bf16[8,8,3,128]{3,0,2,1:T(8,128)(2,1)S(1)}, u32[]{:S(2)}, u32[]{:S(2)}) %collective-permute-start.22) | collective-permute-done | bytes 49184 | tf_op jit(solution)/shard_map/ppermute | solution.py:234
  103.9 0.9 convolution_bitcast_fusion
  (109 shorter events, 6.9 us)
Async XLA Ops:
  0.6 9.4 %copy-start = (bf16[2,2,1,64,128]{4,3,2,1,0:T(8,128)(2,1)S(1)}, bf16[2,2,1,64,128]{4,3,2,1,0:T(8,128)(2,1)}, u32[]{:S(2)}) copy-start(bf16[2,2,1,64,128]{4,3,2,1,0:T(8,128)(2,1)} %param.14) | copy-start | bytes 196612
  4.8 7.3 %collective-permute-start.6 = (f32[4,8,8,3]{2,1,3,0:T(8,128)S(1)}, f32[4,8,8,3]{2,1,3,0:T(8,128)S(1)}, u32[]{:S(2)}, u32[]{:S(2)}) collective-permute-start(f32[4,8,8,3]{2,1,3,0:T(8,128)S(1)} %get-tuple-element.81), channel_id=1, source_target_pairs={{0,1},{1,2},{2,3},{3,0},{4,5},{5,6},{6,7},{7,4},{8,9},{9,10},{10,1... | collective-permute-start | bytes 9224 | tf_op jit(solution)/shard_map/ppermute | solution.py:234
  7.9 4.6 %collective-permute-start.7 = (f32[4,8,8,3]{2,1,3,0:T(8,128)S(1)}, f32[4,8,8,3]{2,1,3,0:T(8,128)S(1)}, u32[]{:S(2)}, u32[]{:S(2)}) collective-permute-start(f32[4,8,8,3]{2,1,3,0:T(8,128)S(1)} %get-tuple-element.82), channel_id=1, source_target_pairs={{1,0},{2,1},{3,2},{0,3},{5,4},{6,5},{7,6},{4,7},{9,8},{10,9},{11,1... | collective-permute-start | bytes 9224 | tf_op jit(solution)/shard_map/ppermute | solution.py:234
  10.3 10.9 %copy-start.5 = (f32[5,2,4,2,4,1,4]{0,6,5,4,3,2,1:T(4,128)S(1)}, f32[5,2,4,2,4,1,4]{0,6,5,4,3,2,1:T(4,128)}, u32[]{:S(2)}) copy-start(f32[5,2,4,2,4,1,4]{0,6,5,4,3,2,1:T(4,128)} %constant.87) | copy-start | bytes 15364
  12.6 8.8 %copy-start.7 = (f32[128,16]{0,1:T(8,128)S(1)}, f32[128,16]{0,1:T(8,128)}, u32[]{:S(2)}) copy-start(f32[128,16]{0,1:T(8,128)} %param.18) | copy-start | bytes 24580
  12.6 8.9 %copy-start.6 = (f32[3,10,128]{2,0,1:T(4,128)S(1)}, f32[3,10,128]{2,0,1:T(4,128)}, u32[]{:S(2)}) copy-start(f32[3,10,128]{2,0,1:T(4,128)} %param.16) | copy-start | bytes 46084
  12.7 12.8 %copy-start.4 = (f32[4,14,14,10]{2,1,3,0:T(8,128)S(1)}, f32[4,14,14,10]{2,1,3,0:T(8,128)}, u32[]{:S(2)}) copy-start(f32[4,14,14,10]{2,1,3,0:T(8,128)} %constant.17.clone) | copy-start | bytes 94084
  12.7 6.3 %collective-permute-start.8 = (f32[4,8,3,10]{2,1,3,0:T(8,128)S(1)}, f32[4,8,3,10]{2,1,3,0:T(8,128)S(1)}, u32[]{:S(2)}, u32[]{:S(2)}) collective-permute-start(f32[4,8,3,10]{2,1,3,0:T(8,128)S(1)} %get-tuple-element.75), channel_id=1, source_target_pairs={{0,4},{4,8},{8,12},{12,0},{1,5},{5,9},{9,13},{13,1},{2,6},{6,10},{... | collective-permute-start | bytes 11528 | tf_op jit(solution)/shard_map/ppermute | solution.py:234
  12.8 6.2 %collective-permute-start.9 = (f32[4,8,3,10]{2,1,3,0:T(8,128)S(1)}, f32[4,8,3,10]{2,1,3,0:T(8,128)S(1)}, u32[]{:S(2)}, u32[]{:S(2)}) collective-permute-start(f32[4,8,3,10]{2,1,3,0:T(8,128)S(1)} %get-tuple-element.76), channel_id=1, source_target_pairs={{4,0},{8,4},{12,8},{0,12},{5,1},{9,5},{13,9},{1,13},{6,2},{10,6},{... | collective-permute-start | bytes 11528 | tf_op jit(solution)/shard_map/ppermute | solution.py:234
  15.1 17.9 %collective-permute-start = (bf16[8,8,3,128]{3,0,2,1:T(8,128)(2,1)}, bf16[8,8,3,128]{3,0,2,1:T(8,128)(2,1)S(1)}, u32[]{:S(2)}, u32[]{:S(2)}) collective-permute-start(bf16[8,8,3,128]{3,0,2,1:T(8,128)(2,1)} %get-tuple-element.83), channel_id=1, source_target_pairs={{0,1},{1,2},{2,3},{3,0},{4,5},{5,6},{6,7},{7,4},{8,9},{9,10},{10,1... | collective-permute-start | bytes 147464 | tf_op jit(solution)/shard_map/ppermute | solution.py:234
  16.2 16.9 %collective-permute-start.1 = (bf16[8,8,3,128]{3,0,2,1:T(8,128)(2,1)S(1)}, bf16[8,8,3,128]{3,0,2,1:T(8,128)(2,1)S(1)}, u32[]{:S(2)}, u32[]{:S(2)}) collective-permute-start(bf16[8,8,3,128]{3,0,2,1:T(8,128)(2,1)S(1)} %get-tuple-element.84), channel_id=1, source_target_pairs={{1,0},{2,1},{3,2},{0,3},{5,4},{6,5},{7,6},{4,7},{9,8},{10,9},{11,1... | collective-permute-start | bytes 147464 | tf_op jit(solution)/shard_map/ppermute | solution.py:234
  19.2 5.1 %collective-permute-start.10 = (f32[4,3,14,10]{2,1,3,0:T(4,128)S(1)}, f32[4,3,14,10]{2,1,3,0:T(4,128)S(1)}, u32[]{:S(2)}, u32[]{:S(2)}) collective-permute-start(f32[4,3,14,10]{2,1,3,0:T(4,128)S(1)} %get-tuple-element.73), channel_id=1, source_target_pairs={{0,16},{16,0},{1,17},{17,1},{2,18},{18,2},{3,19},{19,3},{4,20},{20... | collective-permute-start | bytes 20168 | tf_op jit(solution)/shard_map/ppermute | solution.py:234
  20.7 4.8 %collective-permute-start.11 = (f32[4,3,14,10]{2,1,3,0:T(4,128)S(1)}, f32[4,3,14,10]{2,1,3,0:T(4,128)S(1)}, u32[]{:S(2)}, u32[]{:S(2)}) collective-permute-start(f32[4,3,14,10]{2,1,3,0:T(4,128)S(1)} %get-tuple-element.74), channel_id=1, source_target_pairs={{16,0},{0,16},{17,1},{1,17},{18,2},{2,18},{19,3},{3,19},{20,4},{4,... | collective-permute-start | bytes 20168 | tf_op jit(solution)/shard_map/ppermute | solution.py:234
  33.1 3.7 %collective-permute-start.2 = (bf16[8,3,10,128]{3,0,2,1:T(8,128)(2,1)S(1)}, bf16[8,3,10,128]{3,0,2,1:T(8,128)(2,1)S(1)}, u32[]{:S(2)}, u32[]{:S(2)}) collective-permute-start(bf16[8,3,10,128]{3,0,2,1:T(8,128)(2,1)S(1)} %get-tuple-element.77), channel_id=1, source_target_pairs={{0,4},{4,8},{8,12},{12,0},{1,5},{5,9},{9,13},{13,1},{2,6},{6,10},{... | collective-permute-start | bytes 184328 | tf_op jit(solution)/shard_map/ppermute | solution.py:234
  33.1 3.6 %collective-permute-start.3 = (bf16[8,3,10,128]{3,0,2,1:T(8,128)(2,1)S(1)}, bf16[8,3,10,128]{3,0,2,1:T(8,128)(2,1)S(1)}, u32[]{:S(2)}, u32[]{:S(2)}) collective-permute-start(bf16[8,3,10,128]{3,0,2,1:T(8,128)(2,1)S(1)} %get-tuple-element.78), channel_id=1, source_target_pairs={{4,0},{8,4},{12,8},{0,12},{5,1},{9,5},{13,9},{1,13},{6,2},{10,6},{... | collective-permute-start | bytes 184328 | tf_op jit(solution)/shard_map/ppermute | solution.py:234
  36.9 6.2 %collective-permute-start.4 = (bf16[3,14,10,128]{3,0,2,1:T(4,128)(2,1)S(1)}, bf16[3,14,10,128]{3,0,2,1:T(4,128)(2,1)S(1)}, u32[]{:S(2)}, u32[]{:S(2)}) collective-permute-start(bf16[3,14,10,128]{3,0,2,1:T(4,128)(2,1)S(1)} %get-tuple-element.67), channel_id=1, source_target_pairs={{0,16},{16,0},{1,17},{17,1},{2,18},{18,2},{3,19},{19,3},{4,20},{20... | collective-permute-start | bytes 322568 | tf_op jit(solution)/shard_map/ppermute | solution.py:234
  38.5 7.7 %collective-permute-start.5 = (bf16[3,14,10,128]{3,0,2,1:T(4,128)(2,1)S(1)}, bf16[3,14,10,128]{3,0,2,1:T(4,128)(2,1)S(1)}, u32[]{:S(2)}, u32[]{:S(2)}) collective-permute-start(bf16[3,14,10,128]{3,0,2,1:T(4,128)(2,1)S(1)} %get-tuple-element.68), channel_id=1, source_target_pairs={{16,0},{0,16},{17,1},{1,17},{18,2},{2,18},{19,3},{3,19},{20,4},{4,... | collective-permute-start | bytes 322568 | tf_op jit(solution)/shard_map/ppermute | solution.py:234
  46.5 0.8 copy-start.1
  46.5 0.8 copy-start.2
  46.5 0.8 copy-start.3
  70.7 4.0 %collective-permute-start.12 = (bf16[3,3,14,10]{3,2,1,0:T(8,128)(2,1)S(1)}, bf16[3,3,14,10]{3,2,1,0:T(8,128)(2,1)S(1)}, u32[]{:S(2)}, u32[]{:S(2)}) collective-permute-start(bf16[3,3,14,10]{3,2,1,0:T(8,128)(2,1)S(1)} %get-tuple-element.69), channel_id=1, source_target_pairs={{0,16},{16,0},{1,17},{17,1},{2,18},{18,2},{3,19},{19,3},{4,20},{20... | collective-permute-start | bytes 7568 | tf_op jit(solution)/shard_map/ppermute | solution.py:234
  72.3 4.0 %collective-permute-start.13 = (bf16[3,3,14,10]{3,2,1,0:T(8,128)(2,1)S(1)}, bf16[3,3,14,10]{3,2,1,0:T(8,128)(2,1)S(1)}, u32[]{:S(2)}, u32[]{:S(2)}) collective-permute-start(bf16[3,3,14,10]{3,2,1,0:T(8,128)(2,1)S(1)} %get-tuple-element.70), channel_id=1, source_target_pairs={{16,0},{0,16},{17,1},{1,17},{18,2},{2,18},{19,3},{3,19},{20,4},{4,... | collective-permute-start | bytes 7568 | tf_op jit(solution)/shard_map/ppermute | solution.py:234
  76.3 3.3 %collective-permute-start.14 = (bf16[3,8,3,10]{3,2,1,0:T(4,128)(2,1)S(1)}, bf16[3,8,3,10]{3,2,1,0:T(4,128)(2,1)S(1)}, u32[]{:S(2)}, u32[]{:S(2)}) collective-permute-start(bf16[3,8,3,10]{3,2,1,0:T(4,128)(2,1)S(1)} %get-tuple-element.79), channel_id=1, source_target_pairs={{0,4},{4,8},{8,12},{12,0},{1,5},{5,9},{9,13},{13,1},{2,6},{6,10},{... | collective-permute-start | bytes 4328 | tf_op jit(solution)/shard_map/ppermute | solution.py:234
  76.4 3.3 %collective-permute-start.15 = (bf16[3,8,3,10]{3,2,1,0:T(4,128)(2,1)S(1)}, bf16[3,8,3,10]{3,2,1,0:T(4,128)(2,1)S(1)}, u32[]{:S(2)}, u32[]{:S(2)}) collective-permute-start(bf16[3,8,3,10]{3,2,1,0:T(4,128)(2,1)S(1)} %get-tuple-element.80), channel_id=1, source_target_pairs={{4,0},{8,4},{12,8},{0,12},{5,1},{9,5},{13,9},{1,13},{6,2},{10,6},{... | collective-permute-start | bytes 4328 | tf_op jit(solution)/shard_map/ppermute | solution.py:234
  79.8 7.0 %collective-permute-start.16 = (bf16[3,8,8,3]{3,2,1,0:T(8,128)(2,1)S(1)}, bf16[3,8,8,3]{3,2,1,0:T(8,128)(2,1)S(1)}, u32[]{:S(2)}, u32[]{:S(2)}) collective-permute-start(bf16[3,8,8,3]{3,2,1,0:T(8,128)(2,1)S(1)} %get-tuple-element.85), channel_id=1, source_target_pairs={{0,1},{1,2},{2,3},{3,0},{4,5},{5,6},{6,7},{7,4},{8,9},{9,10},{10,1... | collective-permute-start | bytes 3464 | tf_op jit(solution)/shard_map/ppermute | solution.py:234
  80.4 6.4 %collective-permute-start.17 = (bf16[3,8,8,3]{3,2,1,0:T(8,128)(2,1)S(1)}, bf16[3,8,8,3]{3,2,1,0:T(8,128)(2,1)S(1)}, u32[]{:S(2)}, u32[]{:S(2)}) collective-permute-start(bf16[3,8,8,3]{3,2,1,0:T(8,128)(2,1)S(1)} %get-tuple-element.86), channel_id=1, source_target_pairs={{1,0},{2,1},{3,2},{0,3},{5,4},{6,5},{7,6},{4,7},{9,8},{10,9},{11,1... | collective-permute-start | bytes 3464 | tf_op jit(solution)/shard_map/ppermute | solution.py:234
  84.0 6.4 %collective-permute-start.18 = (bf16[3,14,10,128]{3,0,2,1:T(4,128)(2,1)S(1)}, bf16[3,14,10,128]{3,0,2,1:T(4,128)(2,1)S(1)}, u32[]{:S(2)}, u32[]{:S(2)}) collective-permute-start(bf16[3,14,10,128]{3,0,2,1:T(4,128)(2,1)S(1)} %bitcast.142), channel_id=1, source_target_pairs={{0,16},{16,0},{1,17},{17,1},{2,18},{18,2},{3,19},{19,3},{4,20},{20... | collective-permute-start | bytes 322568 | tf_op jit(solution)/shard_map/ppermute | solution.py:234
  84.7 8.8 %collective-permute-start.19 = (bf16[3,14,10,128]{3,0,2,1:T(4,128)(2,1)S(1)}, bf16[3,14,10,128]{3,0,2,1:T(4,128)(2,1)S(1)}, u32[]{:S(2)}, u32[]{:S(2)}) collective-permute-start(bf16[3,14,10,128]{3,0,2,1:T(4,128)(2,1)S(1)} %bitcast.143), channel_id=1, source_target_pairs={{16,0},{0,16},{17,1},{1,17},{18,2},{2,18},{19,3},{3,19},{20,4},{4,... | collective-permute-start | bytes 322568 | tf_op jit(solution)/shard_map/ppermute | solution.py:234
  93.6 3.7 %collective-permute-start.20 = (bf16[8,3,10,128]{3,0,2,1:T(8,128)(2,1)S(1)}, bf16[8,3,10,128]{3,0,2,1:T(8,128)(2,1)S(1)}, u32[]{:S(2)}, u32[]{:S(2)}) collective-permute-start(bf16[8,3,10,128]{3,0,2,1:T(8,128)(2,1)S(1)} %get-tuple-element.65), channel_id=1, source_target_pairs={{0,4},{4,8},{8,12},{12,0},{1,5},{5,9},{9,13},{13,1},{2,6},{6,10},{... | collective-permute-start | bytes 184328 | tf_op jit(solution)/shard_map/ppermute | solution.py:234
  93.8 3.5 %collective-permute-start.21 = (bf16[8,3,10,128]{3,0,2,1:T(8,128)(2,1)S(1)}, bf16[8,3,10,128]{3,0,2,1:T(8,128)(2,1)S(1)}, u32[]{:S(2)}, u32[]{:S(2)}) collective-permute-start(bf16[8,3,10,128]{3,0,2,1:T(8,128)(2,1)S(1)} %get-tuple-element.66), channel_id=1, source_target_pairs={{4,0},{8,4},{12,8},{0,12},{5,1},{9,5},{13,9},{1,13},{6,2},{10,6},{... | collective-permute-start | bytes 184328 | tf_op jit(solution)/shard_map/ppermute | solution.py:234
  97.4 6.4 %collective-permute-start.22 = (bf16[8,8,3,128]{3,0,2,1:T(8,128)(2,1)S(1)}, bf16[8,8,3,128]{3,0,2,1:T(8,128)(2,1)S(1)}, u32[]{:S(2)}, u32[]{:S(2)}) collective-permute-start(bf16[8,8,3,128]{3,0,2,1:T(8,128)(2,1)S(1)} %get-tuple-element.71), channel_id=1, source_target_pairs={{0,1},{1,2},{2,3},{3,0},{4,5},{5,6},{6,7},{7,4},{8,9},{9,10},{10,1... | collective-permute-start | bytes 147464 | tf_op jit(solution)/shard_map/ppermute | solution.py:234
  97.5 6.3 %collective-permute-start.23 = (bf16[8,8,3,128]{3,0,2,1:T(8,128)(2,1)S(1)}, bf16[8,8,3,128]{3,0,2,1:T(8,128)(2,1)S(1)}, u32[]{:S(2)}, u32[]{:S(2)}) collective-permute-start(bf16[8,8,3,128]{3,0,2,1:T(8,128)(2,1)S(1)} %get-tuple-element.72), channel_id=1, source_target_pairs={{1,0},{2,1},{3,2},{0,3},{5,4},{6,5},{7,6},{4,7},{9,8},{10,9},{11,1... | collective-permute-start | bytes 147464 | tf_op jit(solution)/shard_map/ppermute | solution.py:234

commit v2 on v1

--- a/solution.py
+++ b/solution.py
@@ -56,8 +56,10 @@
 
 def compute_kernel(
     dims,
-    feat_ref,
-    posj_ref,
+    layer_ref,
+    posw_ref,
+    pick_ref,
+    pick_t_ref,
     rpos_ref,
     radial_ref,
     coupling_ref,
@@ -65,8 +67,10 @@
     hw_ref,
     ow_ref,
     fgrad_ref,
+    wsum_ref,
+    node_ref,
+    posj_ref,
     fj_ref,
-    node_ref,
     slab_ref,
     edge_ref,
     field_ref,
@@ -87,14 +91,24 @@
     root3 = math.sqrt(3.0)
 
     def build(x, carry):
-        full = feat_ref[x].astype(jnp.float32)
+        full = jnp.dot(pick_ref[...], layer_ref[x], preferred_element_type=jnp.float32)
+        full = full.astype(jnp.bfloat16)
         for by in range(nby):
-            start = by * BLOCK * depth
-            slab_ref[by, x] = full[start : start + rows].astype(jnp.bfloat16)
+            slab_ref[by, x] = full[by * rows : (by + 1) * rows]
             acc_ref[by, x] = jnp.zeros((rows, full.shape[1]), jnp.float32)
         return carry
 
     lax.fori_loop(0, px, build, 0)
+    wsum_ref[...] = jnp.zeros(wsum_ref.shape, jnp.float32)
+    fj_ref[...] = jnp.zeros(fj_ref.shape, jnp.float32)
+
+    def place_columns(by, carry):
+        for bx in range(nbx):
+            for k in range(wide):
+                posj_ref[by * nbx + bx, :, k * rows : (k + 1) * rows] = posw_ref[by, bx * BLOCK + k]
+        return carry
+
+    lax.fori_loop(0, nby, place_columns, 0)
 
     def forward(blk, carry):
         by, bx = blk // nbx, lax.rem(blk, nbx)
@@ -203,8 +217,10 @@
                 along * n + across * s_sum[m + 1] for m, n in enumerate((nx, ny, nz))
             ]
             for m in range(3):
-                fj_ref[blk, m : m + 1, c : c + w] = -jnp.sum(outs[m], axis=0, keepdims=True)
+                fj_ref[m : m + 1, c : c + w] = -jnp.sum(outs[m], axis=0, keepdims=True)
                 total[m] = total[m] + jnp.sum(outs[m], axis=1, keepdims=True)
+        for k in range(wide):
+            wsum_ref[by, bx * BLOCK + k] += fj_ref[:, k * rows : (k + 1) * rows]
         lane = lax.broadcasted_iota(jnp.int32, (own, node_ref.shape[1]), 1)
         here = pl.ds(blk * own, own)
         node_ref[here] = jnp.where(
@@ -217,43 +233,321 @@
     lax.fori_loop(0, nbx * nby, backward, 0)
 
     def merge(x, carry):
-        fgrad_ref[x] = jnp.zeros(fgrad_ref.shape[1:], jnp.float32)
-        for by in range(nby):
-            start = by * BLOCK * depth
-            fgrad_ref[x, start : start + rows] += acc_ref[by, x]
+        stack = jnp.concatenate([acc_ref[by, x] for by in range(nby)], axis=0)
+        top = stack.astype(jnp.bfloat16)
+        rest = (stack - top.astype(jnp.float32)).astype(jnp.bfloat16)
+        fgrad_ref[x] = jnp.dot(
+            pick_t_ref[...], top, preferred_element_type=jnp.float32
+        ) + jnp.dot(pick_t_ref[...], rest, preferred_element_type=jnp.float32)
         return carry
 
     lax.fori_loop(0, px, merge, 0)
 
 
-def shift(block, axis, up):
+def ring(axis):
     count = lax.axis_size(axis)
-    pairs = [(i, (i + 1) % count) for i in range(count)]
-    if not up:
-        pairs = [(b, a) for a, b in pairs]
-    return lax.ppermute(block, axis, pairs)
-
-
-def widen(block, axis, dim, reach):
-    extent = block.shape[dim]
-    low = shift(lax.slice_in_dim(block, extent - reach, extent, axis=dim), axis, True)
-    high = shift(lax.slice_in_dim(block, 0, reach, axis=dim), axis, False)
-    return jnp.concatenate([low, block, high], axis=dim)
-
-
-def fold_back(block, axis, dim, reach):
-    extent = block.shape[dim]
-    low = lax.slice_in_dim(block, 0, reach, axis=dim).astype(jnp.bfloat16)
-    high = lax.slice_in_dim(block, extent - reach, extent, axis=dim).astype(jnp.bfloat16)
-    to_high = shift(low, axis, False).astype(block.dtype)
-    to_low = shift(high, axis, True).astype(block.dtype)
-    core = lax.slice_in_dim(block, reach, extent - reach, axis=dim)
-    rest = extent - 3 * reach
-    low_pad = [(0, 0)] * block.ndim
-    high_pad = [(0, 0)] * block.ndim
-    low_pad[dim] = (0, rest)
-    high_pad[dim] = (rest, 0)
-    return core + jnp.pad(to_low, low_pad) + jnp.pad(to_high, high_pad)
+    me = lax.axis_index(axis)
+    return lax.rem(me + count - 1, count), lax.rem(me + 1, count)
+
+
+def greet(around):
+    barrier = pltpu.get_barrier_semaphore()
+    for axis, sides in around.items():
+        for side in sides:
+            pl.semaphore_signal(
+                barrier, inc=1, device_id={axis: side}, device_id_type=pl.DeviceIdType.MESH
+            )
+    return barrier
+
+
+def sender(send_sem, recv_sem):
+    def send(slot, source, target, axis, side):
+        copy = pltpu.make_async_remote_copy(
+            src_ref=source,
+            dst_ref=target,
+            send_sem=send_sem.at[slot],
+            recv_sem=recv_sem.at[slot],
+            device_id={axis: side},
+            device_id_type=pl.DeviceIdType.MESH,
+        )
+        copy.start()
+        return copy
+
+    return send
+
+
+def spread_kernel(
+    dims,
+    place_ref,
+    feat_ref,
+    small_ref,
+    zsel_ref,
+    ysel_ref,
+    layer_ref,
+    tile_ref,
+    zs_ref,
+    ys_ref,
+    send_sem,
+    recv_sem,
+):
+    sx, lat, reach, o, zp, yp = dims
+    around = {axis: ring(axis) for axis in ("gz", "gy", "gx")}
+    barrier = greet(around)
+    send = sender(send_sem, recv_sem)
+    tile_ref[0, 0, 0] = small_ref[...]
+    for col in range(sx // lat):
+        sites = jnp.dot(place_ref[col], feat_ref[col], preferred_element_type=jnp.float32)
+        sites = sites.astype(jnp.bfloat16)
+        for k in range(lat):
+            x = col * lat + k
+            own = sites[k * o : (k + 1) * o]
+            layer_ref[reach + x, 0:o] = own
+            faces = jnp.dot(zsel_ref[...], own, preferred_element_type=jnp.float32)
+            faces = faces.astype(jnp.bfloat16)
+            zs_ref[0, x] = faces[:zp]
+            zs_ref[1, x] = faces[zp:]
+    pl.semaphore_wait(barrier, 6)
+
+    z0, y0 = o, o + 2 * zp
+    inner = pl.ds(reach, sx)
+    low, high = pl.ds(reach, reach), pl.ds(sx, reach)
+    halo_low, halo_high = pl.ds(0, reach), pl.ds(reach + sx, reach)
+
+    def send_x(slot, lanes, tiles):
+        left, right = around["gx"]
+        return [
+            send(slot, layer_ref.at[low, lanes], layer_ref.at[halo_high, lanes], "gx", left),
+            send(slot + 1, layer_ref.at[high, lanes], layer_ref.at[halo_low, lanes], "gx", right),
+            send(slot + 2, tile_ref.at[(0,) + tiles], tile_ref.at[(2,) + tiles], "gx", left),
+            send(slot + 3, tile_ref.at[(0,) + tiles], tile_ref.at[(1,) + tiles], "gx", right),
+        ]
+
+    left, right = around["gz"]
+    z_copies = [
+        send(0, zs_ref.at[0], layer_ref.at[inner, pl.ds(z0 + zp, zp)], "gz", left),
+        send(1, zs_ref.at[1], layer_ref.at[inner, pl.ds(z0, zp)], "gz", right),
+        send(2, tile_ref.at[0, 0, 0], tile_ref.at[0, 0, 2], "gz", left),
+        send(3, tile_ref.at[0, 0, 0], tile_ref.at[0, 0, 1], "gz", right),
+    ]
+    x_copies = send_x(8, pl.ds(0, o), (0, 0))
+    for copy in z_copies:
+        copy.wait_recv()
+
+    def faces_y(x, carry):
+        faces = jnp.dot(ysel_ref[...], layer_ref[reach + x, 0:y0], preferred_element_type=jnp.float32)
+        faces = faces.astype(jnp.bfloat16)
+        ys_ref[0, x] = faces[:yp]
+        ys_ref[1, x] = faces[yp:]
+        return carry
+
+    lax.fori_loop(0, sx, faces_y, 0)
+    left, right = around["gy"]
+    y_copies = [
+        send(4, ys_ref.at[0], layer_ref.at[inner, pl.ds(y0 + yp, yp)], "gy", left),
+        send(5, ys_ref.at[1], layer_ref.at[inner, pl.ds(y0, yp)], "gy", right),
+        send(6, tile_ref.at[0, 0], tile_ref.at[0, 2], "gy", left),
+        send(7, tile_ref.at[0, 0], tile_ref.at[0, 1], "gy", right),
+    ]
+    x_copies += send_x(12, pl.ds(z0, 2 * zp), (0, pl.ds(1, 2)))
+    for copy in y_copies:
+        copy.wait_recv()
+    x_copies += send_x(16, pl.ds(y0, 2 * yp), (pl.ds(1, 2),))
+    for copy in x_copies:
+        copy.wait_recv()
+    for copy in z_copies + y_copies + x_copies:
+        copy.wait_send()
+
+
+def gather_kernel(
+    dims,
+    place_ref,
+    place_t_ref,
+    grad_ref,
+    force_ref,
+    node_ref,
+    zsel_ref,
+    ysel_ref,
+    out_ref,
+    small_ref,
+    sum_ref,
+    fsum_ref,
+    gs_ref,
+    gr_ref,
+    ys_ref,
+    yr_ref,
+    zs_ref,
+    zr_ref,
+    fr_ref,
+    fyr_ref,
+    fzr_ref,
+    send_sem,
+    recv_sem,
+):
+    sx, lat, reach, o, zp, yp = dims
+    around = {axis: ring(axis) for axis in ("gz", "gy", "gx")}
+    barrier = greet(around)
+    send = sender(send_sem, recv_sem)
+    z0, y0 = o, o + 2 * zp
+    gs_ref[0] = grad_ref[0:reach].astype(jnp.bfloat16)
+    gs_ref[1] = grad_ref[reach + sx : sx + 2 * reach].astype(jnp.bfloat16)
+    sum_ref[...] = grad_ref[reach : reach + sx]
+    pl.semaphore_wait(barrier, 6)
+
+    left, right = around["gx"]
+    pieces = [pl.ds(y0, 2 * yp), pl.ds(z0, 2 * zp), pl.ds(0, o)]
+    x_copies = []
+    for n, lanes in enumerate(pieces):
+        for side, target in ((0, left), (1, right)):
+            x_copies.append(
+                send(
+                    2 * n + side,
+                    gs_ref.at[side, :, lanes],
+                    gr_ref.at[side, :, lanes],
+                    "gx",
+                    target,
+                )
+            )
+        if n == 0:
+            f_copies = [
+                send(6, force_ref.at[1], fr_ref.at[0], "gx", left),
+                send(7, force_ref.at[2], fr_ref.at[1], "gx", right),
+            ]
+
+    def add_x(n, start, size):
+        x_copies[2 * n].wait_recv()
+        x_copies[2 * n + 1].wait_recv()
+        rows = slice(start, start + size)
+        sum_ref[sx - reach : sx, rows] += gr_ref[0, :, rows].astype(jnp.float32)
+        sum_ref[0:reach, rows] += gr_ref[1, :, rows].astype(jnp.float32)
+
+    add_x(0, y0, 2 * yp)
+    ys_ref[0] = sum_ref[:, y0 : y0 + yp].astype(jnp.bfloat16)
+    ys_ref[1] = sum_ref[:, y0 + yp : y0 + 2 * yp].astype(jnp.bfloat16)
+    left, right = around["gy"]
+    y_copies = [
+        send(8, ys_ref.at[0], yr_ref.at[0], "gy", left),
+        send(9, ys_ref.at[1], yr_ref.at[1], "gy", right),
+    ]
+    for copy in f_copies:
+        copy.wait_recv()
+    fsum_ref[...] = force_ref[0] + fr_ref[0] + fr_ref[1]
+    fy_copies = [
+        send(10, fsum_ref.at[1], fyr_ref.at[0], "gy", left),
+        send(11, fsum_ref.at[2], fyr_ref.at[1], "gy", right),
+    ]
+    add_x(1, z0, 2 * zp)
+    for copy in y_copies:
+        copy.wait_recv()
+
+    def add_y(x, carry):
+        both = jnp.concatenate([yr_ref[1, x], yr_ref[0, x]], axis=0)
+        sum_ref[x, 0:y0] += lax.dot_general(
+            ysel_ref[...], both, (((0,), (0,)), ((), ())), preferred_element_type=jnp.float32
+        )
+        return carry
+
+    lax.fori_loop(0, sx, add_y, 0)
+    zs_ref[0] = sum_ref[:, z0 : z0 + zp].astype(jnp.bfloat16)
+    zs_ref[1] = sum_ref[:, z0 + zp : z0 + 2 * zp].astype(jnp.bfloat16)
+    zleft, zright = around["gz"]
+    z_copies = [
+        send(12, zs_ref.at[0], zr_ref.at[0], "gz", zleft),
+        send(13, zs_ref.at[1], zr_ref.at[1], "gz", zright),
+    ]
+    for copy in fy_copies:
+        copy.wait_recv()
+    fsum_ref[0] += fyr_ref[0] + fyr_ref[1]
+    fz_copies = [
+        send(14, fsum_ref.at[0, 1], fzr_ref.at[0], "gz", zleft),
+        send(15, fsum_ref.at[0, 2], fzr_ref.at[1], "gz", zright),
+    ]
+    add_x(2, 0, o)
+    for copy in z_copies:
+        copy.wait_recv()
+    for copy in fz_copies:
+        copy.wait_recv()
+    tile = node_ref[...] + fsum_ref[0, 0] + fzr_ref[0] + fzr_ref[1]
+    part = tile.shape[0] // (sx // lat)
+    for col in range(sx // lat):
+        sites = []
+        for k in range(lat):
+            x = col * lat + k
+            both = jnp.concatenate([zr_ref[1, x], zr_ref[0, x]], axis=0)
+            sites.append(
+                sum_ref[x, 0:o]
+                + lax.dot_general(
+                    zsel_ref[...], both, (((0,), (0,)), ((), ())), preferred_element_type=jnp.float32
+                )
+            )
+        whole = jnp.concatenate(sites, axis=0)
+        top = whole.astype(jnp.bfloat16)
+        rest = (whole - top.astype(jnp.float32)).astype(jnp.bfloat16)
+        out_ref[col] = jnp.dot(
+            place_t_ref[col], top, preferred_element_type=jnp.float32
+        ) + jnp.dot(place_t_ref[col], rest, preferred_element_type=jnp.float32)
+        small_ref[col] = jnp.dot(
+            tile[col * part : (col + 1) * part],
+            place_ref[col].astype(jnp.float32),
+            precision=HIGH,
+            preferred_element_type=jnp.float32,
+        )
+    for copy in x_copies + f_copies + y_copies + fy_copies + z_copies + fz_copies:
+        copy.wait_send()
+
+
+def tables(sx, sy, sz, reach):
+    py, depth = sy + 2 * reach, sz + 2 * reach
+    wide, nby = BLOCK + 2 * reach, sy // BLOCK
+    up = lambda n: -(-n // 16) * 16
+    o, zp, yp = sy * sz, up(sy * reach), up(reach * depth)
+    z0, y0 = o, o + 2 * zp
+    total = y0 + 2 * yp
+
+    def row(y, z):
+        if y < reach:
+            return y0 + y * depth + z
+        if y >= reach + sy:
+            return y0 + yp + (y - reach - sy) * depth + z
+        y -= reach
+        if z < reach:
+            return z0 + y * reach + z
+        if z >= reach + sz:
+            return z0 + zp + y * reach + z - reach - sz
+        return y * sz + z - reach
+
+    def spot(n, size):
+        if n < reach:
+            return 1, size - reach + n
+        if n >= reach + size:
+            return 2, n - reach - size
+        return 0, n - reach
+
+    pick = np.zeros((nby, wide, depth, total), np.float32)
+    pick_pos = np.zeros((9 * o, nby, wide, depth), np.float32)
+    for by in range(nby):
+        for y in range(wide):
+            for z in range(depth):
+                pick[by, y, z, row(by * BLOCK + y, z)] = 1
+                tile_y, at_y = spot(by * BLOCK + y, sy)
+                tile_z, at_z = spot(z, sz)
+                pick_pos[(tile_y * 3 + tile_z) * o + at_y * sz + at_z, by, y, z] = 1
+    zsel = np.zeros((2, zp, o), np.float32)
+    for y in range(sy):
+        for k in range(reach):
+            zsel[0, y * reach + k, y * sz + k] = 1
+            zsel[1, y * reach + k, y * sz + sz - reach + k] = 1
+    ysel = np.zeros((2, yp, y0), np.float32)
+    for k in range(reach):
+        for z in range(depth):
+            ysel[0, k * depth + z, row(reach + k, z)] = 1
+            ysel[1, k * depth + z, row(sy + k, z)] = 1
+    return (
+        (o, zp, yp, total),
+        pick.reshape(-1, total),
+        pick_pos.reshape(9 * o, -1),
+        zsel.reshape(2 * zp, o),
+        ysel.reshape(2 * yp, y0),
+    )
 
 
 def body(
@@ -276,17 +570,20 @@
     wide, depth = BLOCK + 2 * reach, sz + 2 * reach
     near, own = wide * wide * depth, BLOCK * BLOCK * sz
     px, py = sx + 2 * reach, sy + 2 * reach
-    rows_full = -(-py * depth // 16) * 16
+    rows = wide * depth
+    blocks = nbx * nby
+    (o, zp, yp, total), pick, pick_pos, zsel, ysel = tables(sx, sy, sz, reach)
+    column = cy * cz * capacity
 
     occupied = (jnp.arange(capacity, dtype=jnp.int32) < counts[..., None]).astype(jnp.float32)
     site = jnp.clip(jnp.floor(local_pos * (1.0 / spacing)).astype(jnp.int32), 0, lat - 1)
-    code = (site[:, :, :, 0] * lat + site[:, :, :, 1]) * lat + site[:, :, :, 2]
-    place = code[:, :, :, None, :] == jnp.arange(capacity, dtype=jnp.int32)[:, None]
-    place_half = place.astype(jnp.bfloat16)
-    place_full = place.astype(jnp.float32)
-    feat_sites = jnp.einsum(
-        "xyzts,xyzsc->xyztc", place_half, features, preferred_element_type=jnp.float32
-    ).astype(jnp.bfloat16)
+    cell_y = np.arange(cy, dtype=np.int32)[None, :, None, None] * lat
+    cell_z = np.arange(cz, dtype=np.int32)[None, None, :, None] * lat
+    code = (site[:, :, :, 0] * sy + site[:, :, :, 1] + cell_y) * sz + site[:, :, :, 2] + cell_z
+    code = code.reshape(cx, column)
+    count = np.arange(column, dtype=np.int32)
+    place = (code[:, None, :] == count[None, :, None]).astype(jnp.bfloat16)
+    place_t = (code[:, :, None] == count[None, None, :]).astype(jnp.bfloat16)
     small = jnp.concatenate(
         [
             local_pos,
@@ -295,21 +592,40 @@
         ],
         axis=3,
     )
-    small_sites = jnp.einsum("xyzks,xyzts->kxyzt", small, place_full, precision=HIGH)
-
-    feat_grid = feat_sites.reshape(cx, cy, cz, lat, lat, lat, channels)
-    feat_grid = feat_grid.transpose(0, 3, 1, 4, 2, 5, 6).reshape(sx, sy, sz, channels)
-    small_grid = small_sites.reshape(5, cx, cy, cz, lat, lat, lat)
-    small_grid = small_grid.transpose(0, 1, 4, 2, 5, 3, 6).reshape(5, sx, sy, sz)
-
-    feat_pad = widen(feat_grid, "gz", 2, reach)
-    feat_pad = widen(feat_pad, "gy", 1, reach)
-    feat_pad = widen(feat_pad, "gx", 0, reach)
-    feat_pad = feat_pad.reshape(px, py * depth, channels)
-    feat_pad = jnp.pad(feat_pad, ((0, 0), (0, rows_full - py * depth), (0, 0)))
-    pos_pad = small_grid[:4]
-    for axis, dim in (("gz", 3), ("gy", 2), ("gx", 1)):
-        pos_pad = widen(pos_pad, axis, dim, reach)
+    small = small.transpose(0, 3, 1, 2, 4).reshape(cx, 5, column)
+    small_sites = jnp.einsum("xks,xst->xkt", small, place_t.astype(jnp.float32), precision=HIGH)
+
+    vmem = pl.BlockSpec(memory_space=pltpu.VMEM)
+    dims = (sx, lat, reach, o, zp, yp)
+    limit = 50 * 1024 * 1024
+    zsel_half = jnp.asarray(zsel, jnp.bfloat16)
+    ysel_half = jnp.asarray(ysel, jnp.bfloat16)
+    layers, tiles = pl.pallas_call(
+        functools.partial(spread_kernel, dims),
+        out_shape=(
+            jax.ShapeDtypeStruct((px, total, channels), jnp.bfloat16),
+            jax.ShapeDtypeStruct((3, 3, 3, cx * 4, lat * o), jnp.float32),
+        ),
+        in_specs=[vmem] * 5,
+        out_specs=(vmem, vmem),
+        scratch_shapes=[
+            pltpu.VMEM((2, sx, zp, channels), jnp.bfloat16),
+            pltpu.VMEM((2, sx, yp, channels), jnp.bfloat16),
+            pltpu.SemaphoreType.DMA((20,)),
+            pltpu.SemaphoreType.DMA((20,)),
+        ],
+        compiler_params=pltpu.CompilerParams(
+            collective_id=0, has_side_effects=True, vmem_limit_bytes=limit
+        ),
+        name="halo_out",
+    )(
+        place,
+        features.reshape(cx, column, channels),
+        small_sites[:, :4].reshape(cx * 4, lat * o),
+        zsel_half,
+        ysel_half,
+    )
+
     steps = [
         np.floor((np.arange(n) - reach) / lat).astype(np.float32) * SIDE
         for n in (px, py, depth)
@@ -318,36 +634,40 @@
     shifts[0] = steps[0][:, None, None]
     shifts[1] = steps[1][None, :, None]
     shifts[2] = steps[2][None, None, :]
-    pos_pad = pos_pad + shifts
-    posj = jnp.stack(
+    slab_shifts = np.stack(
+        [shifts[:, :, by * BLOCK : by * BLOCK + wide].reshape(4, px, rows) for by in range(nby)]
+    ).transpose(0, 2, 1, 3)
+    order = (1, 0, 2)
+    posw = jnp.stack([tiles[n] for n in order]).reshape(3, 9, cx, 4, lat, o)
+    posw = posw.transpose(0, 2, 4, 3, 1, 5).reshape(3 * sx, 4, 9 * o)[sx - reach : 2 * sx + reach]
+    posw = jnp.dot(posw.reshape(px * 4, 9 * o), jnp.asarray(pick_pos), precision=HIGH)
+    posw = posw.reshape(px, 4, nby, rows).transpose(2, 0, 1, 3) + slab_shifts
+    own_shift = np.concatenate(
         [
-            pos_pad[:, bx * BLOCK : bx * BLOCK + wide, by * BLOCK : by * BLOCK + wide].reshape(4, near)
-            for by in range(nby)
-            for bx in range(nbx)
+            shifts[:, reach : reach + sx, reach : reach + sy, reach : reach + sz],
+            np.zeros((1, sx, sy, sz), np.float32),
         ]
     )
-    own_shift = np.concatenate(
-        [shifts[:, reach : reach + sx, reach : reach + sy, reach : reach + sz], np.zeros((1, sx, sy, sz), np.float32)]
-    )
+    small_grid = small_sites.reshape(cx, 5, lat, sy, sz).transpose(1, 0, 2, 3, 4).reshape(5, sx, sy, sz)
     rpos = (small_grid + own_shift).reshape(5, nbx, BLOCK, nby, BLOCK, sz)
-    rpos = rpos.transpose(3, 1, 2, 4, 5, 0).reshape(nby * nbx, own, 5)
+    rpos = rpos.transpose(3, 1, 2, 4, 5, 0).reshape(blocks, own, 5)
     rpos = jnp.pad(rpos, ((0, 0), (0, 0), (0, 3)))
 
     spec_pad = -(-coupling.shape[1] // 8) * 8 - coupling.shape[1]
     total_own = sx * sy * sz
-    rows = wide * depth
-    blocks = nbx * nby
-    vmem = pl.BlockSpec(memory_space=pltpu.VMEM)
-    fgrad, fj, node = pl.pallas_call(
+    pick_half = jnp.asarray(pick, jnp.bfloat16)
+    fgrad, wsum, node = pl.pallas_call(
         functools.partial(compute_kernel, (sx, sy, sz, reach, nb)),
         out_shape=(
-            jax.ShapeDtypeStruct((px, rows_full, channels), jnp.float32),
-            jax.ShapeDtypeStruct((blocks, 3, near), jnp.float32),
+            jax.ShapeDtypeStruct((px, total, channels), jnp.float32),
+            jax.ShapeDtypeStruct((nby, px, 4, rows), jnp.float32),
             jax.ShapeDtypeStruct((total_own, 128), jnp.float32),
         ),
-        in_specs=[vmem] * 8,
+        in_specs=[vmem] * 10,
         out_specs=(vmem, vmem, vmem),
         scratch_shapes=[
+            pltpu.VMEM((blocks, 4, near), jnp.float32),
+            pltpu.VMEM((4, near), jnp.float32),
             pltpu.VMEM((nby, px, rows, channels), jnp.bfloat16),
             pltpu.VMEM((blocks, nb * 4 * own, near), jnp.bfloat16),
             pltpu.VMEM((blocks, 8, own, near), jnp.float32),
@@ -356,11 +676,13 @@
             pltpu.VMEM((nby, px, rows, channels), jnp.float32),
             pltpu.VMEM((nb * 4 * own, near), jnp.float32),
         ],
-        compiler_params=pltpu.CompilerParams(vmem_limit_bytes=50 * 1024 * 1024),
+        compiler_params=pltpu.CompilerParams(vmem_limit_bytes=limit),
         name="pair_layer",
     )(
-        feat_pad,
-        posj,
+        layers,
+        posw,
+        pick_half,
+        jnp.asarray(pick.T, jnp.bfloat16),
         rpos,
         radial_weights,
         jnp.pad(coupling, ((0, 0), (0, spec_pad), (0, 0))),
@@ -369,39 +691,55 @@
         output_weights[None, :],
     )
 
-    grad = fgrad[:, : py * depth].reshape(px, py, depth, channels)
-    for axis, dim in (("gx", 0), ("gy", 1), ("gz", 2)):
-        grad = fold_back(grad, axis, dim, reach)
-    fj = fj.reshape(nby, nbx, 3, wide, wide, depth)
-    force = jnp.zeros((3, px, py, depth), jnp.float32)
-    for by in range(nby):
-        for bx in range(nbx):
-            force = force + jnp.pad(
-                fj[by, bx],
-                (
-                    (0, 0),
-                    (bx * BLOCK, px - wide - bx * BLOCK),
-                    (by * BLOCK, py - wide - by * BLOCK),
-                    (0, 0),
-                ),
-            )
-    for axis, dim in (("gx", 1), ("gy", 2), ("gz", 3)):
-        force = fold_back(force, axis, dim, reach)
+    force = wsum.transpose(1, 2, 0, 3).reshape(px * 4, nby * rows)
+    force = jnp.dot(force, jnp.asarray(pick_pos.T), precision=HIGH).reshape(px, 4, 9 * o)
+    force = jnp.pad(force, ((sx - reach, sx - reach), (0, 0), (0, 0)))
+    force = force.reshape(3, cx, lat, 4, 9, o).transpose(0, 4, 1, 3, 2, 5)
+    force = jnp.stack([force[n] for n in order]).reshape(3, 3, 3, cx * 4, lat * o)
     node = node[:, :4].reshape(nby, nbx, BLOCK, BLOCK, sz, 4)
-    node = node.transpose(5, 1, 2, 0, 3, 4).reshape(4, sx, sy, sz)
-    node = node + jnp.pad(force, ((0, 1), (0, 0), (0, 0), (0, 0)))
-
-    def to_cells(grid):
-        lead = grid.shape[3:]
-        cells = grid.reshape((cx, lat, cy, lat, cz, lat) + lead)
-        cells = cells.transpose((0, 2, 4, 1, 3, 5) + tuple(range(6, cells.ndim)))
-        return cells.reshape((cx, cy, cz, capacity) + lead)
-
-    feature_grad = jnp.einsum("xyzts,xyztc->xyzsc", place_full, to_cells(grad), precision=HIGH)
-    node_slots = jnp.einsum(
-        "xyzts,xyztk->xyzks", place_full, to_cells(node.transpose(1, 2, 3, 0)), precision=HIGH
-    )
-    return (node_slots[:, :, :, 3], node_slots[:, :, :, :3], feature_grad)
+    node = node.transpose(5, 1, 2, 0, 3, 4).reshape(4, cx, lat * o)
+    node = node.transpose(1, 0, 2).reshape(cx * 4, lat * o)
+
+    def half(*shape):
+        return pltpu.VMEM(shape + (channels,), jnp.bfloat16)
+
+    def tile(*lead):
+        return pltpu.VMEM(lead + (cx * 4, lat * o), jnp.float32)
+
+    grad, slots = pl.pallas_call(
+        functools.partial(gather_kernel, dims),
+        out_shape=(
+            jax.ShapeDtypeStruct((cx, column, channels), jnp.float32),
+            jax.ShapeDtypeStruct((cx, 4, column), jnp.float32),
+        ),
+        in_specs=[vmem] * 7,
+        out_specs=(vmem, vmem),
+        scratch_shapes=[
+            pltpu.VMEM((sx, total, channels), jnp.float32),
+            tile(3, 3),
+            half(2, reach, total),
+            half(2, reach, total),
+            half(2, sx, yp),
+            half(2, sx, yp),
+            half(2, sx, zp),
+            half(2, sx, zp),
+            tile(2, 3, 3),
+            tile(2, 3),
+            tile(2),
+            pltpu.SemaphoreType.DMA((16,)),
+            pltpu.SemaphoreType.DMA((16,)),
+        ],
+        compiler_params=pltpu.CompilerParams(
+            collective_id=1, has_side_effects=True, vmem_limit_bytes=limit
+        ),
+        name="halo_back",
+    )(place, place_t, fgrad, force, node, zsel_half, ysel_half)
+    slots = slots.reshape(cx, 4, cy, cz, capacity).transpose(0, 2, 3, 1, 4)
+    return (
+        slots[:, :, :, 3],
+        slots[:, :, :, :3],
+        grad.reshape(cx, cy, cz, capacity, channels),
+    )
 
 
 def solution(mesh):

time: 105 us -> 79.7 us (0.76)
  Pallas kernels: 21.3 us -> 65.2 us
  starting transfers between devices: 32.3 us -> 0 us
  waiting for transfers between devices: 29.4 us -> 0 us
  local copies, waits for them, and re-layouts: 15 us -> 7.4 us
    pallas_call x0 -> x2, Pallas kernels: none -> 37.4 us  [the longest x1 19.5 us: body(): pl.pallas_call(functools.partial(spread_kernel, dims), out_shape=(jax.Sha...]
    ppermute x24 -> x0, starting transfers between devices: 32.3 us -> none  [shift(): return lax.ppermute(block, axis, pairs)]
    ppermute x24 -> x0, waiting for transfers between devices: 29.4 us -> none  [shift(): return lax.ppermute(block, axis, pairs)]
    pallas_call x1, Pallas kernels: 21.3 us -> 27.8 us  [body(): pl.pallas_call(functools.partial(compute_kernel, (sx, sy, sz, reach, nb))...]
    slice x31 -> x4, local copies, waits for them, and re-layouts: 6.32 us -> 0.66 us  [the longest x1 0.6 us: body(): slots[:, :, :, :3]]
    another operation x18 -> x1, local copies, waits for them, and re-layouts: 2.44 us -> 0.17 us  [body(): jnp.stack([force[n] for n in order]).reshape(3, 3, 3, cx * 4, lat * o)]
    reshape x4 -> x10, local copies, waits for them, and re-layouts: 2.51 us -> 1.45 us  [the longest x2 0.51 us: body(): posw = jnp.stack([tiles[n] for n in order]).reshape(3, 9, cx, 4, lat, o)]
    dot_general x4 -> x3, matrix products: 1.71 us -> 2.45 us  [the longest x1 0.94 us: body(): jnp.dot(posw.reshape(px * 4, 9 * o), jnp.asarray(pick_pos), precision=HIGH)]
  transfers between devices with their start and end apart: 24 -> 0, of which waited for: 14 -> 0; matrix products, arithmetic and copies ran while one was open for 11% -> 0% of each run, Pallas kernels for 0% -> 0%
where the time goes in v2:
time: 79.7 us; the launch traced here: 79.2 us
  Pallas kernels  65.2 us (82%)
  local copies, waits for them, and re-layouts  7.4 us (9%)
  other arithmetic  3.17 us (4%)
  matrix products  2.45 us (3%)
  between operations  1.01 us (1%)
    pallas_call x1, Pallas kernels, body(): pl.pallas_call(functools.partial(compute_kernel, (sx, sy, sz, reach, nb))...  27.8 us
    pallas_call x1, Pallas kernels, body(): pl.pallas_call(functools.partial(spread_kernel, dims), out_shape=(jax.Sha...  19.5 us
    pallas_call x1, Pallas kernels, body(): pl.pallas_call(functools.partial(gather_kernel, dims), out_shape=(jax.Sha...  17.9 us
    unnamed x25, local copies, waits for them, and re-layouts  2.73 us

profile of v2, /device:TPU:0, one launch (start us, length us, event | category | flops | bytes accessed | tf_op | source)
XLA Modules:
  0.0 79.2 jit_solution(9793400638196634365)
XLA Ops:
  0.6 0.0 copy-start.2
  0.6 0.0 copy-start.3
  0.7 0.0 copy-start.5
  0.7 0.1 add.88
  0.7 0.1 add.89
  0.8 0.7 compare_convert_fusion
  1.6 0.7 convert_bitcast_fusion
  2.3 0.7 maximum_bitcast_fusion
  3.0 0.1 reshape.171
  3.1 0.7 convert_clamp_fusion
  3.8 0.1 add.86
  3.9 0.1 squeeze.8
  4.0 0.9 %fusion.9 = (f32[2,5,128]{2,1,0:T(8,128)S(1)}, f32[2,5,128]{2,1,0:T(8,128)S(1)}) fusion(f32[2,5,128]{2,1,0:T(8,128)} %constant.68, f32[2,5,128]{2,1,0:T(8,128)S(1)} %reshape.171, s32[2,128]{1,0:T(2,128)S(1)} %multiply_add_fusion), kind=kOutput, calls=%fused_computation.27 | convolution fusion | flops 2000128 | bytes 21504 | tf_op jit(solution)/shard_map/xks,xst->xkt/dot_general | solution.py:596
  4.9 0.7 copy.41
  5.7 0.8 %copy.42.hw_ref = f32[128,16]{1,0:T(8,128)S(1)} copy(f32[128,16]{0,1:T(8,128)} %param.28) | data formatting | bytes 16384 | tf_op args[7]
  6.5 0.1 fusion.1
  6.6 0.2 reshape.167
  6.8 0.5 copy.39
  7.3 0.0 copy-done.2
  7.3 0.0 copy-done.3
  7.4 0.0 copy-done.5
  7.4 19.5 %halo_out.1 = (bf16[14,160,128]{2,1,0:T(8,128)(2,1)S(1)}, f32[3,3,3,8,128]{4,3,2,1,0:T(8,128)S(1)}) custom-call(bf16[2,128,128]{2,1,0:T(8,128)(2,1)S(1)} %get-tuple-element.32.place_ref, bf16[2,128,128]{2,1,0:T(8,128)(2,1)S(1)} %bitcast.63, f32[8,128]{1,0:T(8,128)S(1)} %bitcast.65, bf16[64,32]{1,0:T(8,128)(2,1)S(1)} %copy-done.3, bf16[64,96]{1,0:T(8,128)(2,1)S(1)} %copy-done.2), custom_call_target="tpu_custom_call" | custom-call | tf_op jit(solution)/shard_map/halo_out/pallas_call | solution.py:603
  26.9 0.2 reshape.150
  27.2 0.0 copy-start.8
  27.2 0.0 copy-start.10
  27.2 0.3 copy.60
  27.5 0.0 copy-start
  27.5 0.0 copy-start.1
  27.5 0.0 copy-start.4
  27.5 0.0 copy-start.6
  27.5 0.0 copy-start.7
  27.6 0.2 reshape.151
  27.7 0.5 copy-done.8
  28.2 0.9 %fusion.4 = f32[14,4,4,80]{3,0,2,1:T(8,128)S(1)} fusion(f32[4,80,288,1]{2,1,0,3:T(8,128)S(1)} %copy-done.8, f32[24,4,288]{2,0,1:T(8,128)S(1)} %reshape.151), kind=kOutput, calls=%fused_computation.11 | convolution fusion | flops 61931520 | bytes 661504 | tf_op jit(solution)/shard_map/dot_general | solution.py:643
  29.2 0.0 copy-done.10
  29.2 0.0 copy-start.9
  29.2 0.1 fusion.3.posw_ref
  29.3 0.0 copy-done
  29.3 0.0 copy-done.1
  29.3 0.0 copy-done.4
  29.3 0.0 copy-done.6
  29.3 0.0 copy-done.7
  29.3 27.8 %pair_layer.1 = (f32[14,160,128]{2,1,0:T(8,128)S(1)}, f32[4,14,4,80]{3,2,1,0:T(4,128)S(1)}, f32[256,128]{1,0:T(8,128)S(1)}) custom-call(bf16[14,160,128]{2,1,0:T(8,128)(2,1)S(1)} %get-tuple-element.10.layer_ref, f32[4,14,4,80]{3,2,1,0:T(4,128)S(1)} %fusion.3.posw_ref, bf16[320,160]{1,0:T(8,128)(2,1)S(1)} %copy-done, bf16[160,320]{1,0:T(8,128)(2,1)S(1)} %copy-done.1, ...), custom_call_target="tpu_custom_call" | custom-call | tf_op jit(solution)/shard_map/pair_layer/pallas_call | solution.py:659
  57.2 0.1 reshape.172
  57.3 0.0 copy-done.9
  57.3 0.6 fusion.10
  57.9 0.6 copy.46
  58.5 0.2 reshape.159
  58.7 0.1 reshape.156
  58.9 0.1 fusion.7
  59.0 0.1 pad_maximum_fusion
  59.0 0.2 copy.45
  59.2 0.2 reshape.157.force_ref
  59.5 17.9 %halo_back.1 = (f32[2,128,128]{2,1,0:T(8,128)S(1)}, f32[2,4,128]{2,1,0:T(4,128)S(1)}) custom-call(bf16[2,128,128]{2,1,0:T(8,128)(2,1)S(1)} %get-tuple-element.32.place_ref, bf16[2,128,128]{2,1,0:T(8,128)(2,1)S(1)} %get-tuple-element.31.place_t_ref, f32[14,160,128]{2,1,0:T(8,128)S(1)} %get-tuple-element.12.grad_ref, ...), custom_call_target="tpu_custom_call" | custom-call | tf_op jit(solution)/shard_map/halo_back/pallas_call | solution.py:709
  77.3 0.1 reshape.161
  77.4 0.6 slice_bitcast_fusion.2
  78.0 0.6 slice.65
  78.6 0.7 copy.63
  (15 shorter events, 0.2 us)
Async XLA Ops:
  0.6 6.7 %copy-start.2 = (bf16[64,96]{1,0:T(8,128)(2,1)S(1)}, bf16[64,96]{1,0:T(8,128)(2,1)}, u32[]{:S(2)}) copy-start(bf16[64,96]{1,0:T(8,128)(2,1)} %constant.41.clone.ysel_ref) | copy-start | bytes 36868
  0.6 6.7 %copy-start.3 = (bf16[64,32]{1,0:T(8,128)(2,1)S(1)}, bf16[64,32]{1,0:T(8,128)(2,1)}, u32[]{:S(2)}) copy-start(bf16[64,32]{1,0:T(8,128)(2,1)} %constant.40.clone.zsel_ref) | copy-start | bytes 12292
  0.7 6.7 %copy-start.5 = (bf16[2,2,1,64,128]{4,3,2,1,0:T(8,128)(2,1)S(1)}, bf16[2,2,1,64,128]{4,3,2,1,0:T(8,128)(2,1)}, u32[]{:S(2)}) copy-start(bf16[2,2,1,64,128]{4,3,2,1,0:T(8,128)(2,1)} %param.24) | copy-start | bytes 196612
  27.2 1.0 %copy-start.8 = (f32[4,80,288,1]{2,1,0,3:T(8,128)S(1)}, f32[4,80,288,1]{2,1,0,3:T(8,128)}, u32[]{:S(2)}) copy-start(f32[4,80,288,1]{2,1,0,3:T(8,128)} %constant.69) | copy-start | bytes 1105924
  27.2 2.0 %copy-start.10 = (f32[14,4,4,80]{3,1,0,2:T(4,128)S(1)}, f32[14,4,4,80]{3,1,0,2:T(4,128)}, u32[]{:S(2)}) copy-start(f32[14,4,4,80]{3,1,0,2:T(4,128)} %constant.65) | copy-start | bytes 215044
  27.5 1.8 %copy-start = (bf16[320,160]{1,0:T(8,128)(2,1)S(1)}, bf16[320,160]{1,0:T(8,128)(2,1)}, u32[]{:S(2)}) copy-start(bf16[320,160]{1,0:T(8,128)(2,1)} %constant.45.clone.pick_ref) | copy-start | bytes 307204
  27.5 1.8 %copy-start.1 = (bf16[160,320]{1,0:T(8,128)(2,1)S(1)}, bf16[160,320]{1,0:T(8,128)(2,1)}, u32[]{:S(2)}) copy-start(bf16[160,320]{1,0:T(8,128)(2,1)} %constant.46.clone.pick_t_ref) | copy-start | bytes 307204
  27.5 1.8 %copy-start.4 = (f32[128,128]{1,0:T(8,128)S(1)}, f32[128,128]{1,0:T(8,128)}, u32[]{:S(2)}) copy-start(f32[128,128]{1,0:T(8,128)} %mixing_ref.1) | copy-start | bytes 196612
  27.5 1.8 %copy-start.6 = (f32[2,8,128]{2,1,0:T(8,128)S(1)}, f32[2,8,128]{2,1,0:T(8,128)}, u32[]{:S(2)}) copy-start(f32[2,8,128]{2,1,0:T(8,128)} %radial_ref.1) | copy-start | bytes 24580
  27.5 1.8 %copy-start.7 = (f32[16]{0:T(128)S(1)}, f32[16]{0:T(128)}, u32[]{:S(2)}) copy-start(f32[16]{0:T(128)} %param.29) | copy-start | bytes 196
  29.2 28.2 %copy-start.9 = (f32[320,288,1]{0,1,2:T(8,128)S(1)}, f32[320,288,1]{0,1,2:T(8,128)}, u32[]{:S(2)}) copy-start(f32[320,288,1]{0,1,2:T(8,128)} %constant.70) | copy-start | bytes 1105924

commit v3 on v2

--- a/solution.py
+++ b/solution.py
@@ -72,12 +72,14 @@
     posj_ref,
     fj_ref,
     slab_ref,
-    edge_ref,
+    even_ref,
+    odd_ref,
     field_ref,
     sv_ref,
     en_ref,
     acc_ref,
-    g_ref,
+    geven_ref,
+    godd_ref,
 ):
     sx, sy, sz, reach, nb = dims
     nbx, nby = sx // BLOCK, sy // BLOCK
@@ -90,28 +92,24 @@
     chunks = [(c, min(128, near - c)) for c in range(0, near, 128)]
     root3 = math.sqrt(3.0)
 
-    def build(x, carry):
+    for x in range(px):
         full = jnp.dot(pick_ref[...], layer_ref[x], preferred_element_type=jnp.float32)
         full = full.astype(jnp.bfloat16)
         for by in range(nby):
             slab_ref[by, x] = full[by * rows : (by + 1) * rows]
             acc_ref[by, x] = jnp.zeros((rows, full.shape[1]), jnp.float32)
-        return carry
-
-    lax.fori_loop(0, px, build, 0)
     wsum_ref[...] = jnp.zeros(wsum_ref.shape, jnp.float32)
     fj_ref[...] = jnp.zeros(fj_ref.shape, jnp.float32)
 
-    def place_columns(by, carry):
+    for by in range(nby):
         for bx in range(nbx):
             for k in range(wide):
                 posj_ref[by * nbx + bx, :, k * rows : (k + 1) * rows] = posw_ref[by, bx * BLOCK + k]
-        return carry
-
-    lax.fori_loop(0, nby, place_columns, 0)
-
-    def forward(blk, carry):
-        by, bx = blk // nbx, lax.rem(blk, nbx)
+
+    blocks = nbx * nby
+    half = blocks // 2
+
+    def basis(blk, edge_ref, slot):
         pi = rpos_ref[blk]
         for c, w in chunks:
             pj = posj_ref[blk, :, c : c + w]
@@ -131,10 +129,13 @@
             for b in range(nb):
                 for m in range(4):
                     k = (b * 4 + m) * own
-                    edge_ref[blk, k : k + own, c : c + w] = (qs[m] * now).astype(jnp.bfloat16)
+                    edge_ref[slot, k : k + own, c : c + w] = (qs[m] * now).astype(jnp.bfloat16)
                 before, now = now, twice * now - before
+
+    def gather(blk, edge_ref, slot):
+        by, bx = blk // nbx, lax.rem(blk, nbx)
         slab = slab_ref[by, pl.ds(bx * BLOCK, wide)].reshape(near, -1)
-        summed = jnp.dot(edge_ref[blk], slab, preferred_element_type=jnp.float32)
+        summed = jnp.dot(edge_ref[slot], slab, preferred_element_type=jnp.float32)
         for m in range(4):
             total = None
             for b in range(nb):
@@ -142,9 +143,19 @@
                 term = summed[k : k + own] * radial_ref[min(m, 1), b : b + 1, :]
                 total = term if total is None else total + term
             sv_ref[m, pl.ds(blk * own, own)] = total
+
+    def forward(i, carry):
+        gather(2 * i, even_ref, i)
+        basis(2 * i + 1, odd_ref, i)
+        gather(2 * i + 1, odd_ref, i)
+        basis(2 * i + 2, even_ref, i + 1)
         return carry
 
-    lax.fori_loop(0, nbx * nby, forward, 0)
+    basis(0, even_ref, 0)
+    lax.fori_loop(0, half - 1, forward, 0)
+    gather(blocks - 2, even_ref, half - 1)
+    basis(blocks - 1, odd_ref, half - 1)
+    gather(blocks - 1, odd_ref, half - 1)
 
     flat = rpos_ref[...].reshape(nbx * nby * own, -1)
     occ = flat[:, 3:4]
@@ -172,7 +183,7 @@
     for m in range(1, 4):
         sv_ref[m] = twice_d * sv_ref[m]
 
-    def backward(blk, carry):
+    def scatter(blk, edge_ref, slot, g_ref):
         by, bx = blk // nbx, lax.rem(blk, nbx)
         parts = []
         for b in range(nb):
@@ -187,8 +198,11 @@
             d_half, slab, (((1,), (1,)), ((), ())), preferred_element_type=jnp.float32
         )
         d_turn = d_full.T.astype(jnp.bfloat16)
-        turned = jnp.dot(d_turn, edge_ref[blk], preferred_element_type=jnp.float32)
+        turned = jnp.dot(d_turn, edge_ref[slot], preferred_element_type=jnp.float32)
         acc_ref[by, pl.ds(bx * BLOCK, wide)] += turned.T.reshape(wide, rows, -1)
+
+    def forces(blk, g_ref):
+        by, bx = blk // nbx, lax.rem(blk, nbx)
         total = [jnp.zeros((own, 1), jnp.float32) for _ in range(3)]
         for c, w in chunks:
             nx, ny, nz, inv, q, p, s1, c1 = (field_ref[blk, n, :, c : c + w] for n in range(8))
@@ -228,20 +242,27 @@
             total[0],
             jnp.where(lane == 1, total[1], jnp.where(lane == 2, total[2], en_ref[here])),
         )
+
+    def backward(i, carry):
+        scatter(2 * i + 1, odd_ref, i, godd_ref)
+        forces(2 * i, geven_ref)
+        scatter(2 * i + 2, even_ref, i + 1, geven_ref)
+        forces(2 * i + 1, godd_ref)
         return carry
 
-    lax.fori_loop(0, nbx * nby, backward, 0)
-
-    def merge(x, carry):
+    scatter(0, even_ref, 0, geven_ref)
+    lax.fori_loop(0, half - 1, backward, 0)
+    scatter(blocks - 1, odd_ref, half - 1, godd_ref)
+    forces(blocks - 2, geven_ref)
+    forces(blocks - 1, godd_ref)
+
+    for x in range(px):
         stack = jnp.concatenate([acc_ref[by, x] for by in range(nby)], axis=0)
         top = stack.astype(jnp.bfloat16)
         rest = (stack - top.astype(jnp.float32)).astype(jnp.bfloat16)
         fgrad_ref[x] = jnp.dot(
             pick_t_ref[...], top, preferred_element_type=jnp.float32
         ) + jnp.dot(pick_t_ref[...], rest, preferred_element_type=jnp.float32)
-        return carry
-
-    lax.fori_loop(0, px, merge, 0)
 
 
 def ring(axis):
@@ -278,13 +299,17 @@
 
 def spread_kernel(
     dims,
-    place_ref,
+    spacing,
+    counts_ref,
+    pos_ref,
+    kind_ref,
     feat_ref,
-    small_ref,
     zsel_ref,
     ysel_ref,
     layer_ref,
     tile_ref,
+    place_ref,
+    small_ref,
     zs_ref,
     ys_ref,
     send_sem,
@@ -294,8 +319,35 @@
     around = {axis: ring(axis) for axis in ("gz", "gy", "gx")}
     barrier = greet(around)
     send = sender(send_sem, recv_sem)
-    tile_ref[0, 0, 0] = small_ref[...]
-    for col in range(sx // lat):
+    cx, cy, cz, _, capacity = pos_ref.shape
+    sy, sz = cy * lat, cz * lat
+    slot = lax.broadcasted_iota(jnp.int32, (1, capacity), 1)
+    for col in range(cx):
+        pieces, codes = [], []
+        for cell_y in range(cy):
+            for cell_z in range(cz):
+                xyz = pos_ref[col, cell_y, cell_z]
+                site = jnp.clip(jnp.floor(xyz * (1.0 / spacing)), 0.0, lat - 1.0)
+                codes.append(
+                    (site[0:1] * sy + site[1:2] + cell_y * lat) * sz + site[2:3] + cell_z * lat
+                )
+                occ = (slot < counts_ref[col, cell_y, cell_z]).astype(jnp.float32)
+                kind = kind_ref[col, cell_y, cell_z : cell_z + 1].astype(jnp.float32)
+                pieces.append(
+                    jnp.concatenate([xyz, occ, kind, jnp.zeros((3, capacity), jnp.float32)], axis=0)
+                )
+        code = jnp.concatenate(codes, axis=1)
+        small = jnp.concatenate(pieces, axis=1)
+        count = code.shape[1]
+        place = (
+            code == lax.broadcasted_iota(jnp.int32, (count, count), 0).astype(jnp.float32)
+        ).astype(jnp.float32)
+        small = lax.dot_general(
+            small, place, (((1,), (1,)), ((), ())), precision=HIGH, preferred_element_type=jnp.float32
+        )
+        small_ref[col] = small
+        tile_ref[0, 0, 0, col * 4 : (col + 1) * 4] = small[0:4]
+        place_ref[col] = place.astype(jnp.bfloat16)
         sites = jnp.dot(place_ref[col], feat_ref[col], preferred_element_type=jnp.float32)
         sites = sites.astype(jnp.bfloat16)
         for k in range(lat):
@@ -361,14 +413,14 @@
 def gather_kernel(
     dims,
     place_ref,
-    place_t_ref,
     grad_ref,
     force_ref,
     node_ref,
     zsel_ref,
     ysel_ref,
     out_ref,
-    small_ref,
+    energy_ref,
+    xyz_ref,
     sum_ref,
     fsum_ref,
     gs_ref,
@@ -482,15 +534,21 @@
         whole = jnp.concatenate(sites, axis=0)
         top = whole.astype(jnp.bfloat16)
         rest = (whole - top.astype(jnp.float32)).astype(jnp.bfloat16)
-        out_ref[col] = jnp.dot(
-            place_t_ref[col], top, preferred_element_type=jnp.float32
-        ) + jnp.dot(place_t_ref[col], rest, preferred_element_type=jnp.float32)
-        small_ref[col] = jnp.dot(
+        turn = place_ref[col].astype(jnp.float32).T.astype(jnp.bfloat16)
+        out_ref[col] = jnp.dot(turn, top, preferred_element_type=jnp.float32) + jnp.dot(
+            turn, rest, preferred_element_type=jnp.float32
+        )
+        slots = jnp.dot(
             tile[col * part : (col + 1) * part],
             place_ref[col].astype(jnp.float32),
             precision=HIGH,
             preferred_element_type=jnp.float32,
         )
+        _, cy, cz, _, capacity = xyz_ref.shape
+        for n in range(cy * cz):
+            lanes = slice(n * capacity, (n + 1) * capacity)
+            xyz_ref[col, n // cz, n % cz] = slots[0:3, lanes]
+            energy_ref[col, n // cz, n % cz : n % cz + 1] = slots[3:4, lanes]
     for copy in x_copies + f_copies + y_copies + fy_copies + z_copies + fz_copies:
         copy.wait_send()
 
@@ -575,39 +633,21 @@
     (o, zp, yp, total), pick, pick_pos, zsel, ysel = tables(sx, sy, sz, reach)
     column = cy * cz * capacity
 
-    occupied = (jnp.arange(capacity, dtype=jnp.int32) < counts[..., None]).astype(jnp.float32)
-    site = jnp.clip(jnp.floor(local_pos * (1.0 / spacing)).astype(jnp.int32), 0, lat - 1)
-    cell_y = np.arange(cy, dtype=np.int32)[None, :, None, None] * lat
-    cell_z = np.arange(cz, dtype=np.int32)[None, None, :, None] * lat
-    code = (site[:, :, :, 0] * sy + site[:, :, :, 1] + cell_y) * sz + site[:, :, :, 2] + cell_z
-    code = code.reshape(cx, column)
-    count = np.arange(column, dtype=np.int32)
-    place = (code[:, None, :] == count[None, :, None]).astype(jnp.bfloat16)
-    place_t = (code[:, :, None] == count[None, None, :]).astype(jnp.bfloat16)
-    small = jnp.concatenate(
-        [
-            local_pos,
-            occupied[:, :, :, None],
-            species.astype(jnp.float32)[:, :, :, None],
-        ],
-        axis=3,
-    )
-    small = small.transpose(0, 3, 1, 2, 4).reshape(cx, 5, column)
-    small_sites = jnp.einsum("xks,xst->xkt", small, place_t.astype(jnp.float32), precision=HIGH)
-
     vmem = pl.BlockSpec(memory_space=pltpu.VMEM)
     dims = (sx, lat, reach, o, zp, yp)
     limit = 50 * 1024 * 1024
     zsel_half = jnp.asarray(zsel, jnp.bfloat16)
     ysel_half = jnp.asarray(ysel, jnp.bfloat16)
-    layers, tiles = pl.pallas_call(
-        functools.partial(spread_kernel, dims),
+    layers, tiles, place, small_sites = pl.pallas_call(
+        functools.partial(spread_kernel, dims, spacing),
         out_shape=(
             jax.ShapeDtypeStruct((px, total, channels), jnp.bfloat16),
             jax.ShapeDtypeStruct((3, 3, 3, cx * 4, lat * o), jnp.float32),
+            jax.ShapeDtypeStruct((cx, column, column), jnp.bfloat16),
+            jax.ShapeDtypeStruct((cx, 8, column), jnp.float32),
         ),
-        in_specs=[vmem] * 5,
-        out_specs=(vmem, vmem),
+        in_specs=[pl.BlockSpec(memory_space=pltpu.SMEM)] + [vmem] * 5,
+        out_specs=(vmem,) * 4,
         scratch_shapes=[
             pltpu.VMEM((2, sx, zp, channels), jnp.bfloat16),
             pltpu.VMEM((2, sx, yp, channels), jnp.bfloat16),
@@ -619,9 +659,10 @@
         ),
         name="halo_out",
     )(
-        place,
+        counts,
+        local_pos,
+        species,
         features.reshape(cx, column, channels),
-        small_sites[:, :4].reshape(cx * 4, lat * o),
         zsel_half,
         ysel_half,
     )
@@ -648,7 +689,7 @@
             np.zeros((1, sx, sy, sz), np.float32),
         ]
     )
-    small_grid = small_sites.reshape(cx, 5, lat, sy, sz).transpose(1, 0, 2, 3, 4).reshape(5, sx, sy, sz)
+    small_grid = small_sites[:, :5].reshape(cx, 5, lat, sy, sz).transpose(1, 0, 2, 3, 4).reshape(5, sx, sy, sz)
     rpos = (small_grid + own_shift).reshape(5, nbx, BLOCK, nby, BLOCK, sz)
     rpos = rpos.transpose(3, 1, 2, 4, 5, 0).reshape(blocks, own, 5)
     rpos = jnp.pad(rpos, ((0, 0), (0, 0), (0, 3)))
@@ -669,11 +710,13 @@
             pltpu.VMEM((blocks, 4, near), jnp.float32),
             pltpu.VMEM((4, near), jnp.float32),
             pltpu.VMEM((nby, px, rows, channels), jnp.bfloat16),
-            pltpu.VMEM((blocks, nb * 4 * own, near), jnp.bfloat16),
+            pltpu.VMEM((blocks // 2, nb * 4 * own, near), jnp.bfloat16),
+            pltpu.VMEM((blocks // 2, nb * 4 * own, near), jnp.bfloat16),
             pltpu.VMEM((blocks, 8, own, near), jnp.float32),
             pltpu.VMEM((4, total_own, channels), jnp.float32),
             pltpu.VMEM((total_own, 128), jnp.float32),
             pltpu.VMEM((nby, px, rows, channels), jnp.float32),
+            pltpu.VMEM((nb * 4 * own, near), jnp.float32),
             pltpu.VMEM((nb * 4 * own, near), jnp.float32),
         ],
         compiler_params=pltpu.CompilerParams(vmem_limit_bytes=limit),
@@ -706,14 +749,15 @@
     def tile(*lead):
         return pltpu.VMEM(lead + (cx * 4, lat * o), jnp.float32)
 
-    grad, slots = pl.pallas_call(
+    grad, energy, forces = pl.pallas_call(
         functools.partial(gather_kernel, dims),
         out_shape=(
             jax.ShapeDtypeStruct((cx, column, channels), jnp.float32),
-            jax.ShapeDtypeStruct((cx, 4, column), jnp.float32),
+            jax.ShapeDtypeStruct((cx, cy, cz, capacity), jnp.float32),
+            jax.ShapeDtypeStruct((cx, cy, cz, 3, capacity), jnp.float32),
         ),
-        in_specs=[vmem] * 7,
-        out_specs=(vmem, vmem),
+        in_specs=[vmem] * 6,
+        out_specs=(vmem, vmem, vmem),
         scratch_shapes=[
             pltpu.VMEM((sx, total, channels), jnp.float32),
             tile(3, 3),
@@ -733,13 +777,8 @@
             collective_id=1, has_side_effects=True, vmem_limit_bytes=limit
         ),
         name="halo_back",
-    )(place, place_t, fgrad, force, node, zsel_half, ysel_half)
-    slots = slots.reshape(cx, 4, cy, cz, capacity).transpose(0, 2, 3, 1, 4)
-    return (
-        slots[:, :, :, 3],
-        slots[:, :, :, :3],
-        grad.reshape(cx, cy, cz, capacity, channels),
-    )
+    )(place, fgrad, force, node, zsel_half, ysel_half)
+    return energy, forces, grad.reshape(cx, cy, cz, capacity, channels)
 
 
 def solution(mesh):

time: 79.7 us -> 71.7 us (0.90)
  Pallas kernels: 65.2 us -> 56.2 us
  local copies, waits for them, and re-layouts: 7.4 us -> 11.6 us
  other arithmetic: 3.17 us -> 0.88 us
  matrix products: 2.45 us -> 1.51 us
    pallas_call x1, Pallas kernels: 27.8 us -> 18.3 us  [body(): pl.pallas_call(functools.partial(compute_kernel, (sx, sy, sz, reach, nb))...]
    unnamed x25 -> x35, local copies, waits for them, and re-layouts: 2.73 us -> 8.61 us
    dot_general x1 -> x0, matrix products: 0.94 us -> none  [body(): jnp.einsum('xks,xst->xkt', small, place_t.astype(jnp.float32), precision=...]
    convert_element_type x2 -> x0, other arithmetic: 0.85 us -> none  [the longest x1 0.75 us: body(): (jnp.arange(capacity, dtype=jnp.int32) < counts[..., None]).astype(jnp.fl...]
where the time goes in v3:
time: 71.7 us; the launch traced here: 71.1 us
  Pallas kernels  56.2 us (78%)
  local copies, waits for them, and re-layouts  11.6 us (16%)
  matrix products  1.51 us (2%)
  between operations  0.94 us (1%)
  other arithmetic  0.88 us (1%)
    pallas_call x1, Pallas kernels, body(): pl.pallas_call(functools.partial(spread_kernel, dims, spacing), out_shape...  20.1 us
    pallas_call x1, Pallas kernels, body(): pl.pallas_call(functools.partial(compute_kernel, (sx, sy, sz, reach, nb))...  18.3 us
    pallas_call x1, Pallas kernels, body(): pl.pallas_call(functools.partial(gather_kernel, dims), out_shape=(jax.Sha...  17.8 us
    unnamed x35, local copies, waits for them, and re-layouts  8.61 us

profile of v3, /device:TPU:0, one launch (start us, length us, event | category | flops | bytes accessed | tf_op | source)
XLA Modules:
  0.0 71.1 jit_solution(14172255093796493105)
XLA Ops:
  0.6 0.8 %copy.29.counts_ref = s32[2,2,1]{2,1,0:T(2,128)S(1)} copy(s32[2,2,1]{1,2,0:T(1,128)} %param.18) | data formatting | bytes 32 | tf_op args[1]
  1.4 0.7 copy.30.pos_ref
  2.1 0.7 %copy.36 = f32[3,10,128]{2,1,0:T(8,128)S(1)} copy(f32[3,10,128]{2,0,1:T(4,128)} %param.22) | data formatting | bytes 30720 | tf_op args[5]
  2.8 0.8 %copy.37.hw_ref = f32[128,16]{1,0:T(8,128)S(1)} copy(f32[128,16]{0,1:T(8,128)} %param.24) | data formatting | bytes 16384 | tf_op args[7]
  3.6 0.0 copy-start.2
  3.6 0.7 copy-done.2
  4.3 0.0 copy-start.4
  4.3 0.7 %copy-done.4 = bf16[64,32]{1,0:T(8,128)(2,1)S(1)} copy-done((bf16[64,32]{1,0:T(8,128)(2,1)S(1)}, bf16[64,32]{1,0:T(8,128)(2,1)}, u32[]{:S(2)}) %copy-start.4) | copy-done | bytes 4120
  5.1 0.0 copy-start.7
  5.1 0.8 %copy-done.7 = bf16[2,2,1,64,128]{4,3,2,1,0:T(8,128)(2,1)S(1)} copy-done((bf16[2,2,1,64,128]{4,3,2,1,0:T(8,128)(2,1)S(1)}, bf16[2,2,1,64,128]{4,3,2,1,0:T(8,128)(2,1)}, u32[]{:S(2)}) %copy-start.7) | copy-done | bytes 65560
  5.9 0.0 copy-start.9
  5.9 0.7 copy-done.9
  6.6 20.1 %halo_out.1 = (bf16[14,160,128]{2,1,0:T(8,128)(2,1)S(1)}, f32[3,3,3,8,128]{4,3,2,1,0:T(8,128)S(1)}, bf16[2,128,128]{2,1,0:T(8,128)(2,1)S(1)}, f32[2,8,128]{2,1,0:T(8,128)S(1)}) custom-call(s32[2,2,1]{2,1,0:T(2,128)S(1)} %copy.29.counts_ref, f32[2,2,1,3,64]{4,3,2,1,0:T(4,128)S(1)} %copy.30.pos_ref, s32[2,2,1,64]{3,2,1,0:T(1,128)S(1)} %copy-done.9, ...), custom_call_target="tpu_custom_call" | custom-call | tf_op jit(solution)/shard_map/halo_out/pallas_call | solution.py:641
  26.7 0.7 slice_add_fusion
  27.4 0.2 reshape.71
  27.6 0.5 copy.34
  28.2 0.2 reshape.55
  28.4 0.0 copy-start.11
  28.4 0.0 copy-start.13
  28.4 0.3 copy.52
  28.7 0.0 copy-start
  28.7 0.0 copy-start.1
  28.7 0.0 copy-start.6
  28.8 0.0 copy-start.8
  28.8 0.0 copy-start.10
  28.8 0.2 reshape.56
  29.0 0.5 copy-done.11
  29.4 0.9 %fusion.1 = f32[14,4,4,80]{3,0,2,1:T(8,128)S(1)} fusion(f32[4,80,288,1]{2,1,0,3:T(8,128)S(1)} %copy-done.11, f32[24,4,288]{2,0,1:T(8,128)S(1)} %reshape.56), kind=kOutput, calls=%fused_computation.6 | convolution fusion | flops 61931520 | bytes 661504 | tf_op jit(solution)/shard_map/dot_general | solution.py:684
  30.4 0.0 copy-done.13
  30.4 0.0 copy-start.12
  30.4 0.1 fusion.posw_ref
  30.5 0.0 copy-done
  30.5 0.0 copy-done.1
  30.5 0.0 copy-done.6
  30.5 0.0 copy-done.8
  30.5 0.0 copy-done.10
  30.5 18.3 %pair_layer.1 = (f32[14,160,128]{2,1,0:T(8,128)S(1)}, f32[4,14,4,80]{3,2,1,0:T(4,128)S(1)}, f32[256,128]{1,0:T(8,128)S(1)}) custom-call(bf16[14,160,128]{2,1,0:T(8,128)(2,1)S(1)} %get-tuple-element.14.layer_ref, f32[4,14,4,80]{3,2,1,0:T(4,128)S(1)} %fusion.posw_ref, bf16[320,160]{1,0:T(8,128)(2,1)S(1)} %copy-done, bf16[160,320]{1,0:T(8,128)(2,1)S(1)} %copy-done.1, ...), custom_call_target="tpu_custom_call" | custom-call | tf_op jit(solution)/shard_map/pair_layer/pallas_call | solution.py:700
  48.9 0.1 reshape.75
  49.0 0.0 copy-done.12
  49.1 0.6 fusion.4
  49.7 0.6 copy.41
  50.2 0.2 reshape.64
  50.5 0.1 reshape.61
  50.6 0.1 fusion.2
  50.7 0.1 pad_maximum_fusion
  50.8 0.0 copy-start.3
  50.8 0.0 copy-start.5
  50.8 0.2 copy.40
  51.0 0.2 reshape.62.force_ref
  51.2 0.3 copy-done.3
  51.5 0.0 copy-done.5
  51.5 17.8 %halo_back.1 = (f32[2,128,128]{2,1,0:T(8,128)S(1)}, f32[2,2,1,64]{3,2,1,0:T(1,128)S(1)}, f32[2,2,1,3,64]{4,3,2,1,0:T(4,128)S(1)}) custom-call(bf16[2,128,128]{2,1,0:T(8,128)(2,1)S(1)} %get-tuple-element.13.place_ref, f32[14,160,128]{2,1,0:T(8,128)S(1)} %get-tuple-element.17.grad_ref, f32[3,3,3,8,128]{4,3,2,1,0:T(8,128)S(1)} %reshape.62.force_ref, ...), custom_call_target="tpu_custom_call" | custom-call | tf_op jit(solution)/shard_map/halo_back/pallas_call | solution.py:752
  69.3 0.6 copy.43
  69.9 0.6 copy.55
  70.5 0.7 copy.56
  (9 shorter events, 0.1 us)
Async XLA Ops:
  3.6 0.7 %copy-start.2 = (bf16[64,96]{1,0:T(8,128)(2,1)S(1)}, bf16[64,96]{1,0:T(8,128)(2,1)}, u32[]{:S(2)}) copy-start(bf16[64,96]{1,0:T(8,128)(2,1)} %constant.20.clone.ysel_ref) | copy-start | bytes 36868
  4.3 0.7 %copy-start.4 = (bf16[64,32]{1,0:T(8,128)(2,1)S(1)}, bf16[64,32]{1,0:T(8,128)(2,1)}, u32[]{:S(2)}) copy-start(bf16[64,32]{1,0:T(8,128)(2,1)} %constant.19.clone.zsel_ref) | copy-start | bytes 12292
  5.1 0.8 %copy-start.7 = (bf16[2,2,1,64,128]{4,3,2,1,0:T(8,128)(2,1)S(1)}, bf16[2,2,1,64,128]{4,3,2,1,0:T(8,128)(2,1)}, u32[]{:S(2)}) copy-start(bf16[2,2,1,64,128]{4,3,2,1,0:T(8,128)(2,1)} %param.20) | copy-start | bytes 196612
  5.9 0.7 copy-start.9
  28.4 1.0 %copy-start.11 = (f32[4,80,288,1]{2,1,0,3:T(8,128)S(1)}, f32[4,80,288,1]{2,1,0,3:T(8,128)}, u32[]{:S(2)}) copy-start(f32[4,80,288,1]{2,1,0,3:T(8,128)} %constant.43) | copy-start | bytes 1105924
  28.4 2.0 %copy-start.13 = (f32[14,4,4,80]{3,1,0,2:T(4,128)S(1)}, f32[14,4,4,80]{3,1,0,2:T(4,128)}, u32[]{:S(2)}) copy-start(f32[14,4,4,80]{3,1,0,2:T(4,128)} %constant.39) | copy-start | bytes 215044
  28.7 1.8 %copy-start = (bf16[320,160]{1,0:T(8,128)(2,1)S(1)}, bf16[320,160]{1,0:T(8,128)(2,1)}, u32[]{:S(2)}) copy-start(bf16[320,160]{1,0:T(8,128)(2,1)} %constant.24.clone.pick_ref) | copy-start | bytes 307204
  28.7 1.8 %copy-start.1 = (bf16[160,320]{1,0:T(8,128)(2,1)S(1)}, bf16[160,320]{1,0:T(8,128)(2,1)}, u32[]{:S(2)}) copy-start(bf16[160,320]{1,0:T(8,128)(2,1)} %constant.25.clone.pick_t_ref) | copy-start | bytes 307204
  28.7 1.8 %copy-start.6 = (f32[128,128]{1,0:T(8,128)S(1)}, f32[128,128]{1,0:T(8,128)}, u32[]{:S(2)}) copy-start(f32[128,128]{1,0:T(8,128)} %mixing_ref.1) | copy-start | bytes 196612
  28.8 1.8 %copy-start.8 = (f32[2,8,128]{2,1,0:T(8,128)S(1)}, f32[2,8,128]{2,1,0:T(8,128)}, u32[]{:S(2)}) copy-start(f32[2,8,128]{2,1,0:T(8,128)} %radial_ref.1) | copy-start | bytes 24580
  28.8 1.8 %copy-start.10 = (f32[16]{0:T(128)S(1)}, f32[16]{0:T(128)}, u32[]{:S(2)}) copy-start(f32[16]{0:T(128)} %param.25) | copy-start | bytes 196
  30.4 18.7 %copy-start.12 = (f32[320,288,1]{0,1,2:T(8,128)S(1)}, f32[320,288,1]{0,1,2:T(8,128)}, u32[]{:S(2)}) copy-start(f32[320,288,1]{0,1,2:T(8,128)} %constant.44) | copy-start | bytes 1105924
  50.8 0.7 %copy-start.3 = (bf16[64,96]{1,0:T(8,128)(2,1)S(1)}, bf16[64,96]{1,0:T(8,128)(2,1)}, u32[]{:S(2)}) copy-start(bf16[64,96]{1,0:T(8,128)(2,1)} %constant.20.clone.ysel_ref) | copy-start | bytes 36868
  50.8 0.7 %copy-start.5 = (bf16[64,32]{1,0:T(8,128)(2,1)S(1)}, bf16[64,32]{1,0:T(8,128)(2,1)}, u32[]{:S(2)}) copy-start(bf16[64,32]{1,0:T(8,128)(2,1)} %constant.19.clone.zsel_ref) | copy-start | bytes 12292

commit v4 on v1

v4 whole, which is shorter than its diff:
```python
import functools
import math

import jax
import jax.numpy as jnp
import numpy as np
from jax import lax
from jax.experimental import pallas as pl
from jax.experimental.pallas import tpu as pltpu
from jax.sharding import PartitionSpec as P

SIDE = 7.0
CUTOFF = 5.0
JITTER = 0.3
BLOCK = 2
HIGH = lax.Precision.HIGHEST


def lattice_of(capacity):
    lat = round(capacity ** (1.0 / 3.0))
    spacing = SIDE / lat
    reach = 0
    while (reach + 1 - 2 * JITTER) * spacing < CUTOFF:
        reach += 1
    return lat, spacing, reach


def pair_fields(pj, pi):
    dx = pj[0:1, :] - pi[:, 0:1]
    dy = pj[1:2, :] - pi[:, 1:2]
    dz = pj[2:3, :] - pi[:, 2:3]
    sq = dx * dx + dy * dy + dz * dz
    near = jnp.logical_and(sq < CUTOFF * CUTOFF, sq > 0.01)
    weight = jnp.where(near, pj[3:4, :] * pi[:, 3:4], 0.0)
    safe = jnp.where(near, sq, 1.0)
    inv = lax.rsqrt(safe)
    r = safe * inv
    u = r * (1.0 / CUTOFF)
    u2 = u * u
    u5 = u2 * u2 * u
    env = 1.0 + u5 * u * (-28.0 + u * (48.0 - 21.0 * u))
    denv = u5 * (-168.0 + u * (336.0 - 168.0 * u)) * (1.0 / CUTOFF)
    amp = weight * inv * math.sqrt(2.0 / CUTOFF)
    q = amp * env
    p = amp * denv - q * inv
    t = u * math.pi - 0.5 * math.pi
    t2 = t * t
    cos_t = 1.0 + t2 * (
        -1.0 / 2 + t2 * (1.0 / 24 + t2 * (-1.0 / 720 + t2 * (1.0 / 40320 + t2 * (-1.0 / 3628800 + t2 * (1.0 / 479001600)))))
    )
    sin_t = t * (
        1.0 + t2 * (-1.0 / 6 + t2 * (1.0 / 120 + t2 * (-1.0 / 5040 + t2 * (1.0 / 362880 + t2 * (-1.0 / 39916800)))))
    )
    return dx * inv, dy * inv, dz * inv, inv, q, p, cos_t, -sin_t


def compute_kernel(
    dims,
    layer_ref,
    tile_ref,
    small_ref,
    pick_hbm,
    pick_t_hbm,
    spot_hbm,
    shift_hbm,
    turn_hbm,
    origin_hbm,
    radial_hbm,
    coupling_hbm,
    mixing_hbm,
    hw_hbm,
    ow_hbm,
    gsend_ref,
    gown_ref,
    force_ref,
    out_ref,
    pick_ref,
    pick_t_ref,
    spot_ref,
    shift_ref,
    turn_ref,
    origin_ref,
    radial_ref,
    coupling_ref,
    mixing_ref,
    hw_ref,
    ow_ref,
    rpos_ref,
    wsum_ref,
    node_ref,
    posj_ref,
    fj_ref,
    slab_ref,
    even_ref,
    odd_ref,
    field_ref,
    sv_ref,
    en_ref,
    acc_ref,
    geven_ref,
    godd_ref,
    load_sem,
):
    sx, sy, sz, reach, nb, lat = dims
    nbx, nby = sx // BLOCK, sy // BLOCK
    wide = BLOCK + 2 * reach
    depth = sz + 2 * reach
    rows = wide * depth
    near = wide * rows
    own = BLOCK * BLOCK * sz
    px = sx + 2 * reach
    cx = sx // lat
    o = sy * sz
    chunks = [(c, min(128, near - c)) for c in range(0, near, 128)]
    root3 = math.sqrt(3.0)

    loads = [
        pltpu.make_async_copy(source, target, load_sem.at[n])
        for n, (source, target) in enumerate(
            [
                (pick_hbm, pick_ref),
                (spot_hbm, spot_ref),
                (shift_hbm, shift_ref),
                (turn_hbm, turn_ref),
                (origin_hbm, origin_ref),
                (radial_hbm, radial_ref),
                (coupling_hbm, coupling_ref),
                (mixing_hbm, mixing_ref),
                (hw_hbm, hw_ref),
                (ow_hbm, ow_ref),
                (pick_t_hbm, pick_t_ref),
            ]
        )
    ]
    for load in loads:
        load.start()
    wsum_ref[...] = jnp.zeros(wsum_ref.shape, jnp.float32)
    fj_ref[...] = jnp.zeros(fj_ref.shape, jnp.float32)
    force_ref[...] = jnp.zeros(force_ref.shape, jnp.float32)
    for load in loads:
        load.wait()

    for x in range(px):
        full = jnp.dot(pick_ref[...], layer_ref[x], preferred_element_type=jnp.float32)
        full = full.astype(jnp.bfloat16)
        for by in range(nby):
            slab_ref[by, x] = full[by * rows : (by + 1) * rows]
            acc_ref[by, x] = jnp.zeros((rows, full.shape[1]), jnp.float32)

    def layer_spot(x):
        at = x - reach
        side = 1 if at < 0 else 2 if at >= sx else 0
        at = at % sx
        return side, at // lat, slice((at % lat) * o, (at % lat + 1) * o)

    spot = spot_ref[...].astype(jnp.float32)
    lines = []
    for x in range(px):
        side, cell, lanes = layer_spot(x)
        lines.append(
            jnp.concatenate(
                [tile_ref[side, n // 3, n % 3, cell][:, lanes] for n in range(9)], axis=1
            )
        )
    columns = (
        jnp.dot(
            jnp.concatenate(lines, axis=0), spot, precision=HIGH, preferred_element_type=jnp.float32
        )
        + shift_ref[...]
    )
    for by in range(nby):
        for bx in range(nbx):
            for k in range(wide):
                x = bx * BLOCK + k
                posj_ref[by * nbx + bx, :, k * rows : (k + 1) * rows] = columns[
                    x * 4 : x * 4 + 4, by * rows : (by + 1) * rows
                ]
    turn = turn_ref[...].astype(jnp.float32)
    mine = jnp.concatenate([small_ref[n].T for n in range(cx)], axis=0)
    mine = jnp.dot(turn, mine, precision=HIGH, preferred_element_type=jnp.float32) + origin_ref[...]
    rpos_ref[...] = mine.reshape(nbx * nby, own, mine.shape[1])

    blocks = nbx * nby
    half = blocks // 2

    def basis(blk, edge_ref, slot):
        pi = rpos_ref[blk]
        for c, w in chunks:
            pj = posj_ref[blk, :, c : c + w]
            nx, ny, nz, inv, q, p, s1, c1 = pair_fields(pj, pi)
            field_ref[blk, 0, :, c : c + w] = nx
            field_ref[blk, 1, :, c : c + w] = ny
            field_ref[blk, 2, :, c : c + w] = nz
            field_ref[blk, 3, :, c : c + w] = inv
            field_ref[blk, 4, :, c : c + w] = q
            field_ref[blk, 5, :, c : c + w] = p
            field_ref[blk, 6, :, c : c + w] = s1
            field_ref[blk, 7, :, c : c + w] = c1
            twice = 2.0 * c1
            before, now = jnp.zeros_like(s1), s1
            q3 = root3 * q
            qs = (q, q3 * nx, q3 * ny, q3 * nz)
            for b in range(nb):
                for m in range(4):
                    k = (b * 4 + m) * own
                    edge_ref[slot, k : k + own, c : c + w] = (qs[m] * now).astype(jnp.bfloat16)
                before, now = now, twice * now - before

    def gather(blk, edge_ref, slot):
        by, bx = blk // nbx, lax.rem(blk, nbx)
        slab = slab_ref[by, pl.ds(bx * BLOCK, wide)].reshape(near, -1)
        summed = jnp.dot(edge_ref[slot], slab, preferred_element_type=jnp.float32)
        for m in range(4):
            total = None
            for b in range(nb):
                k = (b * 4 + m) * own
                term = summed[k : k + own] * radial_ref[min(m, 1), b : b + 1, :]
                total = term if total is None else total + term
            sv_ref[m, pl.ds(blk * own, own)] = total

    def forward(i, carry):
        gather(2 * i, even_ref, i)
        basis(2 * i + 1, odd_ref, i)
        gather(2 * i + 1, odd_ref, i)
        basis(2 * i + 2, even_ref, i + 1)
        return carry

    basis(0, even_ref, 0)
    lax.fori_loop(0, half - 1, forward, 0)
    gather(blocks - 2, even_ref, half - 1)
    basis(blocks - 1, odd_ref, half - 1)
    gather(blocks - 1, odd_ref, half - 1)

    flat = rpos_ref[...].reshape(nbx * nby * own, -1)
    occ = flat[:, 3:4]
    kind = flat[:, 4:5]
    spec = lax.broadcasted_iota(jnp.int32, (flat.shape[0], coupling_ref.shape[0]), 1)
    onehot = (kind.astype(jnp.int32) == spec).astype(jnp.float32)
    wq = [
        jnp.dot(onehot, coupling_ref[:, n], precision=HIGH, preferred_element_type=jnp.float32)
        for n in range(3)
    ]
    scalar = sv_ref[0]
    length_sq = sv_ref[1] * sv_ref[1] + sv_ref[2] * sv_ref[2] + sv_ref[3] * sv_ref[3]
    product = wq[0] * scalar + wq[1] * scalar * scalar + wq[2] * length_sq
    fold = lax.dot_general(
        mixing_ref[...],
        hw_ref[...],
        (((1,), (1,)), ((), ())),
        precision=HIGH,
        preferred_element_type=jnp.float32,
    )
    hidden = jnp.dot(product, fold, precision=HIGH, preferred_element_type=jnp.float32)
    logistic = jax.nn.sigmoid(hidden)
    energy = occ * jnp.sum(ow_ref[...] * hidden * logistic, axis=1, keepdims=True)
    d_hidden = occ * ow_ref[...] * logistic * (1.0 + hidden * (1.0 - logistic))
    d_product = lax.dot_general(
        d_hidden, fold, (((1,), (1,)), ((), ())), precision=HIGH, preferred_element_type=jnp.float32
    )
    en_ref[...] = jnp.broadcast_to(energy, en_ref.shape)
    sv_ref[0] = d_product * (wq[0] + 2.0 * wq[1] * scalar)
    twice_d = 2.0 * wq[2] * d_product
    for m in range(1, 4):
        sv_ref[m] = twice_d * sv_ref[m]

    def scatter(blk, edge_ref, slot, g_ref):
        by, bx = blk // nbx, lax.rem(blk, nbx)
        parts = []
        for b in range(nb):
            for m in range(4):
                parts.append(
                    sv_ref[m, pl.ds(blk * own, own)] * radial_ref[min(m, 1), b : b + 1, :]
                )
        d_full = jnp.concatenate(parts, axis=0)
        d_half = d_full.astype(jnp.bfloat16)
        slab = slab_ref[by, pl.ds(bx * BLOCK, wide)].reshape(near, -1)
        g_ref[...] = lax.dot_general(
            d_half, slab, (((1,), (1,)), ((), ())), preferred_element_type=jnp.float32
        )
        d_turn = d_full.T.astype(jnp.bfloat16)
        turned = jnp.dot(d_turn, edge_ref[slot], preferred_element_type=jnp.float32)
        acc_ref[by, pl.ds(bx * BLOCK, wide)] += turned.T.reshape(wide, rows, -1)

    def forces(blk, g_ref):
        by, bx = blk // nbx, lax.rem(blk, nbx)
        total = [jnp.zeros((own, 1), jnp.float32) for _ in range(3)]
        for c, w in chunks:
            nx, ny, nz, inv, q, p, s1, c1 = (field_ref[blk, n, :, c : c + w] for n in range(8))
            twice = 2.0 * c1
            s_before, s_now = jnp.zeros_like(s1), s1
            c_before, c_now = jnp.ones_like(c1), c1
            s_sum = [None] * 4
            c_sum = [None] * 4
            for b in range(nb):
                scaled = (b + 1.0) * c_now
                for m in range(4):
                    k = (b * 4 + m) * own
                    g = g_ref[k : k + own, c : c + w]
                    s_sum[m] = g * s_now if b == 0 else s_sum[m] + g * s_now
                    c_sum[m] = g * scaled if b == 0 else c_sum[m] + g * scaled
                s_before, s_now = s_now, twice * s_now - s_before
                c_before, c_now = c_now, twice * c_now - c_before
            s_dot = nx * s_sum[1] + ny * s_sum[2] + nz * s_sum[3]
            c_dot = nx * c_sum[1] + ny * c_sum[2] + nz * c_sum[3]
            slope = (q * (math.pi / CUTOFF)) * (c_sum[0] + root3 * c_dot) + p * (
                s_sum[0] + root3 * s_dot
            )
            across = root3 * q * inv
            along = slope - across * s_dot
            outs = [
                along * n + across * s_sum[m + 1] for m, n in enumerate((nx, ny, nz))
            ]
            for m in range(3):
                fj_ref[m : m + 1, c : c + w] = -jnp.sum(outs[m], axis=0, keepdims=True)
                total[m] = total[m] + jnp.sum(outs[m], axis=1, keepdims=True)
        for k in range(wide):
            wsum_ref[by, bx * BLOCK + k] += fj_ref[:, k * rows : (k + 1) * rows]
        lane = lax.broadcasted_iota(jnp.int32, (own, node_ref.shape[1]), 1)
        here = pl.ds(blk * own, own)
        node_ref[here] = jnp.where(
            lane == 0,
            total[0],
            jnp.where(lane == 1, total[1], jnp.where(lane == 2, total[2], en_ref[here])),
        )

    def backward(i, carry):
        scatter(2 * i + 1, odd_ref, i, godd_ref)
        forces(2 * i, geven_ref)
        scatter(2 * i + 2, even_ref, i + 1, geven_ref)
        forces(2 * i + 1, godd_ref)
        return carry

    scatter(0, even_ref, 0, geven_ref)
    lax.fori_loop(0, half - 1, backward, 0)
    scatter(blocks - 1, odd_ref, half - 1, godd_ref)
    forces(blocks - 2, geven_ref)
    forces(blocks - 1, godd_ref)

    for x in range(px):
        stack = jnp.concatenate([acc_ref[by, x] for by in range(nby)], axis=0)
        top = stack.astype(jnp.bfloat16)
        rest = (stack - top.astype(jnp.float32)).astype(jnp.bfloat16)
        total = jnp.dot(pick_t_ref[...], top, preferred_element_type=jnp.float32) + jnp.dot(
            pick_t_ref[...], rest, preferred_element_type=jnp.float32
        )
        gsend_ref[x] = total.astype(jnp.bfloat16)
        if reach <= x < reach + sx:
            gown_ref[x - reach] = total[0:o]

    lines = jnp.concatenate(
        [jnp.concatenate([wsum_ref[by, x] for by in range(nby)], axis=1) for x in range(px)], axis=0
    )
    lines = lax.dot_general(
        lines, spot, (((1,), (1,)), ((), ())), precision=HIGH, preferred_element_type=jnp.float32
    )
    for x in range(px):
        side, cell, lanes = layer_spot(x)
        for n in range(9):
            force_ref[side, n // 3, n % 3, cell, :, lanes] = lines[
                x * 4 : x * 4 + 4, n * o : (n + 1) * o
            ]
    nodes = lax.dot_general(
        node_ref[...], turn, (((0,), (0,)), ((), ())), precision=HIGH, preferred_element_type=jnp.float32
    )
    for n in range(cx):
        out_ref[n] = nodes[0:4, n * lat * o : (n + 1) * lat * o]


def ring(axis):
    count = lax.axis_size(axis)
    me = lax.axis_index(axis)
    return lax.rem(me + count - 1, count), lax.rem(me + 1, count)


DIRECTIONS = [
    (a, b, c)
    for a in (-1, 1, 0)
    for b in (0, -1, 1)
    for c in (0, -1, 1)
    if (a, b, c) != (0, 0, 0)
]


def slot_of(step):
    return {0: 0, -1: 1, 1: 2}[step]


def partners():
    around = {axis: (lax.axis_index(axis),) + ring(axis) for axis in ("gx", "gy", "gz")}
    return {
        d: {axis: around[axis][slot_of(step)] for axis, step in zip(("gx", "gy", "gz"), d)}
        for d in DIRECTIONS
    }


def greet(around):
    barrier = pltpu.get_barrier_semaphore()
    for target in around.values():
        pl.semaphore_signal(
            barrier, inc=1, device_id=target, device_id_type=pl.DeviceIdType.MESH
        )
    return barrier


def sender(send_sem, recv_sem):
    def send(slot, source, target, device):
        copy = pltpu.make_async_remote_copy(
            src_ref=source,
            dst_ref=target,
            send_sem=send_sem.at[slot],
            recv_sem=recv_sem.at[slot],
            device_id=device,
            device_id_type=pl.DeviceIdType.MESH,
        )
        copy.start()
        return copy

    return send


def spread_kernel(
    dims,
    spacing,
    counts_ref,
    pos_hbm,
    kind_hbm,
    feat_hbm,
    faces_hbm,
    layer_ref,
    tile_ref,
    place_ref,
    small_ref,
    pos_ref,
    kind_ref,
    feat_ref,
    faces_ref,
    out_ref,
    load_sem,
    send_sem,
    recv_sem,
):
    sx, lat, reach, o, pieces = dims
    around = partners()
    loads = [
        pltpu.make_async_copy(source, target, load_sem.at[n])
        for n, (source, target) in enumerate(
            [(pos_hbm, pos_ref), (kind_hbm, kind_ref), (feat_hbm, feat_ref), (faces_hbm, faces_ref)]
        )
    ]
    for load in loads:
        load.start()
    barrier = greet(around)
    send = sender(send_sem, recv_sem)
    for load in loads:
        load.wait()
    cx, cy, _, cz, capacity = pos_ref.shape
    sy, sz = cy * lat, cz * lat
    slot = lax.broadcasted_iota(jnp.int32, (1, capacity), 1)
    for col in range(cx):
        parts, codes = [], []
        for cell_y in range(cy):
            for cell_z in range(cz):
                xyz = [pos_ref[col, cell_y, n, cell_z : cell_z + 1] for n in range(3)]
                site = [
                    jnp.clip(jnp.floor(v * (1.0 / spacing)), 0.0, lat - 1.0) for v in xyz
                ]
                codes.append((site[0] * sy + site[1] + cell_y * lat) * sz + site[2] + cell_z * lat)
                occ = (slot < counts_ref[col, cell_z, cell_y]).astype(jnp.float32)
                kind = kind_ref[col, cell_y, cell_z : cell_z + 1].astype(jnp.float32)
                parts.append(
                    jnp.concatenate(xyz + [occ, kind, jnp.zeros((3, capacity), jnp.float32)], axis=0)
                )
        code = jnp.concatenate(codes, axis=1)
        small = jnp.concatenate(parts, axis=1)
        count = code.shape[1]
        place = (
            code == lax.broadcasted_iota(jnp.int32, (count, count), 0).astype(jnp.float32)
        ).astype(jnp.float32)
        small = lax.dot_general(
            small, place, (((1,), (1,)), ((), ())), precision=HIGH, preferred_element_type=jnp.float32
        )
        small_ref[col] = small
        tile_ref[0, 0, 0, col] = small[0:4]
        place_ref[col] = place.astype(jnp.bfloat16)
        sites = jnp.dot(place_ref[col], feat_ref[col], preferred_element_type=jnp.float32)
        sites = sites.astype(jnp.bfloat16)
        for k in range(lat):
            x = col * lat + k
            mine = sites[k * o : (k + 1) * o]
            layer_ref[reach + x, 0:o] = mine
            out_ref[x, 0:o] = mine
            faces = jnp.dot(faces_ref[...], mine, preferred_element_type=jnp.float32)
            out_ref[x, o:] = faces.astype(jnp.bfloat16)
    pl.semaphore_wait(barrier, len(around))

    from_x = {-1: pl.ds(0, reach), 1: pl.ds(sx - reach, reach), 0: pl.ds(0, sx)}
    to_x = {-1: pl.ds(reach + sx, reach), 1: pl.ds(0, reach), 0: pl.ds(reach, sx)}
    cell = {-1: pl.ds(0, 1), 1: pl.ds(cx - 1, 1), 0: pl.ds(0, cx)}
    copies = []
    for n, (a, b, c) in enumerate(DIRECTIONS):
        start, size = pieces[(b, c)]
        copies.append(
            send(
                2 * n,
                out_ref.at[from_x[a], pl.ds(start, size)],
                layer_ref.at[to_x[a], pl.ds(pieces[(-b, -c)][0], size)],
                around[(a, b, c)],
            )
        )
        copies.append(
            send(
                2 * n + 1,
                tile_ref.at[0, 0, 0, cell[a]],
                tile_ref.at[slot_of(-a), slot_of(-b), slot_of(-c), cell[a]],
                around[(a, b, c)],
            )
        )
    for copy in copies:
        copy.wait_recv()
    for copy in copies:
        copy.wait_send()


def gather_kernel(
    dims,
    place_ref,
    gsend_ref,
    gown_ref,
    force_ref,
    node_ref,
    faces_ref,
    out_ref,
    energy_ref,
    xyz_ref,
    inner_ref,
    outer_ref,
    back_ref,
    send_sem,
    recv_sem,
):
    sx, lat, reach, o, pieces = dims
    cx = sx // lat
    around = partners()
    back_ref[...] = jnp.zeros(back_ref.shape, jnp.float32)
    barrier = greet(around)
    send = sender(send_sem, recv_sem)
    pl.semaphore_wait(barrier, len(around))

    from_x = {-1: pl.ds(0, reach), 1: pl.ds(reach + sx, reach), 0: pl.ds(reach, sx)}
    cell = {-1: pl.ds(cx - 1, 1), 1: pl.ds(0, 1), 0: pl.ds(0, cx)}
    copies = []
    for n, (a, b, c) in enumerate(DIRECTIONS):
        start, size = pieces[(b, c)]
        rows = pl.ds(pieces[(-b, -c)][0], size)
        into = inner_ref.at[:, rows] if a == 0 else outer_ref.at[slot_of(-a) - 1, :, rows]
        copies.append(
            send(2 * n, gsend_ref.at[from_x[a], pl.ds(start, size)], into, around[(a, b, c)])
        )
        copies.append(
            send(
                2 * n + 1,
                force_ref.at[slot_of(a), slot_of(b), slot_of(c), cell[a]],
                back_ref.at[slot_of(-a), slot_of(-b), slot_of(-c), cell[a]],
                around[(a, b, c)],
            )
        )
    for copy in copies:
        copy.wait_recv()

    tile = node_ref[...] + force_ref[0, 0, 0]
    for a, b, c in DIRECTIONS:
        tile = tile + back_ref[slot_of(a), slot_of(b), slot_of(c)]

    def spread(received):
        return lax.dot_general(
            faces_ref[...], received, (((0,), (0,)), ((), ())), preferred_element_type=jnp.float32
        )

    _, cy, _, cz, capacity = xyz_ref.shape
    for col in range(cx):
        sites = []
        for k in range(lat):
            x = col * lat + k
            total = gown_ref[x] + spread(inner_ref[x, o:])
            for side, at in ((0, x), (1, x - (sx - reach))):
                if 0 <= at < reach:
                    total = total + outer_ref[side, at, 0:o].astype(jnp.float32)
                    total = total + spread(outer_ref[side, at, o:])
            sites.append(total)
        whole = jnp.concatenate(sites, axis=0)
        top = whole.astype(jnp.bfloat16)
        rest = (whole - top.astype(jnp.float32)).astype(jnp.bfloat16)
        place = place_ref[col].astype(jnp.float32)
        turn = place.T.astype(jnp.bfloat16)
        out_ref[col] = jnp.dot(turn, top, preferred_element_type=jnp.float32) + jnp.dot(
            turn, rest, preferred_element_type=jnp.float32
        )
        slots = jnp.dot(tile[col], place, precision=HIGH, preferred_element_type=jnp.float32)
        for n in range(cy * cz):
            lanes = slice(n * capacity, (n + 1) * capacity)
            for m in range(3):
                xyz_ref[col, n // cz, m, n % cz : n % cz + 1] = slots[m : m + 1, lanes]
            energy_ref[col, n // cz, n % cz : n % cz + 1] = slots[3:4, lanes]
    for copy in copies:
        copy.wait_send()


def tables(sx, sy, sz, reach, lat):
    px, py, depth = sx + 2 * reach, sy + 2 * reach, sz + 2 * reach
    wide, nbx, nby = BLOCK + 2 * reach, sx // BLOCK, sy // BLOCK
    o = sy * sz
    extent = {0: (sy, sz), -1: (reach, reach), 1: (reach, reach)}
    pieces, total = {}, 0
    for b in (0, -1, 1):
        for c in (0, -1, 1):
            size = extent[b][0] * extent[c][1]
            pieces[(b, c)] = (total, -(-size // 16) * 16)
            total += pieces[(b, c)][1]

    def spot(n, size):
        if n < reach:
            return -1, n
        if n >= reach + size:
            return 1, n - reach - size
        return 0, n - reach

    pick = np.zeros((nby, wide, depth, total), np.float32)
    pick_pos = np.zeros((9 * o, nby, wide, depth), np.float32)
    for by in range(nby):
        for y in range(wide):
            for z in range(depth):
                b, at_y = spot(by * BLOCK + y, sy)
                c, at_z = spot(z, sz)
                pick[by, y, z, pieces[(b, c)][0] + at_y * extent[c][1] + at_z] = 1
                tile_y = sy - reach + at_y if b < 0 else at_y
                tile_z = sz - reach + at_z if c < 0 else at_z
                line = (slot_of(b) * 3 + slot_of(c)) * o + tile_y * sz + tile_z
                pick_pos[line, by, y, z] = 1
    faces = np.zeros((total - o, o), np.float32)
    for (b, c), (start, _) in pieces.items():
        if (b, c) == (0, 0):
            continue
        for y in range(extent[b][0]):
            for z in range(extent[c][1]):
                from_y = sy - reach + y if b > 0 else y
                from_z = sz - reach + z if c > 0 else z
                faces[start - o + y * extent[c][1] + z, from_y * sz + from_z] = 1
    steps = [np.floor((np.arange(n) - reach) / lat).astype(np.float32) * SIDE for n in (px, py, depth)]
    shifts = np.zeros((px, 4, py, depth), np.float32)
    shifts[:, 0] = steps[0][:, None, None]
    shifts[:, 1] = steps[1][None, :, None]
    shifts[:, 2] = steps[2][None, None, :]
    shift = np.stack([shifts[:, :, by * BLOCK : by * BLOCK + wide] for by in range(nby)], axis=2)
    count = sx * sy * sz
    index = np.arange(count).reshape(nbx, BLOCK, nby, BLOCK, sz).transpose(2, 0, 1, 3, 4).reshape(-1)
    turn = np.zeros((count, count), np.float32)
    turn[np.arange(count), index] = 1
    inner = shifts[reach : reach + sx, :, reach : reach + sy, reach : reach + sz]
    origin = np.zeros((count, 8), np.float32)
    origin[:, :4] = inner.transpose(0, 2, 3, 1).reshape(count, 4)[index]
    return (
        pieces,
        total,
        pick.reshape(-1, total),
        pick_pos.reshape(9 * o, -1),
        faces,
        shift.reshape(px * 4, -1),
        turn,
        origin,
    )


def body(
    local_pos,
    counts,
    species,
    features,
    radial_weights,
    coupling,
    mixing,
    hidden_weights,
    output_weights,
):
    cx, cy, cz = counts.shape
    capacity, channels = features.shape[3:]
    nb = radial_weights.shape[1]
    lat, spacing, reach = lattice_of(capacity)
    sx, sy, sz = cx * lat, cy * lat, cz * lat
    nbx, nby = sx // BLOCK, sy // BLOCK
    wide, depth = BLOCK + 2 * reach, sz + 2 * reach
    near, own = wide * wide * depth, BLOCK * BLOCK * sz
    px = sx + 2 * reach
    rows = wide * depth
    blocks = nbx * nby
    o = sy * sz
    pieces, total, pick, pick_pos, faces, shift, turn, origin = tables(sx, sy, sz, reach, lat)
    column = cy * cz * capacity
    total_own = sx * sy * sz
    f32, half = jnp.float32, jnp.bfloat16

    vmem = pl.BlockSpec(memory_space=pltpu.VMEM)
    hbm = pl.BlockSpec(memory_space=pl.ANY)
    dims = (sx, lat, reach, o, pieces)
    limit = 50 * 1024 * 1024
    ways = 2 * len(DIRECTIONS)
    faces = jnp.asarray(faces, half)
    local_turned = local_pos.transpose(0, 1, 3, 2, 4)
    feat_flat = features.reshape(cx, column, channels)
    tile_shape = (3, 3, 3, cx, 4, lat * o)
    layers, tiles, place, small_sites = pl.pallas_call(
        functools.partial(spread_kernel, dims, spacing),
        out_shape=(
            jax.ShapeDtypeStruct((px, total, channels), half),
            jax.ShapeDtypeStruct(tile_shape, f32),
            jax.ShapeDtypeStruct((cx, column, column), half),
            jax.ShapeDtypeStruct((cx, 8, column), f32),
        ),
        in_specs=[pl.BlockSpec(memory_space=pltpu.SMEM)] + [hbm] * 4,
        out_specs=(vmem,) * 4,
        scratch_shapes=[
            pltpu.VMEM(local_turned.shape, f32),
            pltpu.VMEM(species.shape, jnp.int32),
            pltpu.VMEM(feat_flat.shape, half),
            pltpu.VMEM(faces.shape, half),
            pltpu.VMEM((sx, total, channels), half),
            pltpu.SemaphoreType.DMA((4,)),
            pltpu.SemaphoreType.DMA((ways,)),
            pltpu.SemaphoreType.DMA((ways,)),
        ],
        compiler_params=pltpu.CompilerParams(
            collective_id=0, has_side_effects=True, vmem_limit_bytes=limit
        ),
        name="halo_out",
    )(counts.transpose(0, 2, 1), local_turned, species, feat_flat, faces)

    fixed = [
        jnp.asarray(pick, half),
        jnp.asarray(pick.T, half),
        jnp.asarray(pick_pos, half),
        jnp.asarray(shift),
        jnp.asarray(turn, half),
        jnp.asarray(origin),
        radial_weights,
        coupling.transpose(1, 0, 2),
        mixing,
        hidden_weights.T,
        output_weights[None, :],
    ]
    gsend, gown, force, node = pl.pallas_call(
        functools.partial(compute_kernel, (sx, sy, sz, reach, nb, lat)),
        out_shape=(
            jax.ShapeDtypeStruct((px, total, channels), half),
            jax.ShapeDtypeStruct((sx, o, channels), f32),
            jax.ShapeDtypeStruct(tile_shape, f32),
            jax.ShapeDtypeStruct((cx, 4, lat * o), f32),
        ),
        in_specs=[vmem] * 3 + [hbm] * len(fixed),
        out_specs=(vmem,) * 4,
        scratch_shapes=[pltpu.VMEM(item.shape, item.dtype) for item in fixed]
        + [
            pltpu.VMEM((blocks, own, 8), f32),
            pltpu.VMEM((nby, px, 4, rows), f32),
            pltpu.VMEM((total_own, 128), f32),
            pltpu.VMEM((blocks, 4, near), f32),
            pltpu.VMEM((4, near), f32),
            pltpu.VMEM((nby, px, rows, channels), half),
            pltpu.VMEM((blocks // 2, nb * 4 * own, near), half),
            pltpu.VMEM((blocks // 2, nb * 4 * own, near), half),
            pltpu.VMEM((blocks, 8, own, near), f32),
            pltpu.VMEM((4, total_own, channels), f32),
            pltpu.VMEM((total_own, 128), f32),
            pltpu.VMEM((nby, px, rows, channels), f32),
            pltpu.VMEM((nb * 4 * own, near), f32),
            pltpu.VMEM((nb * 4 * own, near), f32),
            pltpu.SemaphoreType.DMA((len(fixed),)),
        ],
        compiler_params=pltpu.CompilerParams(vmem_limit_bytes=limit),
        name="pair_layer",
    )(layers, tiles, small_sites, *fixed)

    grad, energy, forces = pl.pallas_call(
        functools.partial(gather_kernel, dims),
        out_shape=(
            jax.ShapeDtypeStruct((cx, column, channels), f32),
            jax.ShapeDtypeStruct((cx, cy, cz, capacity), f32),
            jax.ShapeDtypeStruct((cx, cy, 3, cz, capacity), f32),
        ),
        in_specs=[vmem] * 6,
        out_specs=(vmem, vmem, vmem),
        scratch_shapes=[
            pltpu.VMEM((sx, total, channels), half),
            pltpu.VMEM((2, reach, total, channels), half),
            pltpu.VMEM(tile_shape, f32),
            pltpu.SemaphoreType.DMA((ways,)),
            pltpu.SemaphoreType.DMA((ways,)),
        ],
        compiler_params=pltpu.CompilerParams(
            collective_id=1, has_side_effects=True, vmem_limit_bytes=limit
        ),
        name="halo_back",
    )(place, gsend, gown, force, node, faces)
    return (
        energy,
        forces.transpose(0, 1, 3, 2, 4),
        grad.reshape(cx, cy, cz, capacity, channels),
    )


def solution(mesh):
    placed = (
        P("gx", "gy", "gz", None, None),
        P("gx", "gy", "gz"),
        P("gx", "gy", "gz", None),
        P("gx", "gy", "gz", None, None),
        P(),
        P(),
        P(),
        P(),
        P(),
    )
    return jax.shard_map(
        body,
        mesh=mesh,
        in_specs=placed,
        out_specs=(
            P("gx", "gy", "gz", None),
            P("gx", "gy", "gz", None, None),
            P("gx", "gy", "gz", None, None),
        ),
        check_vma=False,
    )
```

time: 105 us -> 71.8 us (0.68)
  Pallas kernels: 21.3 us -> 60.5 us
  starting transfers between devices: 32.3 us -> 0 us
  waiting for transfers between devices: 29.4 us -> 0 us
  local copies, waits for them, and re-layouts: 15 us -> 10.2 us
  other arithmetic: 3.84 us -> 0 us
  matrix products: 1.71 us -> 0 us
    pallas_call x1 -> x3, Pallas kernels: 21.3 us -> 60.5 us  [the longest x1 21.2 us: body(): pl.pallas_call(functools.partial(compute_kernel, (sx, sy, sz, reach, nb,...]
    ppermute x24 -> x0, starting transfers between devices: 32.3 us -> none  [shift(): return lax.ppermute(block, axis, pairs)]
    ppermute x24 -> x0, waiting for transfers between devices: 29.4 us -> none  [shift(): return lax.ppermute(block, axis, pairs)]
    unnamed x36 -> x37, local copies, waits for them, and re-layouts: 2.78 us -> 10.2 us
    slice x31 -> x0, local copies, waits for them, and re-layouts: 6.32 us -> none  [the longest x17 4.77 us: body(): pos_pad[:, bx * BLOCK:bx * BLOCK + wide, by * BLOCK:by * BLOCK + wide]]
    reshape x5 -> x0, local copies, waits for them, and re-layouts: 3.09 us -> none  [the longest x1 1.64 us: body(): fj = fj.reshape(nby, nbx, 3, wide, wide, depth)]
    another operation x18 -> x0, local copies, waits for them, and re-layouts: 2.44 us -> none  [the longest x17 2.28 us: body(): jnp.stack([pos_pad[:, bx * BLOCK:bx * BLOCK + wide, by * BLOCK:by * BLOCK...]
    dot_general x4 -> x0, matrix products: 1.71 us -> none  [the longest x1 0.92 us: body(): jnp.einsum('xyzts,xyztc->xyzsc', place_full, to_cells(grad), precision=HIGH)]
  transfers between devices with their start and end apart: 24 -> 0, of which waited for: 14 -> 0; matrix products, arithmetic and copies ran while one was open for 11% -> 0% of each run, Pallas kernels for 0% -> 0%
where the time goes in v4:
time: 71.8 us; the launch traced here: 71.4 us
  Pallas kernels  60.5 us (84%)
  local copies, waits for them, and re-layouts  10.2 us (14%)
  between operations  0.74 us (1%)
    pallas_call x1, Pallas kernels, body(): pl.pallas_call(functools.partial(compute_kernel, (sx, sy, sz, reach, nb,...  21.2 us
    pallas_call x1, Pallas kernels, body(): pl.pallas_call(functools.partial(spread_kernel, dims, spacing), out_shape...  20.8 us
    pallas_call x1, Pallas kernels, body(): pl.pallas_call(functools.partial(gather_kernel, dims), out_shape=(jax.Sha...  18.5 us
    unnamed x37, local copies, waits for them, and re-layouts  10.2 us

profile of v4, /device:TPU:0, one launch (start us, length us, event | category | flops | bytes accessed | tf_op | source)
XLA Modules:
  0.0 71.4 jit_solution(12469984146166879395)
XLA Ops:
  0.6 0.0 copy-start.13
  0.6 0.0 copy-start.14
  0.7 0.0 copy-start.15
  0.7 0.7 copy-done.13
  1.3 0.0 copy-done.14
  1.3 0.0 copy-done.15
  1.3 0.0 copy-start.1
  1.3 0.8 %copy-done.1 = bf16[160,32]{1,0:T(8,128)(2,1)S(1)} copy-done((bf16[160,32]{1,0:T(8,128)(2,1)S(1)}, bf16[160,32]{1,0:T(8,128)(2,1)}, u32[]{:S(2)}) %copy-start.1) | copy-done | bytes 10264
  2.1 0.0 copy-start.8
  2.1 0.8 %copy-done.8 = bf16[2,2,1,64,128]{4,3,2,1,0:T(8,128)(2,1)S(1)} copy-done((bf16[2,2,1,64,128]{4,3,2,1,0:T(8,128)(2,1)S(1)}, bf16[2,2,1,64,128]{4,3,2,1,0:T(8,128)(2,1)}, u32[]{:S(2)}) %copy-start.8) | copy-done | bytes 65560
  3.0 0.0 copy-start.7
  3.0 0.0 copy-start.10
  3.0 0.0 copy-start.11
  3.0 0.0 copy-start.12
  3.0 20.8 %halo_out.1 = (bf16[14,192,128]{2,1,0:T(8,128)(2,1)S(1)}, f32[3,3,3,2,4,128]{5,4,3,2,1,0:T(4,128)S(1)}, bf16[2,128,128]{2,1,0:T(8,128)(2,1)S(1)}, f32[2,8,128]{2,1,0:T(8,128)S(1)}) custom-call(s32[2,1,2]{2,1,0:T(1,128)S(1)} %bitcast.18, f32[2,2,3,1,64]{4,3,2,1,0:T(1,128)S(1)} %bitcast.16, s32[2,2,1,64]{3,2,1,0:T(1,128)S(1)} %copy-done.14, ...), custom_call_target="tpu_custom_call" | custom-call | tf_op jit(solution)/shard_map/halo_out/pallas_call | solution.py:710
  23.7 0.0 copy-start.16
  23.8 0.0 copy-done.7
  23.8 0.0 copy-done.10
  23.8 0.0 copy-done.11
  23.8 0.0 copy-done.12
  23.8 0.6 copy-done.16
  24.4 0.0 copy-start
  24.4 0.9 %copy-done = bf16[288,320]{1,0:T(8,128)(2,1)S(1)} copy-done((bf16[288,320]{1,0:T(8,128)(2,1)S(1)}, bf16[288,320]{1,0:T(8,128)(2,1)}, u32[]{:S(2)}) %copy-start) | copy-done | bytes 184344
  25.3 0.0 copy-start.3
  25.3 0.9 %copy-done.3 = bf16[320,192]{1,0:T(8,128)(2,1)S(1)} copy-done((bf16[320,192]{1,0:T(8,128)(2,1)S(1)}, bf16[320,192]{1,0:T(8,128)(2,1)}, u32[]{:S(2)}) %copy-start.3) | copy-done | bytes 122904
  26.2 0.0 copy-start.4
  26.3 0.9 %copy-done.4 = bf16[192,320]{1,0:T(8,128)(2,1)S(1)} copy-done((bf16[192,320]{1,0:T(8,128)(2,1)S(1)}, bf16[192,320]{1,0:T(8,128)(2,1)}, u32[]{:S(2)}) %copy-start.4) | copy-done | bytes 122904
  27.2 0.0 copy-start.5
  27.2 0.9 %copy-done.5 = f32[256,8]{1,0:T(8,128)S(1)} copy-done((f32[256,8]{1,0:T(8,128)S(1)}, f32[256,8]{1,0:T(8,128)}, u32[]{:S(2)}) %copy-start.5) | copy-done | bytes 8216
  28.1 0.0 copy-start.6
  28.1 0.9 %copy-done.6 = bf16[256,256]{1,0:T(8,128)(2,1)S(1)} copy-done((bf16[256,256]{1,0:T(8,128)(2,1)S(1)}, bf16[256,256]{1,0:T(8,128)(2,1)}, u32[]{:S(2)}) %copy-start.6) | copy-done | bytes 131096
  29.0 0.0 copy-start.9
  29.0 0.8 %copy-done.9 = f32[128,128]{1,0:T(8,128)S(1)} copy-done((f32[128,128]{1,0:T(8,128)S(1)}, f32[128,128]{1,0:T(8,128)}, u32[]{:S(2)}) %copy-start.9) | copy-done | bytes 65560
  29.8 0.0 copy-start.2
  29.8 21.2 %pair_layer.1 = (bf16[14,192,128]{2,1,0:T(8,128)(2,1)S(1)}, f32[8,32,128]{2,1,0:T(8,128)S(1)}, f32[3,3,3,2,4,128]{5,4,3,2,1,0:T(4,128)S(1)}, f32[2,4,128]{2,1,0:T(4,128)S(1)}) custom-call(bf16[14,192,128]{2,1,0:T(8,128)(2,1)S(1)} %get-tuple-element.15.layer_ref, f32[3,3,3,2,4,128]{5,4,3,2,1,0:T(4,128)S(1)} %get-tuple-element.16.tile_ref, ...), custom_call_target="tpu_custom_call" | custom-call | tf_op jit(solution)/shard_map/pair_layer/pallas_call | solution.py:749
  51.0 0.0 copy-done.2
  51.0 18.5 %halo_back.1 = (f32[2,128,128]{2,1,0:T(8,128)S(1)}, f32[2,2,1,64]{3,2,1,0:T(1,128)S(1)}, f32[2,2,3,1,64]{4,3,2,1,0:T(1,128)S(1)}) custom-call(bf16[2,128,128]{2,1,0:T(8,128)(2,1)S(1)} %get-tuple-element.14.place_ref, bf16[14,192,128]{2,1,0:T(8,128)(2,1)S(1)} %get-tuple-element.18.gsend_ref, f32[8,32,128]{2,1,0:T(8,128)S(1)} %get-tuple-element.19.gown_ref, ...), custom_call_target="tpu_custom_call" | custom-call | tf_op jit(solution)/shard_map/halo_back/pallas_call | solution.py:781
  69.6 0.6 copy.24
  70.1 0.6 copy.25
  70.7 0.7 copy.26
Async XLA Ops:
  0.6 0.7 copy-start.13
  0.6 0.7 copy-start.14
  0.7 0.7 copy-start.15
  1.3 0.8 %copy-start.1 = (bf16[160,32]{1,0:T(8,128)(2,1)S(1)}, bf16[160,32]{1,0:T(8,128)(2,1)}, u32[]{:S(2)}) copy-start(bf16[160,32]{1,0:T(8,128)(2,1)} %constant.14.clone.faces_hbm.faces_ref) | copy-start | bytes 30724
  2.1 0.8 %copy-start.8 = (bf16[2,2,1,64,128]{4,3,2,1,0:T(8,128)(2,1)S(1)}, bf16[2,2,1,64,128]{4,3,2,1,0:T(8,128)(2,1)}, u32[]{:S(2)}) copy-start(bf16[2,2,1,64,128]{4,3,2,1,0:T(8,128)(2,1)} %param.19) | copy-start | bytes 196612
  3.0 20.8 %copy-start.7 = (f32[56,320]{1,0:T(8,128)S(1)}, f32[56,320]{1,0:T(8,128)}, u32[]{:S(2)}) copy-start(f32[56,320]{1,0:T(8,128)} %constant.18.clone.shift_hbm) | copy-start | bytes 215044
  3.0 20.8 %copy-start.10 = (f32[3,10,128]{2,0,1:T(4,128)S(1)}, f32[3,10,128]{2,0,1:T(4,128)}, u32[]{:S(2)}) copy-start(f32[3,10,128]{2,0,1:T(4,128)} %param.21) | copy-start | bytes 46084
  3.0 20.8 %copy-start.11 = (f32[2,8,128]{2,1,0:T(8,128)S(1)}, f32[2,8,128]{2,1,0:T(8,128)}, u32[]{:S(2)}) copy-start(f32[2,8,128]{2,1,0:T(8,128)} %radial_hbm.1) | copy-start | bytes 24580
  3.0 20.8 %copy-start.12 = (f32[128,16]{0,1:T(8,128)S(1)}, f32[128,16]{0,1:T(8,128)}, u32[]{:S(2)}) copy-start(f32[128,16]{0,1:T(8,128)} %param.23) | copy-start | bytes 24580
  23.7 0.7 copy-start.16
  24.4 0.9 %copy-start = (bf16[288,320]{1,0:T(8,128)(2,1)S(1)}, bf16[288,320]{1,0:T(8,128)(2,1)}, u32[]{:S(2)}) copy-start(bf16[288,320]{1,0:T(8,128)(2,1)} %constant.17.clone.spot_hbm) | copy-start | bytes 552964
  25.3 0.9 %copy-start.3 = (bf16[320,192]{1,0:T(8,128)(2,1)S(1)}, bf16[320,192]{1,0:T(8,128)(2,1)}, u32[]{:S(2)}) copy-start(bf16[320,192]{1,0:T(8,128)(2,1)} %constant.15.clone.pick_hbm) | copy-start | bytes 368644
  26.2 0.9 %copy-start.4 = (bf16[192,320]{1,0:T(8,128)(2,1)S(1)}, bf16[192,320]{1,0:T(8,128)(2,1)}, u32[]{:S(2)}) copy-start(bf16[192,320]{1,0:T(8,128)(2,1)} %constant.16.clone.pick_t_hbm) | copy-start | bytes 368644
  27.2 0.9 %copy-start.5 = (f32[256,8]{1,0:T(8,128)S(1)}, f32[256,8]{1,0:T(8,128)}, u32[]{:S(2)}) copy-start(f32[256,8]{1,0:T(8,128)} %constant.20.clone.origin_hbm) | copy-start | bytes 24580
  28.1 0.9 %copy-start.6 = (bf16[256,256]{1,0:T(8,128)(2,1)S(1)}, bf16[256,256]{1,0:T(8,128)(2,1)}, u32[]{:S(2)}) copy-start(bf16[256,256]{1,0:T(8,128)(2,1)} %constant.19.clone.turn_hbm) | copy-start | bytes 393220
  29.0 0.8 %copy-start.9 = (f32[128,128]{1,0:T(8,128)S(1)}, f32[128,128]{1,0:T(8,128)}, u32[]{:S(2)}) copy-start(f32[128,128]{1,0:T(8,128)} %mixing_hbm.1) | copy-start | bytes 196612
  29.8 21.2 %copy-start.2 = (bf16[160,32]{1,0:T(8,128)(2,1)S(1)}, bf16[160,32]{1,0:T(8,128)(2,1)}, u32[]{:S(2)}) copy-start(bf16[160,32]{1,0:T(8,128)(2,1)} %constant.14.clone.faces_hbm.faces_ref) | copy-start | bytes 30724

commit v5 on v4

--- a/solution.py
+++ b/solution.py
@@ -699,9 +699,9 @@
     f32, half = jnp.float32, jnp.bfloat16
 
     vmem = pl.BlockSpec(memory_space=pltpu.VMEM)
-    hbm = pl.BlockSpec(memory_space=pl.ANY)
+    hbm = pl.BlockSpec(memory_space=pltpu.HBM)
     dims = (sx, lat, reach, o, pieces)
-    limit = 50 * 1024 * 1024
+    limit = 61 * 1024 * 1024
     ways = 2 * len(DIRECTIONS)
     faces = jnp.asarray(faces, half)
     local_turned = local_pos.transpose(0, 1, 3, 2, 4)

time: 71.8 us -> 69.4 us (0.967)
  local copies, waits for them, and re-layouts: 10.2 us -> 3.4 us
  Pallas kernels: 60.5 us -> 65 us
    unnamed x37 -> x7, local copies, waits for them, and re-layouts: 10.2 us -> 3.4 us
    pallas_call x1, Pallas kernels: 18.5 us -> 20.4 us  [body(): pl.pallas_call(functools.partial(gather_kernel, dims), out_shape=(jax.Sha...]
    pallas_call x1, Pallas kernels: 21.2 us -> 23 us  [body(): pl.pallas_call(functools.partial(compute_kernel, (sx, sy, sz, reach, nb,...]
    pallas_call x1, Pallas kernels: 20.8 us -> 21.7 us  [body(): pl.pallas_call(functools.partial(spread_kernel, dims, spacing), out_shape...]
where the time goes in v5:
time: 69.4 us; the launch traced here: 69.1 us
  Pallas kernels  65 us (94%)
  local copies, waits for them, and re-layouts  3.4 us (5%)
    pallas_call x1, Pallas kernels, body(): pl.pallas_call(functools.partial(compute_kernel, (sx, sy, sz, reach, nb,...  23 us
    pallas_call x1, Pallas kernels, body(): pl.pallas_call(functools.partial(spread_kernel, dims, spacing), out_shape...  21.7 us
    pallas_call x1, Pallas kernels, body(): pl.pallas_call(functools.partial(gather_kernel, dims), out_shape=(jax.Sha...  20.4 us
    unnamed x7, local copies, waits for them, and re-layouts  3.4 us

profile of v5, /device:TPU:0, one launch (start us, length us, event | category | flops | bytes accessed | tf_op | source)
XLA Modules:
  0.0 69.1 jit_solution(7296524061007215587)
XLA Ops:
  0.6 21.7 %halo_out.1 = (bf16[14,192,128]{2,1,0:T(8,128)(2,1)}, f32[3,3,3,2,4,128]{5,4,3,2,1,0:T(4,128)}, bf16[2,128,128]{2,1,0:T(8,128)(2,1)}, f32[2,8,128]{2,1,0:T(8,128)}) custom-call(s32[2,1,2]{2,1,0:T(1,128)} %bitcast.18, f32[2,2,3,1,64]{4,3,2,1,0:T(1,128)} %bitcast.16, s32[2,2,1,64]{3,2,1,0:T(1,128)} %kind_hbm.1, bf16[2,128,128]{2,1,0:T(8,128)(2,1)} %bitcast.13, ...), custom_call_target="tpu_custom_call" | custom-call | tf_op jit(solution)/shard_map/halo_out/pallas_call | solution.py:710
  22.3 23.0 %pair_layer.1 = (bf16[14,192,128]{2,1,0:T(8,128)(2,1)}, f32[8,32,128]{2,1,0:T(8,128)}, f32[3,3,3,2,4,128]{5,4,3,2,1,0:T(4,128)}, f32[2,4,128]{2,1,0:T(4,128)}) custom-call(bf16[14,192,128]{2,1,0:T(8,128)(2,1)} %get-tuple-element.15.layer_ref, f32[3,3,3,2,4,128]{5,4,3,2,1,0:T(4,128)} %get-tuple-element.16.tile_ref, f32[2,8,128]{2,1,0:T(8,128)} %get-tuple-element.17.small_ref, ...), custom_call_target="tpu_custom_call" | custom-call | tf_op jit(solution)/shard_map/pair_layer/pallas_call | solution.py:749
  45.3 20.4 %halo_back.1 = (f32[2,128,128]{2,1,0:T(8,128)}, f32[2,2,1,64]{3,2,1,0:T(1,128)}, f32[2,2,3,1,64]{4,3,2,1,0:T(1,128)}) custom-call(bf16[2,128,128]{2,1,0:T(8,128)(2,1)} %get-tuple-element.14.place_ref, bf16[14,192,128]{2,1,0:T(8,128)(2,1)} %get-tuple-element.18.gsend_ref, f32[8,32,128]{2,1,0:T(8,128)} %get-tuple-element.19.gown_ref, ...), custom_call_target="tpu_custom_call" | custom-call | tf_op jit(solution)/shard_map/halo_back/pallas_call | solution.py:781
  65.7 0.0 copy-start.1
  65.7 0.0 copy-start
  65.7 0.7 copy-done.1
  66.4 0.6 copy.24
  66.9 0.0 copy-done
  66.9 0.6 copy.25
  67.5 1.6 %copy.26 = f32[2,2,1,64,128]{4,3,2,1,0:T(8,128)} copy(f32[2,2,1,64,128]{4,3,2,1,0:T(8,128)} %bitcast.12) | data formatting | bytes 262144
Async XLA Ops:
  65.7 0.7 copy-start.1
  65.7 1.2 %copy-start = (f32[2,2,3,1,64]{4,3,2,1,0:T(1,128)S(1)}, f32[2,2,3,1,64]{4,3,2,1,0:T(1,128)}, u32[]{:S(2)}) copy-start(f32[2,2,3,1,64]{4,3,2,1,0:T(1,128)} %get-tuple-element.23) | copy-start | bytes 9220
